TPU v7x, 256 devices: a whole 4x4x8 slice. The times are simulated.
256 devices in a mesh: group: 4 (over y_lo, core), dev: 64 (over x, z, y_hi).
Axes of the slice: x: 4, y: 4 (y_hi: 2, y_lo: 2; y = y_hi * 2 + y_lo), z: 8, core: 2. Of those that a mesh axis runs over, the one named last changes fastest.
Arguments:
- queries: bfloat16 [163840, 768], P(('group', 'dev')), may hold values from -24 to 24
- docids: bfloat16 [163840, 768], P(('group', 'dev')), may hold values from -6 to 6
- labels: int32 [163840], P(('group', 'dev')), may hold values from 0 to 163839, as said below
- head_query: bfloat16 [768, 768], replicated, may hold values from -0.21875 to 0.21875
- head_docid: bfloat16 [768, 768], replicated, may hold values from -0.21875 to 0.21875
Outputs:
- doc_update: bfloat16 [163840, 768], P(('group', 'dev'))
- query_head_step: float32 [768, 768], replicated
- docid_head_step: float32 [768, 768], replicated
Inputs may be any that keep to these rules, and one draw needn't show every extreme that they name: `labels`: each query's positive docid lies in its own block or in one of its 4 source blocks.
All inputs are finite; a program needn't handle non-finite values.
Results may differ from a plain program's by a relative error of at most 0.0075.
Values may be sent and summed in bfloat16 or wider, within the bound.
No kernel may reach another device: no remote copies, remote signals or barrier semaphores. Data moves between devices by JAX's collectives and lax.ppermute only.
A program may use at most 128 MiB of HBM per device.

v0:
```python
import jax
import jax.numpy as jnp
from jax import lax
from jax.sharding import PartitionSpec as P

ROUNDS = 4


LOGIT_SCALE = 5.0
LOGIT_BIAS = -2.0
EPSILON = 1e-06


def swapped(value, axis, stride):
    mask = 2**stride
    pairs = [(source, source ^ mask) for source in range(lax.axis_size(axis))]
    return lax.ppermute(value, axis, pairs)


def shifted(block, axis, distance):
    devices = range(lax.axis_size(axis))
    route = [((i - distance) % len(devices), i) for i in devices]
    return lax.ppermute(block, axis, route)


def project(inputs, weight):
    projected = jnp.dot(inputs, weight, preferred_element_type=jnp.float32)
    inverse = lax.rsqrt(jnp.sum(projected * projected, axis=-1, keepdims=True) + EPSILON)
    return (projected * inverse, inverse)


def direction(grad, unit, inverse):
    inner = jnp.sum(unit * grad, axis=-1, keepdims=True)
    return ((grad - unit * inner) * inverse).astype(jnp.bfloat16)


def route(block, bit_index, shift_by):
    moved = swapped(block, "group", bit_index)
    return shifted(moved, "dev", shift_by)


def per_device(queries, docids, labels, head_query, head_docid):
    block_rows = queries.shape[0]
    query_unit, query_inverse = project(queries, head_query)
    docid_unit, docid_inverse = project(docids, head_docid)
    query_vec = query_unit.astype(jnp.bfloat16)
    docid_vec = docid_unit.astype(jnp.bfloat16)
    group_index = lax.axis_index("group")
    device_index = lax.axis_index("dev")
    device_count = lax.axis_size("dev")
    columns = jnp.arange(block_rows, dtype=jnp.int32)

    def pair_weights(docid_block, doc_start):
        scores = lax.dot_general(
            query_vec, docid_block, (((1,), (1,)), ((), ())), preferred_element_type=jnp.float32
        )
        logits = LOGIT_SCALE * scores + LOGIT_BIAS
        target = jnp.where(labels[:, None] == doc_start + columns[None, :], 1.0, -1.0).astype(
            jnp.float32
        )
        return (-target * jax.nn.sigmoid(-target * logits)).astype(jnp.bfloat16)

    def doc_partial(weights):
        return LOGIT_SCALE * lax.dot_general(
            weights, query_vec, (((0,), (0,)), ((), ())), preferred_element_type=jnp.float32
        )

    own_start = (group_index * device_count + device_index) * block_rows
    weights = pair_weights(docid_vec, own_start)
    query_grad = LOGIT_SCALE * jnp.dot(weights, docid_vec, preferred_element_type=jnp.float32)
    docid_grad = doc_partial(weights)
    for round_no in range(1, ROUNDS + 1):
        bit_index = (round_no - 1) % 2
        source_block = route(docid_vec, bit_index, round_no)
        source_bit_index = (round_no - 1) % 2
        source_group = jnp.bitwise_xor(group_index, 1 << source_bit_index)
        weights = pair_weights(
            source_block,
            (source_group * device_count + (device_index - round_no) % device_count) * block_rows,
        )
        query_grad = query_grad + LOGIT_SCALE * jnp.dot(
            weights, source_block, preferred_element_type=jnp.float32
        )
        returned = route(doc_partial(weights).astype(jnp.bfloat16), bit_index, -round_no)
        docid_grad = docid_grad + returned.astype(jnp.float32)
    query_direct = direction(query_grad, query_unit, query_inverse)
    docid_direct = direction(docid_grad, docid_unit, docid_inverse)
    query_head_grad = lax.dot_general(
        queries, query_direct, (((0,), (0,)), ((), ())), preferred_element_type=jnp.float32
    )
    docid_head_grad = lax.dot_general(
        docids, docid_direct, (((0,), (0,)), ((), ())), preferred_element_type=jnp.float32
    )
    entries = query_head_grad.shape[0] * query_head_grad.shape[1]
    query_total, docid_total = lax.psum((query_head_grad, docid_head_grad), ("group", "dev"))
    query_head_step = query_total * lax.rsqrt(
        jnp.sum(query_total * query_total) / entries + EPSILON
    )
    docid_head_step = docid_total * lax.rsqrt(
        jnp.sum(docid_total * docid_total) / entries + EPSILON
    )
    doc_grad = lax.dot_general(
        docid_direct, head_docid, (((1,), (1,)), ((), ())), preferred_element_type=jnp.float32
    )
    doc_update = (
        doc_grad * lax.rsqrt(jnp.mean(doc_grad * doc_grad, axis=-1, keepdims=True) + EPSILON)
    ).astype(jnp.bfloat16)
    return (doc_update, query_head_step, docid_head_step)


def solution(mesh):
    placed = (P(("group", "dev"), None), P(("group", "dev"), None), P(("group", "dev")), P(), P())
    return jax.shard_map(
        per_device,
        mesh=mesh,
        in_specs=placed,
        out_specs=(P(("group", "dev"), None), P(), P()),
        check_vma=False,
    )
```

profile of v0, /device:TPU:1, one launch (start us, length us, event | category | flops | bytes accessed | tf_op | source)
XLA Modules:
  0.0 605.6 jit_solution(9337751829899209701)
XLA Ops:
  7.2 0.0 copy-start
  7.2 0.0 all-reduce.3.cloned.1.call-start
  7.2 1.2 copy-done
  8.4 2.2 multiply_reduce_fusion.5
  10.7 1.1 multiply_convert_fusion.7
  11.8 3.2 collective-permute-start
  15.0 0.0 collective-permute-start.4
  15.1 2.6 multiply_reduce_fusion.6
  17.6 0.0 copy-start.7
  17.7 0.0 collective-permute-done
  17.7 2.2 collective-permute-start.1
  19.9 0.2 multiply_convert_fusion.8
  20.1 2.4 multiply_convert_fusion.13
  22.5 16.2 %collective-permute-done.4 = bf16[640,768]{1,0:T(8,128)(2,1)} collective-permute-done((bf16[640,768]{1,0:T(8,128)(2,1)}, bf16[640,768]{1,0:T(8,128)(2,1)}, u32[]{:S(2)}, u32[]{:S(2)}) %collective-permute-start.4) | collective-permute-done | bytes 983072 | tf_op jit(solution)/shard_map/ppermute | solution.py:17
  38.7 25.2 %collective-permute-start.8 = (bf16[640,768]{1,0:T(8,128)(2,1)}, bf16[640,768]{1,0:T(8,128)(2,1)S(1)}, u32[]{:S(2)}, u32[]{:S(2)}) collective-permute-start(bf16[640,768]{1,0:T(8,128)(2,1)} %collective-permute-done), channel_id=1, source_target_pairs={{61,0},{62,1},{63,2},{0,3},{1,4},{2,5},{3,6},{4,7},{5,8},{6,9},{7,... | collective-permute-start | bytes 2949128 | tf_op jit(solution)/shard_map/ppermute | solution.py:23
  64.0 4.2 collective-permute-start.11
  68.2 1.2 multiply_convert_fusion.12
  69.4 1.0 multiply_convert_fusion.6
  70.4 1.7 collective-permute-start.2
  72.1 0.0 collective-permute-done.5
  72.1 1.2 multiply_convert_fusion.11
  73.3 1.0 multiply_convert_fusion.5
  74.3 0.7 collective-permute-start.6
  75.0 38.3 %collective-permute-done.8 = bf16[640,768]{1,0:T(8,128)(2,1)S(1)} collective-permute-done((bf16[640,768]{1,0:T(8,128)(2,1)}, bf16[640,768]{1,0:T(8,128)(2,1)S(1)}, u32[]{:S(2)}, u32[]{:S(2)}) %collective-permute-start.8) | collective-permute-done | bytes 983072 | tf_op jit(solution)/shard_map/ppermute | solution.py:23
  113.2 1.2 multiply_convert_fusion.10
  114.5 1.0 multiply_convert_fusion.4
  115.4 3.0 collective-permute-start.9
  118.5 14.7 %collective-permute-done.11 = bf16[640,768]{1,0:T(8,128)(2,1)S(1)} collective-permute-done((bf16[640,768]{1,0:T(8,128)(2,1)}, bf16[640,768]{1,0:T(8,128)(2,1)S(1)}, u32[]{:S(2)}, u32[]{:S(2)}) %collective-permute-start.11) | collective-permute-done | bytes 983072 | tf_op jit(solution)/shard_map/ppermute | solution.py:23
  133.2 1.2 multiply_convert_fusion.9
  134.4 1.0 multiply_convert_fusion.3
  135.3 0.5 collective-permute-start.12
  135.8 2.1 fusion.2
  138.0 0.9 fusion.3
  138.9 0.9 fusion.4
  139.8 0.9 fusion.5
  140.8 0.0 copy-start.3
  140.8 0.0 collective-permute-done.2
  140.8 43.4 %collective-permute-start.3 = (bf16[640,768]{1,0:T(8,128)(2,1)S(1)}, bf16[640,768]{1,0:T(8,128)(2,1)S(1)}, u32[]{:S(2)}, u32[]{:S(2)}) collective-permute-start(bf16[640,768]{1,0:T(8,128)(2,1)S(1)} %collective-permute-done.2), channel_id=1, source_target_pairs={{1,0},{2,1},{3,2},{4,3},{5,4},{6,5},{7,6},{8,7},{9,8},{10,9},{11,1... | collective-permute-start | bytes 2949128 | tf_op jit(solution)/shard_map/ppermute | solution.py:23
  184.2 0.0 collective-permute-done.9
  184.2 2.5 collective-permute-start.10
  186.7 0.0 collective-permute-done.12
  186.7 0.3 collective-permute-start.13
  187.0 1.3 multiply_reduce_fusion.2
  188.3 2.9 convolution_bitcast_fusion.1
  191.2 12.1 %collective-permute-done.3 = bf16[640,768]{1,0:T(8,128)(2,1)S(1)} collective-permute-done((bf16[640,768]{1,0:T(8,128)(2,1)S(1)}, bf16[640,768]{1,0:T(8,128)(2,1)S(1)}, u32[]{:S(2)}, u32[]{:S(2)}) %collective-permute-start.3) | collective-permute-done | bytes 983072 | tf_op jit(solution)/shard_map/ppermute | solution.py:23
  203.3 63.2 %collective-permute-done.7 = bf16[640,768]{1,0:T(8,128)(2,1)S(1)} collective-permute-done((bf16[640,768]{1,0:T(8,128)(2,1)S(1)}, bf16[640,768]{1,0:T(8,128)(2,1)S(1)}, u32[]{:S(2)}, u32[]{:S(2)}) %collective-permute-start.7) | collective-permute-done | bytes 983072 | tf_op jit(solution)/shard_map/ppermute | solution.py:23
  266.5 21.1 %collective-permute-done.10 = bf16[640,768]{1,0:T(8,128)(2,1)S(1)} collective-permute-done((bf16[640,768]{1,0:T(8,128)(2,1)S(1)}, bf16[640,768]{1,0:T(8,128)(2,1)S(1)}, u32[]{:S(2)}, u32[]{:S(2)}) %collective-permute-start.10) | collective-permute-done | bytes 983072 | tf_op jit(solution)/shard_map/ppermute | solution.py:23
  287.6 22.9 %collective-permute-done.13 = bf16[640,768]{1,0:T(8,128)(2,1)S(1)} collective-permute-done((bf16[640,768]{1,0:T(8,128)(2,1)S(1)}, bf16[640,768]{1,0:T(8,128)(2,1)S(1)}, u32[]{:S(2)}, u32[]{:S(2)}) %collective-permute-start.13) | collective-permute-done | bytes 983072 | tf_op jit(solution)/shard_map/ppermute | solution.py:23
  310.4 1.7 multiply_reduce_fusion.4
  312.1 0.0 copy-start.6
  312.1 1.0 multiply_convert_fusion.2
  313.1 0.0 copy-start.4
  313.1 0.9 copy-done.4
  314.1 2.5 convolution_bitcast_fusion
  316.6 0.0 all-reduce.3.cloned.1.call-update
  316.6 1.2 copy-done.5
  317.8 1.0 multiply_reduce_fusion.3
  318.8 1.1 multiply_convert_fusion.1
  320.0 264.4 %all-reduce.3.cloned.1.call-done = (f32[768,768]{0,1:T(8,128)}, f32[768,768]{0,1:T(8,128)}) async-done(((f32[768,768]{0,1:T(8,128)}, f32[768,768]{0,1:T(8,128)}), (f32[768,768]{0,1:T(8,128)}, f32[768,768]{0,1:T(8,128)})) %all-reduce.3.cloned.1.call-update) | async-done | bytes 4718608 | tf_op jit(solution)/shard_map/psum | solution.py:95
  584.3 3.7 multiply_reduce_fusion
  588.8 1.6 broadcast_multiply_fusion
  590.3 3.2 copy.9
  594.1 1.6 broadcast_multiply_fusion.1
  595.7 3.0 copy.8
  (20 shorter events, 0.1 us)
Async XLA Ops:
  7.2 1.3 copy-start
  7.2 577.2 %all-reduce.3.cloned.1.call-start = ((), (), s32[]{:S(2)}) async-start(), calls=%async_computation | async-start | bytes 9437184 | tf_op jit(solution)/shard_map/psum | solution.py:95
  11.8 5.9 collective-permute-start
  15.0 23.7 %collective-permute-start.4 = (bf16[640,768]{1,0:T(8,128)(2,1)}, bf16[640,768]{1,0:T(8,128)(2,1)}, u32[]{:S(2)}, u32[]{:S(2)}) collective-permute-start(bf16[640,768]{1,0:T(8,128)(2,1)} %multiply_convert_fusion.7), channel_id=1, source_target_pairs={{0,128},{64,192},{128,0},{192,64},{1,129},{65,193},{129,1},{193,65... | collective-permute-start | bytes 2949128 | tf_op jit(solution)/shard_map/ppermute | solution.py:17
  17.6 2.5 copy-start.7
  17.7 50.5 %collective-permute-start.1 = (bf16[640,768]{1,0:T(8,128)(2,1)}, bf16[640,768]{1,0:T(8,128)(2,1)S(1)}, u32[]{:S(2)}, u32[]{:S(2)}) collective-permute-start(bf16[640,768]{1,0:T(8,128)(2,1)} %collective-permute-done), channel_id=1, source_target_pairs={{63,0},{0,1},{1,2},{2,3},{3,4},{4,5},{5,6},{6,7},{7,8},{8,9},{9,10... | collective-permute-start | bytes 2949128 | tf_op jit(solution)/shard_map/ppermute | solution.py:23
  38.7 33.4 %collective-permute-start.5 = (bf16[640,768]{1,0:T(8,128)(2,1)}, bf16[640,768]{1,0:T(8,128)(2,1)S(1)}, u32[]{:S(2)}, u32[]{:S(2)}) collective-permute-start(bf16[640,768]{1,0:T(8,128)(2,1)} %collective-permute-done.4), channel_id=1, source_target_pairs={{62,0},{63,1},{0,2},{1,3},{2,4},{3,5},{4,6},{5,7},{6,8},{7,9},{8,1... | collective-permute-start | bytes 2949128 | tf_op jit(solution)/shard_map/ppermute | solution.py:23
  38.7 74.5 %collective-permute-start.8 = (bf16[640,768]{1,0:T(8,128)(2,1)}, bf16[640,768]{1,0:T(8,128)(2,1)S(1)}, u32[]{:S(2)}, u32[]{:S(2)}) collective-permute-start(bf16[640,768]{1,0:T(8,128)(2,1)} %collective-permute-done), channel_id=1, source_target_pairs={{61,0},{62,1},{63,2},{0,3},{1,4},{2,5},{3,6},{4,7},{5,8},{6,9},{7,... | collective-permute-start | bytes 2949128 | tf_op jit(solution)/shard_map/ppermute | solution.py:23
  64.0 69.2 %collective-permute-start.11 = (bf16[640,768]{1,0:T(8,128)(2,1)}, bf16[640,768]{1,0:T(8,128)(2,1)S(1)}, u32[]{:S(2)}, u32[]{:S(2)}) collective-permute-start(bf16[640,768]{1,0:T(8,128)(2,1)} %collective-permute-done.4), channel_id=1, source_target_pairs={{60,0},{61,1},{62,2},{63,3},{0,4},{1,5},{2,6},{3,7},{4,8},{5,9},{6... | collective-permute-start | bytes 2949128 | tf_op jit(solution)/shard_map/ppermute | solution.py:23
  70.4 70.4 %collective-permute-start.2 = (bf16[640,768]{1,0:T(8,128)(2,1)S(1)}, bf16[640,768]{1,0:T(8,128)(2,1)S(1)}, u32[]{:S(2)}, u32[]{:S(2)}) collective-permute-start(bf16[640,768]{1,0:T(8,128)(2,1)S(1)} %multiply_convert_fusion.6), channel_id=1, source_target_pairs={{0,64},{64,0},{128,192},{192,128},{1,65},{65,1},{129,193},{193,129... | collective-permute-start | bytes 2949128 | tf_op jit(solution)/shard_map/ppermute | solution.py:17
  74.3 109.9 %collective-permute-start.6 = (bf16[640,768]{1,0:T(8,128)(2,1)S(1)}, bf16[640,768]{1,0:T(8,128)(2,1)S(1)}, u32[]{:S(2)}, u32[]{:S(2)}) collective-permute-start(bf16[640,768]{1,0:T(8,128)(2,1)S(1)} %multiply_convert_fusion.5), channel_id=1, source_target_pairs={{0,128},{64,192},{128,0},{192,64},{1,129},{65,193},{129,1},{193,65... | collective-permute-start | bytes 2949128 | tf_op jit(solution)/shard_map/ppermute | solution.py:17
  115.4 68.8 %collective-permute-start.9 = (bf16[640,768]{1,0:T(8,128)(2,1)S(1)}, bf16[640,768]{1,0:T(8,128)(2,1)S(1)}, u32[]{:S(2)}, u32[]{:S(2)}) collective-permute-start(bf16[640,768]{1,0:T(8,128)(2,1)S(1)} %multiply_convert_fusion.4), channel_id=1, source_target_pairs={{0,64},{64,0},{128,192},{192,128},{1,65},{65,1},{129,193},{193,129... | collective-permute-start | bytes 2949128 | tf_op jit(solution)/shard_map/ppermute | solution.py:17
  135.3 51.3 %collective-permute-start.12 = (bf16[640,768]{1,0:T(8,128)(2,1)S(1)}, bf16[640,768]{1,0:T(8,128)(2,1)S(1)}, u32[]{:S(2)}, u32[]{:S(2)}) collective-permute-start(bf16[640,768]{1,0:T(8,128)(2,1)S(1)} %multiply_convert_fusion.3), channel_id=1, source_target_pairs={{0,128},{64,192},{128,0},{192,64},{1,129},{65,193},{129,1},{193,65... | collective-permute-start | bytes 2949128 | tf_op jit(solution)/shard_map/ppermute | solution.py:17
  140.8 47.6 %copy-start.3 = (bf16[640,768]{1,0:T(8,128)(2,1)S(1)}, bf16[640,768]{1,0:T(8,128)(2,1)}, u32[]{:S(2)}) copy-start(bf16[640,768]{1,0:T(8,128)(2,1)} %param.5) | copy-start | bytes 2949124
  140.8 62.5 %collective-permute-start.3 = (bf16[640,768]{1,0:T(8,128)(2,1)S(1)}, bf16[640,768]{1,0:T(8,128)(2,1)S(1)}, u32[]{:S(2)}, u32[]{:S(2)}) collective-permute-start(bf16[640,768]{1,0:T(8,128)(2,1)S(1)} %collective-permute-done.2), channel_id=1, source_target_pairs={{1,0},{2,1},{3,2},{4,3},{5,4},{6,5},{7,6},{8,7},{9,8},{10,9},{11,1... | collective-permute-start | bytes 2949128 | tf_op jit(solution)/shard_map/ppermute | solution.py:23
  184.2 82.3 %collective-permute-start.7 = (bf16[640,768]{1,0:T(8,128)(2,1)S(1)}, bf16[640,768]{1,0:T(8,128)(2,1)S(1)}, u32[]{:S(2)}, u32[]{:S(2)}) collective-permute-start(bf16[640,768]{1,0:T(8,128)(2,1)S(1)} %collective-permute-done.6), channel_id=1, source_target_pairs={{2,0},{3,1},{4,2},{5,3},{6,4},{7,5},{8,6},{9,7},{10,8},{11,9},{12,... | collective-permute-start | bytes 2949128 | tf_op jit(solution)/shard_map/ppermute | solution.py:23
  184.2 103.4 %collective-permute-start.10 = (bf16[640,768]{1,0:T(8,128)(2,1)S(1)}, bf16[640,768]{1,0:T(8,128)(2,1)S(1)}, u32[]{:S(2)}, u32[]{:S(2)}) collective-permute-start(bf16[640,768]{1,0:T(8,128)(2,1)S(1)} %collective-permute-done.9), channel_id=1, source_target_pairs={{3,0},{4,1},{5,2},{6,3},{7,4},{8,5},{9,6},{10,7},{11,8},{12,9},{13... | collective-permute-start | bytes 2949128 | tf_op jit(solution)/shard_map/ppermute | solution.py:23
  186.7 123.8 %collective-permute-start.13 = (bf16[640,768]{1,0:T(8,128)(2,1)S(1)}, bf16[640,768]{1,0:T(8,128)(2,1)S(1)}, u32[]{:S(2)}, u32[]{:S(2)}) collective-permute-start(bf16[640,768]{1,0:T(8,128)(2,1)S(1)} %collective-permute-done.12), channel_id=1, source_target_pairs={{4,0},{5,1},{6,2},{7,3},{8,4},{9,5},{10,6},{11,7},{12,8},{13,9},{1... | collective-permute-start | bytes 2949128 | tf_op jit(solution)/shard_map/ppermute | solution.py:23
  312.1 1.9 copy-start.6
  313.1 0.9 copy-start.4
  316.6 1.2 copy-start.5
  584.3 4.4 copy-start.2
  590.3 3.8 copy-start.1
Sparse Core Ops, SparseCore 0:
  316.7 267.5 all-reduce.2
where the time goes:
time: 607 us; the launch traced here: 606 us
  waiting for transfers between devices  453 us (75%)
  starting transfers between devices  87.1 us (14%)
  matrix products  30.4 us (5%)
  between operations  15.5 us (3%)
  other arithmetic  10.3 us (2%)
  local copies, waits for them, and re-layouts  9.6 us (2%)
    psum x1, waiting for transfers between devices, per_device(): lax.psum((query_head_grad, docid_head_grad), ('group', 'dev'))  264 us
    ppermute x8, waiting for transfers between devices, shifted(): return lax.ppermute(block, axis, route)  172 us
    ppermute x8, starting transfers between devices, shifted(): return lax.ppermute(block, axis, route)  77.9 us
    ppermute x6, waiting for transfers between devices, swapped(): return lax.ppermute(value, axis, pairs)  16.2 us
  transfers between devices with their start and end apart: 15, of which 8 were waited for; matrix products, arithmetic and copies ran while one was open for 4% of the time, Pallas kernels for 0%

commit v1 on v0

v1 whole, which is shorter than its diff:
```python
import jax
import jax.numpy as jnp
from jax import lax
from jax.sharding import Mesh
from jax.sharding import PartitionSpec as P

LOGIT_SCALE = 5.0
LOGIT_BIAS = -2.0
EPSILON = 1e-06

AXES = ("y_lo", "core", "x", "z", "y_hi")
SIZES = (2, 2, 4, 8, 2)
PLANE = ("y_lo", "y_hi", "x")
DEVS = 64


def moved(block, flip, shift):
    pairs = []
    for source in range(4 * DEVS):
        group, dev = divmod(source, DEVS)
        pairs.append((source, (group ^ flip) * DEVS + (dev + shift) % DEVS))
    return lax.ppermute(block, AXES, pairs)


def project(inputs, weight):
    projected = jnp.dot(inputs, weight, preferred_element_type=jnp.float32)
    inverse = lax.rsqrt(jnp.sum(projected * projected, axis=-1, keepdims=True) + EPSILON)
    return (projected * inverse, inverse)


def direction(grad, unit, inverse):
    inner = jnp.sum(unit * grad, axis=-1, keepdims=True)
    return ((grad - unit * inner) * inverse).astype(jnp.bfloat16)


def pair_weights(queries, docids, labels, doc_start):
    scores = lax.dot_general(
        queries, docids, (((1,), (1,)), ((), ())), preferred_element_type=jnp.float32
    )
    logits = LOGIT_SCALE * scores + LOGIT_BIAS
    columns = jnp.arange(docids.shape[0], dtype=jnp.int32)
    positive = labels[:, None] == doc_start + columns[None, :]
    return (jax.nn.sigmoid(logits) - jnp.where(positive, 1.0, 0.0)).astype(jnp.bfloat16)


def rows_of(weights, docids):
    return LOGIT_SCALE * jnp.dot(weights, docids, preferred_element_type=jnp.float32)


def columns_of(weights, queries):
    return LOGIT_SCALE * lax.dot_general(
        weights, queries, (((0,), (0,)), ((), ())), preferred_element_type=jnp.float32
    )


def total(partial):
    rows, width = partial.shape
    half = rows // 2
    core = lax.axis_index("core")
    first, second = partial[:half], partial[half:]
    kept = jnp.where(core == 0, first, second)
    sent = jnp.where(core == 0, second, first).astype(jnp.bfloat16)
    value = kept + moved(sent, 1, 0).astype(jnp.float32)
    plane, line = 16, SIZES[3]
    piece = value.astype(jnp.bfloat16).reshape(plane, half // plane, width)
    piece = lax.all_to_all(piece, PLANE, 0, 0, tiled=True)
    value = jnp.sum(piece.astype(jnp.float32), axis=0)
    piece = value.astype(jnp.bfloat16).reshape(line, -1, 128)
    piece = lax.all_to_all(piece, "z", 0, 0, tiled=True)
    value = jnp.sum(piece.astype(jnp.float32), axis=0).astype(jnp.bfloat16)
    piece = jnp.broadcast_to(value[None], (line,) + value.shape)
    piece = lax.all_to_all(piece, "z", 0, 0, tiled=True).reshape(half // plane, width)
    piece = jnp.broadcast_to(piece[None], (plane,) + piece.shape)
    mine = lax.all_to_all(piece, PLANE, 0, 0, tiled=True).reshape(half, width)
    other = moved(mine, 1, 0)
    first = jnp.where(core == 0, mine, other)
    second = jnp.where(core == 0, other, mine)
    return first.astype(jnp.float32), second.astype(jnp.float32)


def unit_rms(grad):
    return grad * lax.rsqrt(jnp.mean(grad * grad) + EPSILON)


def per_device(queries, docids, labels, head_query, head_docid):
    block_rows = queries.shape[0]
    group = lax.axis_index("y_lo") * 2 + lax.axis_index("core")
    dev = (lax.axis_index("x") * 8 + lax.axis_index("z")) * 2 + lax.axis_index("y_hi")

    def start(flip, shift):
        return (jnp.bitwise_xor(group, flip) * DEVS + (dev + shift) % DEVS) * block_rows

    docid_unit, docid_inverse = project(docids, head_docid)
    docid_vec = docid_unit.astype(jnp.bfloat16)
    docid_1 = moved(docid_vec, 1, 1)
    docid_2 = moved(docid_vec, 2, 2)
    query_unit, query_inverse = project(queries, head_query)
    query_vec = query_unit.astype(jnp.bfloat16)
    query_far = moved(query_vec, 0, -2)
    labels_far = moved(labels, 0, -2)

    weights = pair_weights(query_vec, docid_vec, labels, start(0, 0))
    query_grad = rows_of(weights, docid_vec)
    docid_grad = columns_of(weights, query_vec)

    both = jnp.concatenate([query_vec, query_far])
    labels_both = jnp.concatenate([labels, labels_far])
    weights_1 = pair_weights(both, docid_1, labels_both, start(1, -1))
    back_1 = moved(columns_of(weights_1, both).astype(jnp.bfloat16), 1, -1)
    query_both = rows_of(weights_1, docid_1)
    weights_2 = pair_weights(both, docid_2, labels_both, start(2, -2))
    back_2 = moved(columns_of(weights_2, both).astype(jnp.bfloat16), 2, -2)
    query_both = query_both + rows_of(weights_2, docid_2)
    back_far = moved(query_both[block_rows:].astype(jnp.bfloat16), 0, 2)
    query_grad = query_grad + query_both[:block_rows] + back_far.astype(jnp.float32)
    docid_grad = docid_grad + back_1.astype(jnp.float32) + back_2.astype(jnp.float32)

    query_direct = direction(query_grad, query_unit, query_inverse)
    docid_direct = direction(docid_grad, docid_unit, docid_inverse)
    query_head_grad = lax.dot_general(
        queries, query_direct, (((0,), (0,)), ((), ())), preferred_element_type=jnp.float32
    )
    docid_head_grad = lax.dot_general(
        docids, docid_direct, (((0,), (0,)), ((), ())), preferred_element_type=jnp.float32
    )
    query_total, docid_total = total(jnp.concatenate([query_head_grad, docid_head_grad]))
    query_head_step = unit_rms(query_total)
    docid_head_step = unit_rms(docid_total)
    doc_grad = lax.dot_general(
        docid_direct, head_docid, (((1,), (1,)), ((), ())), preferred_element_type=jnp.float32
    )
    doc_update = (
        doc_grad * lax.rsqrt(jnp.mean(doc_grad * doc_grad, axis=-1, keepdims=True) + EPSILON)
    ).astype(jnp.bfloat16)
    return (doc_update, query_head_step, docid_head_step)


def solution(mesh):
    split = Mesh(mesh.devices.reshape(SIZES), AXES)
    rows = P(AXES)
    return jax.shard_map(
        per_device,
        mesh=split,
        in_specs=(rows, rows, rows, P(), P()),
        out_specs=(rows, P(), P()),
        check_vma=False,
    )
```

time: 607 us -> 216 us (0.36)
  waiting for transfers between devices: 453 us -> 63.7 us
  blocking collectives: 0 us -> 59.9 us
  starting transfers between devices: 87.1 us -> 29.5 us
  between operations: 15.5 us -> 2.29 us
  matrix products: 30.4 us -> 40.4 us
    psum x1 -> x0, waiting for transfers between devices: 264 us -> none  [per_device(): lax.psum((query_head_grad, docid_head_grad), ('group', 'dev'))]
    ppermute x14 -> x9, waiting for transfers between devices: 188 us -> 63.7 us  [moved(): return lax.ppermute(block, AXES, pairs)]
    all_to_all x0 -> x4, blocking collectives: none -> 59.9 us  [the longest x1 20.7 us: total(): piece = lax.all_to_all(piece, PLANE, 0, 0, tiled=True)]
    ppermute x14 -> x9, starting transfers between devices: 87 us -> 29.5 us  [moved(): return lax.ppermute(block, AXES, pairs)]
    dot_general x15 -> x9, matrix products: 19.1 us -> 31.8 us  [the longest x3 11.7 us: columns_of(): lax.dot_general(weights, queries, (((0,), (0,)), ((), ())), preferred_ele...]
  transfers between devices with their start and end apart: 15 -> 9, of which waited for: 8 -> 5; matrix products, arithmetic and copies ran while one was open for 4% -> 18% of each run, Pallas kernels for 0% -> 0%
where the time goes in v1:
time: 216 us; the launch traced here: 215 us
  waiting for transfers between devices  63.7 us (29%)
  blocking collectives  59.9 us (28%)
  matrix products  40.4 us (19%)
  starting transfers between devices  29.5 us (14%)
  other arithmetic  10.7 us (5%)
  local copies, waits for them, and re-layouts  8.62 us (4%)
  between operations  2.29 us (1%)
    ppermute x9, waiting for transfers between devices, moved(): return lax.ppermute(block, AXES, pairs)  63.7 us
    ppermute x9, starting transfers between devices, moved(): return lax.ppermute(block, AXES, pairs)  29.5 us
    all_to_all x1, blocking collectives, total(): piece = lax.all_to_all(piece, PLANE, 0, 0, tiled=True)  20.7 us
    all_to_all x1, blocking collectives, total(): mine = lax.all_to_all(piece, PLANE, 0, 0, tiled=True).reshape(half, width)  17.5 us
    all_to_all x1, blocking collectives, total(): piece = lax.all_to_all(piece, 'z', 0, 0, tiled=True)  11.9 us
    dot_general x3, matrix products, columns_of(): lax.dot_general(weights, queries, (((0,), (0,)), ((), ())), preferred_ele...  11.7 us
    dot_general x3, matrix products, pair_weights(): lax.dot_general(queries, docids, (((1,), (1,)), ((), ())), preferred_elem...  11.1 us
    all_to_all x1, blocking collectives, total(): lax.all_to_all(piece, 'z', 0, 0, tiled=True).reshape(half // plane, width)  9.78 us
  transfers between devices with their start and end apart: 9, of which 5 were waited for; matrix products, arithmetic and copies ran while one was open for 18% of the time, Pallas kernels for 0%

profile of v1, /device:TPU:1, one launch (start us, length us, event | category | flops | bytes accessed | tf_op | source)
XLA Modules:
  0.0 215.1 jit_solution(5310077183679292864)
XLA Ops:
  0.6 0.0 copy-start
  0.6 2.7 %multiply_reduce_fusion.4 = (f32[640]{0:T(1024)S(1)}, f32[640,768]{1,0:T(8,128)S(1)}) fusion(bf16[640,768]{1,0:T(8,128)(2,1)} %param.5, bf16[768,768]{1,0:T(8,128)(2,1)} %param.8), kind=kOutput, calls=%fused_computation.41 | convolution fusion | flops 755957120 | bytes 4131328 | tf_op jit(solution)/shard_map/dot_general | solution.py:26
  3.3 0.0 copy-start.10
  3.3 1.1 multiply_convert_fusion.6
  4.5 8.6 %collective-permute-start = (bf16[640,768]{1,0:T(8,128)(2,1)}, bf16[640,768]{1,0:T(8,128)(2,1)}, u32[]{:S(2)}, u32[]{:S(2)}) collective-permute-start(bf16[640,768]{1,0:T(8,128)(2,1)} %multiply_convert_fusion.6), channel_id=1, source_target_pairs={{0,62},{1,63},{2,0},{3,1},{4,2},{5,3},{6,4},{7,5},{8,6},{9,7},{10,... | collective-permute-start | bytes 2949128 | tf_op jit(solution)/shard_map/ppermute | solution.py:22
  13.1 0.0 copy-done
  13.1 1.0 multiply_reduce_fusion.3
  14.1 0.0 copy-start.1
  14.1 0.0 copy-start.9
  14.1 1.2 copy-done.1
  15.4 1.1 multiply_convert_fusion.5
  16.5 3.8 %collective-permute-start.1 = (bf16[640,768]{1,0:T(8,128)(2,1)}, bf16[640,768]{1,0:T(8,128)(2,1)}, u32[]{:S(2)}, u32[]{:S(2)}) collective-permute-start(bf16[640,768]{1,0:T(8,128)(2,1)} %multiply_convert_fusion.5), channel_id=1, source_target_pairs={{0,65},{1,66},{2,67},{3,68},{4,69},{5,70},{6,71},{7,72},{8,73},{9,... | collective-permute-start | bytes 2949128 | tf_op jit(solution)/shard_map/ppermute | solution.py:22
  20.2 0.0 collective-permute-start.4
  20.2 4.9 %collective-permute-start.2 = (s32[640]{0:T(1024)S(1)}, s32[640]{0:T(1024)S(1)}, u32[]{:S(2)}, u32[]{:S(2)}) collective-permute-start(s32[640]{0:T(1024)S(1)} %copy-done.9), channel_id=1, source_target_pairs={{0,62},{1,63},{2,0},{3,1},{4,2},{5,3},{6,4},{7,5},{8,6},{9,7},{10,... | collective-permute-start | bytes 7688 | tf_op jit(solution)/shard_map/ppermute | solution.py:22
  25.1 8.6 %collective-permute-done.2 = s32[640]{0:T(1024)S(1)} collective-permute-done((s32[640]{0:T(1024)S(1)}, s32[640]{0:T(1024)S(1)}, u32[]{:S(2)}, u32[]{:S(2)}) %collective-permute-start.2) | collective-permute-done | bytes 2592 | tf_op jit(solution)/shard_map/ppermute | solution.py:22
  33.8 0.0 collective-permute-done
  33.8 29.1 %collective-permute-done.1 = bf16[640,768]{1,0:T(8,128)(2,1)} collective-permute-done((bf16[640,768]{1,0:T(8,128)(2,1)}, bf16[640,768]{1,0:T(8,128)(2,1)}, u32[]{:S(2)}, u32[]{:S(2)}) %collective-permute-start.1) | collective-permute-done | bytes 983072 | tf_op jit(solution)/shard_map/ppermute | solution.py:22
  62.9 3.8 %fusion.14 = bf16[1280,640]{1,0:T(8,128)(2,1)S(1)} fusion(bf16[640,768]{1,0:T(8,128)(2,1)} %collective-permute-done.1, s32[640]{0:T(1024)S(1)} %iota_add_fusion.1, s32[1280]{0:T(1024)S(1)} %pad_add_fusion, bf16[640,768]{1,0:T(8,128)(2,1)} %collective-permute-done, bf16[640,768]{1,0:T(8,128)(2,1)} %multiply_convert_fusion.6), kind=kOutput, calls=%fused_computation.17 | convolution fusion | flops 1269596160 | bytes 4595200 | tf_op jit(solution)/shard_map/dot_general | solution.py:37
  66.7 4.6 %multiply_convert_fusion.4 = bf16[640,768]{1,0:T(8,128)(2,1)} fusion(bf16[1280,640]{1,0:T(8,128)(2,1)S(1)} %fusion.14, bf16[640,768]{1,0:T(8,128)(2,1)} %collective-permute-done, bf16[640,768]{1,0:T(8,128)(2,1)} %multiply_convert_fusion.6), kind=kOutput, calls=%fused_computation.39 | convolution fusion | flops 1263206400 | bytes 4587520 | tf_op jit(solution)/shard_map/dot_general | solution.py:51
  71.3 4.4 %collective-permute-start.3 = (bf16[640,768]{1,0:T(8,128)(2,1)}, bf16[640,768]{1,0:T(8,128)(2,1)}, u32[]{:S(2)}, u32[]{:S(2)}) collective-permute-start(bf16[640,768]{1,0:T(8,128)(2,1)} %multiply_convert_fusion.4), channel_id=1, source_target_pairs={{0,127},{1,64},{2,65},{3,66},{4,67},{5,68},{6,69},{7,70},{8,71},{9... | collective-permute-start | bytes 2949128 | tf_op jit(solution)/shard_map/ppermute | solution.py:22
  75.7 0.0 collective-permute-done.4
  75.7 3.8 %fusion.13 = bf16[1280,640]{1,0:T(8,128)(2,1)S(1)} fusion(bf16[640,768]{1,0:T(8,128)(2,1)} %collective-permute-done.4, s32[640]{0:T(1024)S(1)} %iota_add_fusion, s32[1280]{0:T(1024)S(1)} %pad_add_fusion, bf16[640,768]{1,0:T(8,128)(2,1)} %collective-permute-done, bf16[640,768]{1,0:T(8,128)(2,1)} %multiply_convert_fusion.6), kind=kOutput, calls=%fused_computation.16 | convolution fusion | flops 1269596160 | bytes 4595200 | tf_op jit(solution)/shard_map/dot_general | solution.py:37
  79.5 0.0 copy-start.12
  79.5 1.2 copy-done.12
  80.7 4.0 %multiply_convert_fusion.3 = bf16[640,768]{1,0:T(8,128)(2,1)} fusion(bf16[1280,640]{1,0:T(8,128)(2,1)S(1)} %fusion.13, bf16[640,768]{1,0:T(8,128)(2,1)} %collective-permute-done, bf16[640,768]{1,0:T(8,128)(2,1)} %multiply_convert_fusion.6), kind=kOutput, calls=%fused_computation.38 | convolution fusion | flops 1263206400 | bytes 4587520 | tf_op jit(solution)/shard_map/dot_general | solution.py:51
  84.7 0.8 collective-permute-start.5
  85.5 3.5 %subtract_convert_fusion = bf16[640,640]{1,0:T(8,128)(2,1)} fusion(bf16[640,768]{1,0:T(8,128)(2,1)} %multiply_convert_fusion.6, bf16[640,768]{1,0:T(8,128)(2,1)} %multiply_convert_fusion.5, s32[640]{0:T(1024)S(1)} %iota_add_fusion.2, s32[640]{0:T(1024)S(1)} %copy-done.9), kind=kOutput, calls=%fused_computation.44 | convolution fusion | flops 632832000 | bytes 2790400 | tf_op jit(solution)/shard_map/dot_general | solution.py:37
  89.1 3.5 %fusion.25 = f32[1280,768]{1,0:T(8,128)S(1)} fusion(bf16[1280,640]{1,0:T(8,128)(2,1)} %copy-done.12, bf16[640,768]{1,0:T(8,128)(2,1)} %collective-permute-done.4), kind=kOutput, calls=%fused_computation.59 | convolution fusion | flops 1258291200 | bytes 6553600 | tf_op jit(solution)/shard_map/dot_general | solution.py:47
  92.6 3.0 %fusion = f32[1280,768]{1,0:T(8,128)S(1)} fusion(f32[1280,768]{1,0:T(8,128)S(1)} %fusion.25, bf16[1280,640]{1,0:T(8,128)(2,1)S(1)} %copy-done.5, bf16[640,768]{1,0:T(8,128)(2,1)} %collective-permute-done.1), kind=kOutput, calls=%fused_computation.1 | convolution fusion | flops 1260257280 | bytes 10485760 | tf_op jit(solution)/shard_map/dot_general | solution.py:47
  95.7 0.0 copy-start.2
  95.7 0.1 slice.20
  95.8 1.0 collective-permute-start.6
  96.8 21.5 %collective-permute-done.3 = bf16[640,768]{1,0:T(8,128)(2,1)} collective-permute-done((bf16[640,768]{1,0:T(8,128)(2,1)}, bf16[640,768]{1,0:T(8,128)(2,1)}, u32[]{:S(2)}, u32[]{:S(2)}) %collective-permute-start.3) | collective-permute-done | bytes 983072 | tf_op jit(solution)/shard_map/ppermute | solution.py:22
  118.3 1.9 collective-permute-done.5
  120.3 3.1 %multiply_reduce_fusion.2 = (f32[640]{0:T(1024)S(1)}, f32[640,768]{1,0:T(8,128)S(1)}) fusion(f32[640,768]{1,0:T(8,128)S(1)} %copy-done.2, f32[640]{0:T(1024)S(1)} %add_rsqrt_fusion.1, bf16[640,768]{1,0:T(8,128)(2,1)} %collective-permute-done.5, bf16[640,768]{1,0:T(8,128)(2,1)} %collective-permute-done.3, bf16[640,640]{1,0:T(8,128)(2,1)S(1)} %copy-done.6, ...), kind=kOutput, calls=%fused_computation.36 | convolution fusion | flops 633077120 | bytes 7705600 | tf_op jit(solution)/shard_map/dot_general | solution.py:51
  123.4 0.0 copy-start.11
  123.4 2.2 %multiply_convert_fusion.2 = bf16[640,768]{1,0:T(8,128)(2,1)S(1)} fusion(f32[640,768]{1,0:T(8,128)S(1)} %copy-done.2, f32[640]{0:T(1024)S(1)} %get-tuple-element.17, f32[640]{0:T(1024)S(1)} %add_rsqrt_fusion.1, bf16[640,768]{1,0:T(8,128)(2,1)} %collective-permute-done.5, bf16[640,768]{1,0:T(8,128)(2,1)} %collective-permute-done.3, ...), kind=kLoop, calls=%fused_computation.35 | loop fusion | flops 4915200 | bytes 6886400 | tf_op jit(solution)/shard_map/convert_element_type | solution.py:33
  125.6 0.0 copy-start.8
  125.6 1.1 fusion.26
  126.7 0.0 copy-start.7
  126.7 0.0 collective-permute-done.6
  126.8 2.5 %multiply_reduce_fusion = (f32[640]{0:T(1024)S(1)}, f32[640,768]{1,0:T(8,128)S(1)}) fusion(f32[640,768]{1,0:T(8,128)S(1)} %get-tuple-element.16, f32[640]{0:T(1024)S(1)} %add_rsqrt_fusion.2, bf16[640,768]{1,0:T(8,128)(2,1)S(1)} %collective-permute-done.6, f32[1280,768]{1,0:T(8,128)S(1)} %fusion, bf16[640,640]{1,0:T(8,128)(2,1)S(1)} %copy-done.6, ...), kind=kOutput, calls=%fused_computation.32 | convolution fusion | flops 632585600 | bytes 8688640 | tf_op jit(solution)/shard_map/dot_general | solution.py:47
  129.3 1.5 fusion.20
  130.8 0.3 fusion.19
  131.1 0.5 collective-permute-start.7
  131.6 2.5 %collective-permute-done.7 = bf16[768,768]{1,0:T(8,128)(2,1)S(1)} collective-permute-done((bf16[768,768]{1,0:T(8,128)(2,1)S(1)}, bf16[768,768]{1,0:T(8,128)(2,1)S(1)}, u32[]{:S(2)}, u32[]{:S(2)}) %collective-permute-start.7) | collective-permute-done | bytes 1179680 | tf_op jit(solution)/shard_map/ppermute | solution.py:22
  134.1 0.4 fusion.17
  134.5 20.7 %all_to_all.20 = bf16[16,48,768]{2,1,0:T(8,128)(2,1)S(1)} all-to-all(bf16[16,48,768]{2,1,0:T(8,128)(2,1)S(1)} %bitcast.31), channel_id=1, replica_groups=mesh['y_lo'=2,'core'=2,'x'=4,'z'=8,'y_hi'=2] {'y_lo','y_hi','x'}, dimensions={0} | all-to-all | bytes 2359296 | tf_op jit(solution)/shard_map/all_to_all | solution.py:66
  155.2 0.2 reduce_sum.92
  155.4 0.1 reshape.57
  155.5 11.9 %all_to_all.21 = bf16[8,36,128]{2,1,0:T(8,128)(2,1)S(1)} all-to-all(bf16[8,36,128]{2,1,0:T(8,128)(2,1)S(1)} %reshape.57), channel_id=1, replica_groups=mesh['y_lo'=2,'core'=2,'x'=4,'z'=8,'y_hi'=2] {'z'}, dimensions={0} | all-to-all | bytes 147456 | tf_op jit(solution)/shard_map/all_to_all | solution.py:69
  167.4 9.8 %all_to_all.22 = bf16[8,36,128]{2,1,0:T(8,128)(2,1)S(1)} all-to-all(bf16[8,36,128]{2,1,0:T(8,128)(2,1)S(1)} %broadcast_in_dim.22), channel_id=1, replica_groups=mesh['y_lo'=2,'core'=2,'x'=4,'z'=8,'y_hi'=2] {'z'}, dimensions={0} | all-to-all | bytes 147456 | tf_op jit(solution)/shard_map/all_to_all | solution.py:72
  177.2 0.1 broadcast_in_dim.23
  177.3 0.1 broadcast_in_dim.24
  177.4 17.5 %all_to_all.23 = bf16[16,48,768]{2,1,0:T(8,128)(2,1)S(1)} all-to-all(bf16[16,48,768]{2,1,0:T(8,128)(2,1)S(1)} %broadcast_in_dim.24), channel_id=1, replica_groups=mesh['y_lo'=2,'core'=2,'x'=4,'z'=8,'y_hi'=2] {'y_lo','y_hi','x'}, dimensions={0} | all-to-all | bytes 2359296 | tf_op jit(solution)/shard_map/all_to_all | solution.py:74
  194.9 0.6 copy.15
  195.5 5.4 %collective-permute-start.8 = (bf16[768,768]{0,1:T(8,128)(2,1)S(1)}, bf16[768,768]{0,1:T(8,128)(2,1)S(1)}, u32[]{:S(2)}, u32[]{:S(2)}) collective-permute-start(bf16[768,768]{0,1:T(8,128)(2,1)S(1)} %copy.15), channel_id=1, source_target_pairs={{0,64},{1,65},{2,66},{3,67},{4,68},{5,69},{6,70},{7,71},{8,72},{9,... | collective-permute-start | bytes 3538952 | tf_op jit(solution)/shard_map/ppermute | solution.py:22
  200.9 2.2 %multiply_reduce_fusion.1 = (f32[640]{0:T(1024)S(1)}, f32[640,768]{1,0:T(8,128)S(1)}) fusion(bf16[640,768]{1,0:T(8,128)(2,1)} %copy-done.8, bf16[768,768]{1,0:T(8,128)(2,1)S(1)} %copy-done), kind=kOutput, calls=%fused_computation.34 | convolution fusion | flops 755957120 | bytes 4131328 | tf_op jit(solution)/shard_map/dot_general | solution.py:129
  203.2 1.1 multiply_convert_fusion.1
  204.3 0.0 collective-permute-done.8
  204.3 1.6 fusion.16
  207.3 2.7 %convert_multiply_fusion = (f32[768,768]{0,1:T(8,128)}, f32[768,768]{0,1:T(8,128)}) fusion(f32[]{:T(128)S(6)} %rsqrt.34, bf16[768,768]{0,1:T(8,128)(2,1)S(1)} %collective-permute-done.8, bf16[768,768]{0,1:T(8,128)(2,1)S(1)} %copy.15, pred[]{:T(512)S(6)} %eq.55, f32[]{:T(128)S(6)} %rsqrt.33), kind=kLoop, calls=%fused_computation.18 | loop fusion | flops 3538944 | bytes 7077897 | tf_op jit(solution)/shard_map/mul | solution.py:82
  210.0 3.2 %copy.18 = f32[768,768]{1,0:T(8,128)} copy(f32[768,768]{0,1:T(8,128)} %get-tuple-element.11) | data formatting | bytes 4718592
  213.1 1.9 copy.17
  (23 shorter events, 0.1 us)
Async XLA Ops:
  0.6 12.4 %copy-start = (bf16[768,768]{1,0:T(8,128)(2,1)S(1)}, bf16[768,768]{1,0:T(8,128)(2,1)}, u32[]{:S(2)}) copy-start(bf16[768,768]{1,0:T(8,128)(2,1)} %param.9) | copy-start | bytes 3538948
  3.3 9.7 %copy-start.10 = (bf16[640,768]{1,0:T(8,128)(2,1)S(1)}, bf16[640,768]{1,0:T(8,128)(2,1)}, u32[]{:S(2)}) copy-start(bf16[640,768]{1,0:T(8,128)(2,1)} %param.6) | copy-start | bytes 2949124
  4.5 29.3 %collective-permute-start = (bf16[640,768]{1,0:T(8,128)(2,1)}, bf16[640,768]{1,0:T(8,128)(2,1)}, u32[]{:S(2)}, u32[]{:S(2)}) collective-permute-start(bf16[640,768]{1,0:T(8,128)(2,1)} %multiply_convert_fusion.6), channel_id=1, source_target_pairs={{0,62},{1,63},{2,0},{3,1},{4,2},{5,3},{6,4},{7,5},{8,6},{9,7},{10,... | collective-permute-start | bytes 2949128 | tf_op jit(solution)/shard_map/ppermute | solution.py:22
  14.1 1.3 copy-start.1
  14.1 6.1 %copy-start.9 = (s32[640]{0:T(1024)S(1)}, s32[640]{0:T(1024)}, u32[]{:S(2)}) copy-start(s32[640]{0:T(1024)} %param.7) | copy-start | bytes 7684
  16.5 46.4 %collective-permute-start.1 = (bf16[640,768]{1,0:T(8,128)(2,1)}, bf16[640,768]{1,0:T(8,128)(2,1)}, u32[]{:S(2)}, u32[]{:S(2)}) collective-permute-start(bf16[640,768]{1,0:T(8,128)(2,1)} %multiply_convert_fusion.5), channel_id=1, source_target_pairs={{0,65},{1,66},{2,67},{3,68},{4,69},{5,70},{6,71},{7,72},{8,73},{9,... | collective-permute-start | bytes 2949128 | tf_op jit(solution)/shard_map/ppermute | solution.py:22
  20.2 55.5 %collective-permute-start.4 = (bf16[640,768]{1,0:T(8,128)(2,1)}, bf16[640,768]{1,0:T(8,128)(2,1)}, u32[]{:S(2)}, u32[]{:S(2)}) collective-permute-start(bf16[640,768]{1,0:T(8,128)(2,1)} %multiply_convert_fusion.5), channel_id=1, source_target_pairs={{0,130},{1,131},{2,132},{3,133},{4,134},{5,135},{6,136},{7,137},{8... | collective-permute-start | bytes 2949128 | tf_op jit(solution)/shard_map/ppermute | solution.py:22
  20.2 13.6 %collective-permute-start.2 = (s32[640]{0:T(1024)S(1)}, s32[640]{0:T(1024)S(1)}, u32[]{:S(2)}, u32[]{:S(2)}) collective-permute-start(s32[640]{0:T(1024)S(1)} %copy-done.9), channel_id=1, source_target_pairs={{0,62},{1,63},{2,0},{3,1},{4,2},{5,3},{6,4},{7,5},{8,6},{9,7},{10,... | collective-permute-start | bytes 7688 | tf_op jit(solution)/shard_map/ppermute | solution.py:22
  66.7 4.6 %copy-start.4 = (bf16[1280,640]{1,0:T(8,128)(2,1)}, bf16[1280,640]{1,0:T(8,128)(2,1)S(1)}, u32[]{:S(2)}) copy-start(bf16[1280,640]{1,0:T(8,128)(2,1)S(1)} %fusion.14) | copy-start | bytes 4915204
  71.3 47.0 %collective-permute-start.3 = (bf16[640,768]{1,0:T(8,128)(2,1)}, bf16[640,768]{1,0:T(8,128)(2,1)}, u32[]{:S(2)}, u32[]{:S(2)}) collective-permute-start(bf16[640,768]{1,0:T(8,128)(2,1)} %multiply_convert_fusion.4), channel_id=1, source_target_pairs={{0,127},{1,64},{2,65},{3,66},{4,67},{5,68},{6,69},{7,70},{8,71},{9... | collective-permute-start | bytes 2949128 | tf_op jit(solution)/shard_map/ppermute | solution.py:22
  79.5 1.2 copy-start.12
  84.7 35.5 %collective-permute-start.5 = (bf16[640,768]{1,0:T(8,128)(2,1)}, bf16[640,768]{1,0:T(8,128)(2,1)}, u32[]{:S(2)}, u32[]{:S(2)}) collective-permute-start(bf16[640,768]{1,0:T(8,128)(2,1)} %multiply_convert_fusion.3), channel_id=1, source_target_pairs={{0,190},{1,191},{2,128},{3,129},{4,130},{5,131},{6,132},{7,133},{8... | collective-permute-start | bytes 2949128 | tf_op jit(solution)/shard_map/ppermute | solution.py:22
  89.1 3.5 %copy-start.5 = (bf16[1280,640]{1,0:T(8,128)(2,1)S(1)}, bf16[1280,640]{1,0:T(8,128)(2,1)}, u32[]{:S(2)}) copy-start(bf16[1280,640]{1,0:T(8,128)(2,1)} %copy-done.4) | copy-start | bytes 4915204
  92.6 27.6 %copy-start.6 = (bf16[640,640]{1,0:T(8,128)(2,1)S(1)}, bf16[640,640]{1,0:T(8,128)(2,1)}, u32[]{:S(2)}) copy-start(bf16[640,640]{1,0:T(8,128)(2,1)} %subtract_convert_fusion) | copy-start | bytes 2457604
  95.7 24.6 %copy-start.2 = (f32[640,768]{1,0:T(8,128)S(1)}, f32[640,768]{1,0:T(8,128)}, u32[]{:S(2)}) copy-start(f32[640,768]{1,0:T(8,128)} %copy-done.1) | copy-start | bytes 5898244
  95.8 31.0 %collective-permute-start.6 = (bf16[640,768]{1,0:T(8,128)(2,1)S(1)}, bf16[640,768]{1,0:T(8,128)(2,1)S(1)}, u32[]{:S(2)}, u32[]{:S(2)}) collective-permute-start(bf16[640,768]{1,0:T(8,128)(2,1)S(1)} %slice.20), channel_id=1, source_target_pairs={{0,2},{1,3},{2,4},{3,5},{4,6},{5,7},{6,8},{7,9},{8,10},{9,11},{10,... | collective-permute-start | bytes 2949128 | tf_op jit(solution)/shard_map/ppermute | solution.py:22
  123.4 2.2 %copy-start.11 = (bf16[640,768]{1,0:T(8,128)(2,1)S(1)}, bf16[640,768]{1,0:T(8,128)(2,1)}, u32[]{:S(2)}) copy-start(bf16[640,768]{1,0:T(8,128)(2,1)} %param.6) | copy-start | bytes 2949124
  125.6 3.6 %copy-start.8 = (bf16[640,768]{1,0:T(8,128)(2,1)}, bf16[640,768]{1,0:T(8,128)(2,1)S(1)}, u32[]{:S(2)}) copy-start(bf16[640,768]{1,0:T(8,128)(2,1)S(1)} %multiply_convert_fusion.2) | copy-start | bytes 2949124
  126.7 2.5 %copy-start.7 = (bf16[640,768]{1,0:T(8,128)(2,1)S(1)}, bf16[640,768]{1,0:T(8,128)(2,1)}, u32[]{:S(2)}) copy-start(bf16[640,768]{1,0:T(8,128)(2,1)} %param.5) | copy-start | bytes 2949124
  131.1 3.0 %collective-permute-start.7 = (bf16[768,768]{1,0:T(8,128)(2,1)S(1)}, bf16[768,768]{1,0:T(8,128)(2,1)S(1)}, u32[]{:S(2)}, u32[]{:S(2)}) collective-permute-start(bf16[768,768]{1,0:T(8,128)(2,1)S(1)} %fusion.19), channel_id=1, source_target_pairs={{0,64},{1,65},{2,66},{3,67},{4,68},{5,69},{6,70},{7,71},{8,72},{9,... | collective-permute-start | bytes 3538952 | tf_op jit(solution)/shard_map/ppermute | solution.py:22
  195.5 8.8 %collective-permute-start.8 = (bf16[768,768]{0,1:T(8,128)(2,1)S(1)}, bf16[768,768]{0,1:T(8,128)(2,1)S(1)}, u32[]{:S(2)}, u32[]{:S(2)}) collective-permute-start(bf16[768,768]{0,1:T(8,128)(2,1)S(1)} %copy.15), channel_id=1, source_target_pairs={{0,64},{1,65},{2,66},{3,67},{4,68},{5,69},{6,70},{7,71},{8,72},{9,... | collective-permute-start | bytes 3538952 | tf_op jit(solution)/shard_map/ppermute | solution.py:22
  209.9 3.2 %copy-start.3 = (f32[768,768]{0,1:T(8,128)S(1)}, f32[768,768]{0,1:T(8,128)}, u32[]{:S(2)}) copy-start(f32[768,768]{0,1:T(8,128)} %get-tuple-element.12) | copy-start | bytes 7077892

commit v2 on v1

v2 whole, which is shorter than its diff:
```python
import functools

import jax
import jax.numpy as jnp
from jax import lax
from jax.experimental import pallas as pl
from jax.experimental.pallas import tpu as pltpu
from jax.sharding import Mesh
from jax.sharding import PartitionSpec as P

LOGIT_SCALE = 5.0
LOGIT_BIAS = -2.0
EPSILON = 1e-06

AXES = ("y_lo", "core", "x", "z", "y_hi")
SIZES = (2, 2, 4, 8, 2)
PLANE = ("y_lo", "y_hi", "x")
DEVS = 64
F32, BF16 = jnp.float32, jnp.bfloat16
VMEM, SMEM = pltpu.VMEM, pltpu.SMEM


def moved(block, flip, shift):
    pairs = []
    for source in range(4 * DEVS):
        group, dev = divmod(source, DEVS)
        pairs.append((source, (group ^ flip) * DEVS + (dev + shift) % DEVS))
    return lax.ppermute(block, AXES, pairs)


def dot(a, b, contract):
    return lax.dot_general(a, b, (contract, ((), ())), preferred_element_type=F32)


PLAIN, ROWS, COLUMNS = ((1,), (0,)), ((1,), (1,)), ((0,), (0,))


def project(inputs, weight):
    projected = dot(inputs, weight, PLAIN)
    inverse = lax.rsqrt(jnp.sum(projected * projected, axis=-1, keepdims=True) + EPSILON)
    return (projected * inverse, inverse)


def direction(grad, unit, inverse):
    inner = jnp.sum(unit * grad, axis=-1, keepdims=True)
    return ((grad - unit * inner) * inverse).astype(BF16)


def pair_weights(docids, queries, labels, doc_start):
    logits = LOGIT_SCALE * dot(docids, queries, ROWS) + LOGIT_BIAS
    rows = doc_start + lax.broadcasted_iota(jnp.int32, logits.shape, 0)
    return (jax.nn.sigmoid(logits) - jnp.where(labels == rows, 1.0, 0.0)).astype(BF16)


def own_kernel(starts, queries, docids, labels, head_query, head_docid,
               docid_vec, docid_unit, docid_inverse, docid_grad, query_head):
    unit, inverse = project(docids[...], head_docid[...])
    docid_unit[...] = unit
    docid_inverse[...] = inverse
    docid_vec[...] = unit.astype(BF16)
    unit, inverse = project(queries[...], head_query[...])
    query_vec = unit.astype(BF16)
    weights = pair_weights(docid_vec[...], query_vec, labels[...], starts[0])
    docid_grad[...] = LOGIT_SCALE * dot(weights, query_vec, PLAIN)
    query_grad = LOGIT_SCALE * dot(weights, docid_vec[...], COLUMNS)
    query_head[...] = dot(queries[...], direction(query_grad, unit, inverse), COLUMNS)


def project_kernel(docids, head_docid, docid_vec, docid_unit, docid_inverse):
    unit, inverse = project(docids[...], head_docid[...])
    docid_unit[...] = unit
    docid_inverse[...] = inverse
    docid_vec[...] = unit.astype(BF16)


def pair(starts, queries, labels, head_query, docid_vec, far_vec, docid_in, head_in):
    unit, inverse = project(queries[...], head_query[...])
    query_vec = unit.astype(BF16)
    weights = pair_weights(far_vec[...], query_vec, labels[...], starts[1])
    far_grad = LOGIT_SCALE * dot(weights, query_vec, PLAIN)
    query_grad = dot(weights, far_vec[...], COLUMNS)
    weights = pair_weights(docid_vec[...], query_vec, labels[...], starts[0])
    docid_grad = docid_in[...] + LOGIT_SCALE * dot(weights, query_vec, PLAIN)
    query_grad = LOGIT_SCALE * (query_grad + dot(weights, docid_vec[...], COLUMNS))
    head = head_in[...] + dot(queries[...], direction(query_grad, unit, inverse), COLUMNS)
    return docid_grad, far_grad, head


def pair_kernel(*refs):
    ins, outs = refs[:8], refs[8:]
    for out, value in zip(outs, pair(*ins), strict=True):
        out[...] = value


def last_kernel(starts, queries, labels, head_query, docid_vec, far_vec, docid_in, head_in, far_in,
                docids, docid_unit, docid_inverse, far, far_unit, far_inverse,
                docid_out, far_sent, kept, sent):
    docid_grad, far_grad, query = pair(
        starts, queries, labels, head_query, docid_vec, far_vec, docid_in, head_in
    )
    far_grad = far_grad + far_in[...]
    docid_out[...] = docid_grad
    far_sent[...] = far_grad.astype(BF16)
    head = dot(docids[...], direction(docid_grad, docid_unit[...], docid_inverse[...]), COLUMNS)
    head = head + dot(far[...], direction(far_grad, far_unit[...], far_inverse[...]), COLUMNS)
    mine = jnp.zeros(head.shape, jnp.int32) + starts[2] == 0
    kept[...] = jnp.where(mine, query, head)
    sent[...] = jnp.where(mine, head, query).astype(BF16)


def update_kernel(docid_grad, back, docid_unit, docid_inverse, head_docid, update):
    grad = docid_grad[...] + back[...].astype(F32)
    direct = direction(grad, docid_unit[...], docid_inverse[...])
    grad = dot(direct, head_docid[...], ROWS)
    scale = lax.rsqrt(jnp.mean(grad * grad, axis=-1, keepdims=True) + EPSILON)
    update[...] = (grad * scale).astype(BF16)


def unit_rms(grad):
    return grad * lax.rsqrt(jnp.sum(grad * grad) / (grad.shape[0] * grad.shape[1]) + EPSILON)


def step_kernel(starts, mine, other, query_step, docid_step):
    mine_step = unit_rms(mine[...].astype(F32))
    other_step = unit_rms(other[...].astype(F32))
    here = jnp.zeros(mine_step.shape, jnp.int32) + starts[2] == 0
    query_step[...] = jnp.where(here, mine_step, other_step)
    docid_step[...] = jnp.where(here, other_step, mine_step)


def call(kernel, outs, *args, flops=0, scalars=True):
    specs = [pl.BlockSpec(memory_space=VMEM) for _ in args]
    if scalars:
        specs[0] = pl.BlockSpec(memory_space=SMEM)
    moved_bytes = sum(a.size * a.dtype.itemsize for a in args)
    moved_bytes += sum(o.size * o.dtype.itemsize for o in outs)
    return pl.pallas_call(
        kernel,
        out_shape=outs,
        in_specs=specs,
        out_specs=[pl.BlockSpec(memory_space=VMEM) for _ in outs],
        compiler_params=pltpu.CompilerParams(vmem_limit_bytes=20 * 2**20),
        cost_estimate=pl.CostEstimate(flops=flops, transcendentals=0, bytes_accessed=moved_bytes),
    )(*args)


def total(kept, sent, back):
    rows, width = kept.shape
    value = kept + moved(sent, 1, 0).astype(F32)
    plane, line = SIZES[0] * SIZES[2] * SIZES[4], SIZES[3]
    piece = value.astype(BF16).reshape(plane, rows // plane, width)
    piece = lax.all_to_all(piece, PLANE, 0, 0, tiled=True)
    piece = jnp.sum(piece.astype(F32), axis=0).astype(BF16)
    piece, back = lax.optimization_barrier((piece, back))
    piece = jnp.broadcast_to(piece[None], (line,) + piece.shape)
    piece = lax.all_to_all(piece, "z", 0, 0, tiled=True)
    piece = jnp.sum(piece.astype(F32), axis=0).astype(BF16)
    piece = jnp.broadcast_to(piece[None], (plane,) + piece.shape)
    mine = lax.all_to_all(piece, PLANE, 0, 0, tiled=True).reshape(rows, width)
    return mine, moved(mine, 1, 0), back


def per_device(queries, docids, labels, head_query, head_docid):
    rows, width = queries.shape
    side = head_query.shape[1]
    core = lax.axis_index("core")
    group = lax.axis_index("y_lo") * 2 + core
    dev = (lax.axis_index("x") * 8 + lax.axis_index("z")) * 2 + lax.axis_index("y_hi")
    own_start = (group * DEVS + dev) * rows
    far_start = (group * DEVS + (dev - 2) % DEVS) * rows
    starts = jnp.stack([own_start, far_start, core]).astype(jnp.int32)

    queries_2, labels_2 = moved(queries, 2, -2), moved(labels, 2, -2)
    far = moved(docids, 0, 2)
    queries_1, labels_1 = moved(queries, 1, -1), moved(labels, 1, -1)

    def out(shape, dtype=F32):
        return jax.ShapeDtypeStruct(shape, dtype)

    block, column, head = (rows, side), (rows, 1), (width, side)
    mul = 2 * rows * width * side
    pair_flops = 2 * rows * rows * side
    docid_vec, docid_unit, docid_inverse, docid_grad, query_head = call(
        own_kernel,
        [out(block, BF16), out(block), out(column), out(block), out(head)],
        starts, queries, docids, labels[None], head_query, head_docid,
        flops=3 * mul + 3 * pair_flops,
    )
    far_vec, far_unit, far_inverse = call(
        project_kernel,
        [out(block, BF16), out(block), out(column)],
        far, head_docid,
        flops=mul, scalars=False,
    )
    docid_grad, far_grad, query_head = call(
        pair_kernel,
        [out(block), out(block), out(head)],
        starts, queries_2, labels_2[None], head_query, docid_vec, far_vec, docid_grad, query_head,
        flops=2 * mul + 6 * pair_flops,
    )
    queries_1, labels_1, far_grad = lax.optimization_barrier((queries_1, labels_1, far_grad))
    docid_grad, far_sent, kept, sent = call(
        last_kernel,
        [out(block), out(block, BF16), out(head), out(head, BF16)],
        starts, queries_1, labels_1[None], head_query, docid_vec, far_vec, docid_grad, query_head, far_grad,
        docids, docid_unit, docid_inverse, far, far_unit, far_inverse,
        flops=4 * mul + 6 * pair_flops,
    )
    back = moved(far_sent, 0, -2)
    mine, other, back = total(kept, sent, back)
    (doc_update,) = call(
        update_kernel,
        [out((rows, width), BF16)],
        docid_grad, back, docid_unit, docid_inverse, head_docid,
        flops=mul, scalars=False,
    )
    query_step, docid_step = call(step_kernel, [out(head), out(head)], starts, mine, other)
    return (doc_update, query_step, docid_step)


def solution(mesh):
    split = Mesh(mesh.devices.reshape(SIZES), AXES)
    rows = P(AXES)
    return jax.shard_map(
        per_device,
        mesh=split,
        in_specs=(rows, rows, rows, P(), P()),
        out_specs=(rows, P(), P()),
        check_vma=False,
    )
```

time: 216 us -> 168 us (0.78)
  matrix products: 40.4 us -> 0 us
  Pallas kernels: 0 us -> 37.4 us
  waiting for transfers between devices: 63.7 us -> 34.1 us
  blocking collectives: 59.9 us -> 50.4 us
  other arithmetic: 10.7 us -> 4 us
  starting transfers between devices: 29.5 us -> 35.1 us
  local copies, waits for them, and re-layouts: 8.62 us -> 5.79 us
    ppermute x9 -> x8, waiting for transfers between devices: 63.7 us -> 22.5 us  [moved(): return lax.ppermute(block, AXES, pairs)]
    dot_general x14 -> x0, matrix products: 40.4 us -> none  [the longest x3 11.7 us: columns_of(): lax.dot_general(weights, queries, (((0,), (0,)), ((), ())), preferred_ele...]
    pallas_call x0 -> x6, Pallas kernels: none -> 37.4 us  [call(): pl.pallas_call(kernel, out_shape=outs, in_specs=specs, out_specs=[pl.Bloc...]
    all_to_all x3 -> x1, blocking collectives: 48 us -> 21.9 us  [total(): mine = lax.all_to_all(piece, PLANE, 0, 0, tiled=True).reshape(rows, width)]
    all_to_all x1, blocking collectives: 11.9 us -> 28.6 us  [total(): piece = lax.all_to_all(piece, 'z', 0, 0, tiled=True)]
    all_to_all x0 -> x1, waiting for transfers between devices: none -> 11.6 us  [total(): piece = lax.all_to_all(piece, PLANE, 0, 0, tiled=True)]
    convert_element_type x6 -> x1, other arithmetic: 6.27 us -> 1.34 us  [total(): piece = value.astype(BF16).reshape(plane, rows // plane, width)]
    all_to_all x0 -> x1, starting transfers between devices: none -> 4.39 us  [total(): piece = lax.all_to_all(piece, PLANE, 0, 0, tiled=True)]
  transfers between devices with their start and end apart: 9 -> 9, of which waited for: 5 -> 5; matrix products, arithmetic and copies ran while one was open for 18% -> 1% of each run, Pallas kernels for 0% -> 13%
where the time goes in v2:
time: 168 us
  blocking collectives  50.4 us (30%)
  Pallas kernels  37.4 us (22%)
  starting transfers between devices  35.1 us (21%)
  waiting for transfers between devices  34.1 us (20%)
  local copies, waits for them, and re-layouts  5.79 us (3%)
  other arithmetic  4 us (2%)
    pallas_call x6, Pallas kernels, call(): pl.pallas_call(kernel, out_shape=outs, in_specs=specs, out_specs=[pl.Bloc...  37.4 us
    ppermute x8, starting transfers between devices, moved(): return lax.ppermute(block, AXES, pairs)  30.7 us
    all_to_all x1, blocking collectives, total(): piece = lax.all_to_all(piece, 'z', 0, 0, tiled=True)  28.6 us
    ppermute x8, waiting for transfers between devices, moved(): return lax.ppermute(block, AXES, pairs)  22.5 us
    all_to_all x1, blocking collectives, total(): mine = lax.all_to_all(piece, PLANE, 0, 0, tiled=True).reshape(rows, width)  21.9 us
    all_to_all x1, waiting for transfers between devices, total(): piece = lax.all_to_all(piece, PLANE, 0, 0, tiled=True)  11.6 us
    unnamed x20, local copies, waits for them, and re-layouts  4.98 us
    all_to_all x1, starting transfers between devices, total(): piece = lax.all_to_all(piece, PLANE, 0, 0, tiled=True)  4.39 us
  transfers between devices with their start and end apart: 9, of which 5 were waited for; matrix products, arithmetic and copies ran while one was open for 1% of the time, Pallas kernels for 13%

profile of v2, /device:TPU:1, one launch (start us, length us, event | category | flops | bytes accessed | tf_op | source)
XLA Modules:
  0.0 167.5 jit_solution(6803764357509034264)
XLA Ops:
  0.6 2.5 %collective-permute-start.4 = (bf16[640,768]{1,0:T(8,128)(2,1)}, bf16[640,768]{1,0:T(8,128)(2,1)}, u32[]{:S(2)}, u32[]{:S(2)}) collective-permute-start(bf16[640,768]{1,0:T(8,128)(2,1)} %docids.3), channel_id=1, source_target_pairs={{0,2},{1,3},{2,4},{3,5},{4,6},{5,7},{6,8},{7,9},{8,10},{9,11},{10,... | collective-permute-start | bytes 2949128 | tf_op jit(solution)/shard_map/ppermute | solution.py:28
  3.2 7.2 %collective-permute-start.2 = (bf16[640,768]{1,0:T(8,128)(2,1)}, bf16[640,768]{1,0:T(8,128)(2,1)}, u32[]{:S(2)}, u32[]{:S(2)}) collective-permute-start(bf16[640,768]{1,0:T(8,128)(2,1)} %queries.1), channel_id=1, source_target_pairs={{0,190},{1,191},{2,128},{3,129},{4,130},{5,131},{6,132},{7,133},{8... | collective-permute-start | bytes 2949128 | tf_op jit(solution)/shard_map/ppermute | solution.py:28
  10.4 4.8 %collective-permute-start.1 = (s32[640]{0:T(1024)}, s32[640]{0:T(1024)S(1)}, u32[]{:S(2)}, u32[]{:S(2)}) collective-permute-start(s32[640]{0:T(1024)} %param.7), channel_id=1, source_target_pairs={{0,127},{1,64},{2,65},{3,66},{4,67},{5,68},{6,69},{7,70},{8,71},{9... | collective-permute-start | bytes 7688 | tf_op jit(solution)/shard_map/ppermute | solution.py:28
  15.2 0.3 collective-permute-start.3
  15.5 0.9 collective-permute-start
  16.4 0.1 pad_add_fusion.starts.refs_0_
  16.5 0.7 broadcast_in_dim.22.labels
  17.2 0.0 copy-start.2
  17.2 1.3 copy-done.2
  18.5 0.0 copy-start.4
  18.5 1.3 copy-done.4
  19.7 0.0 copy-start.6
  19.7 1.2 copy-done.6
  20.9 0.0 copy-start.7
  20.9 1.2 copy-done.7
  22.1 0.0 copy-start.3
  22.1 6.6 %shard_map.76 = (bf16[640,768]{1,0:T(8,128)(2,1)S(1)}, f32[640,768]{1,0:T(8,128)S(1)}, f32[640,1]{1,0:T(8,128)S(1)}, f32[640,768]{1,0:T(8,128)S(1)}, f32[768,768]{1,0:T(8,128)S(1)}) custom-call(s32[3]{0:T(128)S(1)} %pad_add_fusion.starts.refs_0_, bf16[640,768]{1,0:T(8,128)(2,1)S(1)} %copy-done.6, bf16[640,768]{1,0:T(8,128)(2,1)S(1)} %copy-done.7, ...), custom_call_target="tpu_custom_call" | custom-call | flops 4152360960 | bytes 11605004 | tf_op jit(solution)/shard_map/pallas_call | solution.py:137
  28.8 0.0 copy-start.5
  28.8 2.4 %collective-permute-done.3 = s32[640]{0:T(1024)S(1)} collective-permute-done((s32[640]{0:T(1024)}, s32[640]{0:T(1024)S(1)}, u32[]{:S(2)}, u32[]{:S(2)}) %collective-permute-start.3) | collective-permute-done | bytes 2592 | tf_op jit(solution)/shard_map/ppermute | solution.py:28
  31.2 0.0 collective-permute-done.4.docids.far
  31.2 0.0 copy-done.3
  31.2 2.3 %shard_map.77 = (bf16[640,768]{1,0:T(8,128)(2,1)S(1)}, f32[640,768]{1,0:T(8,128)S(1)}, f32[640,1]{1,0:T(8,128)S(1)}) custom-call(bf16[640,768]{1,0:T(8,128)(2,1)} %collective-permute-done.4.docids.far, bf16[768,768]{1,0:T(8,128)(2,1)S(1)} %copy-done.3), custom_call_target="tpu_custom_call" | custom-call | flops 754974720 | bytes 5114368 | tf_op jit(solution)/shard_map/pallas_call | solution.py:137
  33.5 0.0 collective-permute-done.2.refs_1_
  33.6 0.0 copy-done.5
  33.6 0.0 copy-start.8
  33.6 9.1 %shard_map.78 = (f32[640,768]{1,0:T(8,128)S(1)}, f32[640,768]{1,0:T(8,128)S(1)}, f32[768,768]{1,0:T(8,128)S(1)}) custom-call(s32[3]{0:T(128)S(1)} %pad_add_fusion.starts.refs_0_, bf16[640,768]{1,0:T(8,128)(2,1)} %collective-permute-done.2.refs_1_, s32[1,640]{1,0:T(1,128)S(1)} %broadcast_in_dim.10.refs_2_, bf16[768,768]{1,0:T(8,128)(2,1)S(1)} %copy-done.5, ...), custom_call_target="tpu_custom_call" | custom-call | flops 5284823040 | bytes 14748172 | tf_op jit(solution)/shard_map/pallas_call | solution.py:137
  42.7 0.0 collective-permute-done.1
  42.7 9.7 %collective-permute-done.queries = bf16[640,768]{1,0:T(8,128)(2,1)} collective-permute-done((bf16[640,768]{1,0:T(8,128)(2,1)}, bf16[640,768]{1,0:T(8,128)(2,1)}, u32[]{:S(2)}, u32[]{:S(2)}) %collective-permute-start) | collective-permute-done | bytes 983072 | tf_op jit(solution)/shard_map/ppermute | solution.py:28
  52.4 0.0 copy-done.8
  52.4 11.7 %shard_map.79 = (f32[640,768]{1,0:T(8,128)S(1)}, bf16[640,768]{1,0:T(8,128)(2,1)S(1)}, f32[768,768]{1,0:T(8,128)S(1)}, bf16[768,768]{1,0:T(8,128)(2,1)S(1)}) custom-call(s32[3]{0:T(128)S(1)} %pad_add_fusion.starts.refs_0_, bf16[640,768]{1,0:T(8,128)(2,1)} %collective-permute-done.queries, s32[1,640]{1,0:T(1,128)S(1)} %broadcast_in_dim.23.labels, ...), custom_call_target="tpu_custom_call" | custom-call | flops 6794772480 | bytes 22814220 | tf_op jit(solution)/shard_map/pallas_call | solution.py:137
  64.1 0.0 copy-start
  64.1 0.0 copy-start.9
  64.1 1.6 collective-permute-start.5
  65.8 2.5 %collective-permute-done.5 = bf16[768,768]{1,0:T(8,128)(2,1)S(1)} collective-permute-done((bf16[768,768]{1,0:T(8,128)(2,1)S(1)}, bf16[768,768]{1,0:T(8,128)(2,1)S(1)}, u32[]{:S(2)}, u32[]{:S(2)}) %collective-permute-start.5) | collective-permute-done | bytes 1179680 | tf_op jit(solution)/shard_map/ppermute | solution.py:28
  68.2 1.3 add_convert_fusion
  69.6 0.0 copy-done
  69.6 0.0 copy-done.9
  69.6 4.4 %all-to-all-start = ((bf16[16,48,768]{2,1,0:T(8,128)(2,1)}), bf16[16,48,768]{2,1,0:T(8,128)(2,1)}, u32[]{:S(2)}, u32[]{:S(2)}) async-start(bf16[16,48,768]{2,1,0:T(8,128)(2,1)} %bitcast.7), calls=%async_computation | async-start | bytes 2359296 | tf_op jit(solution)/shard_map/all_to_all | solution.py:152
  74.0 7.7 %collective-permute-start.6 = (bf16[640,768]{1,0:T(8,128)(2,1)}, bf16[640,768]{1,0:T(8,128)(2,1)}, u32[]{:S(2)}, u32[]{:S(2)}) collective-permute-start(bf16[640,768]{1,0:T(8,128)(2,1)} %copy-done.9), channel_id=1, source_target_pairs={{0,62},{1,63},{2,0},{3,1},{4,2},{5,3},{6,4},{7,5},{8,6},{9,7},{10,... | collective-permute-start | bytes 2949128 | tf_op jit(solution)/shard_map/ppermute | solution.py:28
  81.6 11.6 %all-to-all-done = bf16[16,48,768]{2,1,0:T(8,128)(2,1)} async-done(((bf16[16,48,768]{2,1,0:T(8,128)(2,1)}), bf16[16,48,768]{2,1,0:T(8,128)(2,1)}, u32[]{:S(2)}, u32[]{:S(2)}) %all-to-all-start) | async-done | bytes 1179680 | tf_op jit(solution)/shard_map/all_to_all | solution.py:152
  93.3 1.4 reduce_sum.24
  94.7 7.9 %collective-permute-done.6.back = bf16[640,768]{1,0:T(8,128)(2,1)} collective-permute-done((bf16[640,768]{1,0:T(8,128)(2,1)}, bf16[640,768]{1,0:T(8,128)(2,1)}, u32[]{:S(2)}, u32[]{:S(2)}) %collective-permute-start.6) | collective-permute-done | bytes 983072 | tf_op jit(solution)/shard_map/ppermute | solution.py:28
  102.6 28.6 %all_to_all.15 = bf16[8,48,768]{2,1,0:T(8,128)(2,1)} all-to-all(bf16[8,48,768]{2,1,0:T(8,128)(2,1)S(1)} %broadcast_in_dim.24), channel_id=1, replica_groups=mesh['y_lo'=2,'core'=2,'x'=4,'z'=8,'y_hi'=2] {'z'}, dimensions={0} | all-to-all | bytes 1179648 | tf_op jit(solution)/shard_map/all_to_all | solution.py:156
  131.2 1.1 reduce_sum.25
  132.3 0.0 copy-start.1
  132.3 0.1 broadcast_in_dim.25
  132.4 21.9 %all_to_all.16 = bf16[16,48,768]{2,1,0:T(8,128)(2,1)S(1)} all-to-all(bf16[16,48,768]{2,1,0:T(8,128)(2,1)S(1)} %broadcast_in_dim.25), channel_id=1, replica_groups=mesh['y_lo'=2,'core'=2,'x'=4,'z'=8,'y_hi'=2] {'y_lo','y_hi','x'}, dimensions={0} | all-to-all | bytes 2359296 | tf_op jit(solution)/shard_map/all_to_all | solution.py:159
  154.3 5.6 %collective-permute-start.7 = (bf16[768,768]{1,0:T(8,128)(2,1)S(1)}, bf16[768,768]{1,0:T(8,128)(2,1)S(1)}, u32[]{:S(2)}, u32[]{:S(2)}) collective-permute-start(bf16[768,768]{1,0:T(8,128)(2,1)S(1)} %bitcast.5), channel_id=1, source_target_pairs={{0,64},{1,65},{2,66},{3,67},{4,68},{5,69},{6,70},{7,71},{8,72},{9,... | collective-permute-start | bytes 3538952 | tf_op jit(solution)/shard_map/ppermute | solution.py:28
  159.9 0.0 copy-done.1
  159.9 3.6 %shard_map.80 = bf16[640,768]{1,0:T(8,128)(2,1)} custom-call(f32[640,768]{1,0:T(8,128)S(1)} %copy-done.1, bf16[640,768]{1,0:T(8,128)(2,1)} %collective-permute-done.6.back, f32[640,768]{1,0:T(8,128)S(1)} %get-tuple-element.35.docid_unit, f32[640,1]{1,0:T(8,128)S(1)} %get-tuple-element.36.docid_inverse, bf16[768,768]{1,0:T(8,128)(2,1)S(1)} %copy-done.3), custom_call_target="tpu_custom_call" | custom-call | flops 754974720 | bytes 7080448 | tf_op jit(solution)/shard_map/pallas_call | solution.py:137
  163.5 0.0 collective-permute-done.7.other
  163.5 4.0 %shard_map.81 = (f32[768,768]{1,0:T(8,128)}, f32[768,768]{1,0:T(8,128)}) custom-call(s32[3]{0:T(128)S(1)} %pad_add_fusion.starts.refs_0_, bf16[768,768]{1,0:T(8,128)(2,1)S(1)} %bitcast.6, bf16[768,768]{1,0:T(8,128)(2,1)S(1)} %collective-permute-done.7.other), custom_call_target="tpu_custom_call" | custom-call | bytes 7077900 | tf_op jit(solution)/shard_map/pallas_call | solution.py:137
  (3 shorter events, 0.0 us)
Async XLA Ops:
  0.6 30.6 %collective-permute-start.4 = (bf16[640,768]{1,0:T(8,128)(2,1)}, bf16[640,768]{1,0:T(8,128)(2,1)}, u32[]{:S(2)}, u32[]{:S(2)}) collective-permute-start(bf16[640,768]{1,0:T(8,128)(2,1)} %docids.3), channel_id=1, source_target_pairs={{0,2},{1,3},{2,4},{3,5},{4,6},{5,7},{6,8},{7,9},{8,10},{9,11},{10,... | collective-permute-start | bytes 2949128 | tf_op jit(solution)/shard_map/ppermute | solution.py:28
  3.2 30.4 %collective-permute-start.2 = (bf16[640,768]{1,0:T(8,128)(2,1)}, bf16[640,768]{1,0:T(8,128)(2,1)}, u32[]{:S(2)}, u32[]{:S(2)}) collective-permute-start(bf16[640,768]{1,0:T(8,128)(2,1)} %queries.1), channel_id=1, source_target_pairs={{0,190},{1,191},{2,128},{3,129},{4,130},{5,131},{6,132},{7,133},{8... | collective-permute-start | bytes 2949128 | tf_op jit(solution)/shard_map/ppermute | solution.py:28
  10.4 32.3 %collective-permute-start.1 = (s32[640]{0:T(1024)}, s32[640]{0:T(1024)S(1)}, u32[]{:S(2)}, u32[]{:S(2)}) collective-permute-start(s32[640]{0:T(1024)} %param.7), channel_id=1, source_target_pairs={{0,127},{1,64},{2,65},{3,66},{4,67},{5,68},{6,69},{7,70},{8,71},{9... | collective-permute-start | bytes 7688 | tf_op jit(solution)/shard_map/ppermute | solution.py:28
  15.2 16.0 %collective-permute-start.3 = (s32[640]{0:T(1024)}, s32[640]{0:T(1024)S(1)}, u32[]{:S(2)}, u32[]{:S(2)}) collective-permute-start(s32[640]{0:T(1024)} %param.7), channel_id=1, source_target_pairs={{0,190},{1,191},{2,128},{3,129},{4,130},{5,131},{6,132},{7,133},{8... | collective-permute-start | bytes 7688 | tf_op jit(solution)/shard_map/ppermute | solution.py:28
  15.5 36.8 %collective-permute-start = (bf16[640,768]{1,0:T(8,128)(2,1)}, bf16[640,768]{1,0:T(8,128)(2,1)}, u32[]{:S(2)}, u32[]{:S(2)}) collective-permute-start(bf16[640,768]{1,0:T(8,128)(2,1)} %queries.1), channel_id=1, source_target_pairs={{0,127},{1,64},{2,65},{3,66},{4,67},{5,68},{6,69},{7,70},{8,71},{9... | collective-permute-start | bytes 2949128 | tf_op jit(solution)/shard_map/ppermute | solution.py:28
  17.2 1.3 copy-start.2
  18.5 1.3 copy-start.4
  19.7 1.2 copy-start.6
  20.9 1.2 copy-start.7
  22.1 9.1 %copy-start.3 = (bf16[768,768]{1,0:T(8,128)(2,1)S(1)}, bf16[768,768]{1,0:T(8,128)(2,1)}, u32[]{:S(2)}) copy-start(bf16[768,768]{1,0:T(8,128)(2,1)} %head_docid.5) | copy-start | bytes 3538948
  28.8 4.8 %copy-start.5 = (bf16[768,768]{1,0:T(8,128)(2,1)S(1)}, bf16[768,768]{1,0:T(8,128)(2,1)}, u32[]{:S(2)}) copy-start(bf16[768,768]{1,0:T(8,128)(2,1)} %head_query.3) | copy-start | bytes 3538948
  33.6 18.8 %copy-start.8 = (bf16[640,768]{1,0:T(8,128)(2,1)S(1)}, bf16[640,768]{1,0:T(8,128)(2,1)}, u32[]{:S(2)}) copy-start(bf16[640,768]{1,0:T(8,128)(2,1)} %docids.3) | copy-start | bytes 2949124
  64.1 5.5 %copy-start = (f32[640,768]{1,0:T(8,128)}, f32[640,768]{1,0:T(8,128)S(1)}, u32[]{:S(2)}) copy-start(f32[640,768]{1,0:T(8,128)S(1)} %get-tuple-element.39.docid_grad) | copy-start | bytes 5898244
  64.1 5.5 %copy-start.9 = (bf16[640,768]{1,0:T(8,128)(2,1)}, bf16[640,768]{1,0:T(8,128)(2,1)S(1)}, u32[]{:S(2)}) copy-start(bf16[640,768]{1,0:T(8,128)(2,1)S(1)} %get-tuple-element.42) | copy-start | bytes 2949124
  64.1 4.1 %collective-permute-start.5 = (bf16[768,768]{1,0:T(8,128)(2,1)S(1)}, bf16[768,768]{1,0:T(8,128)(2,1)S(1)}, u32[]{:S(2)}, u32[]{:S(2)}) collective-permute-start(bf16[768,768]{1,0:T(8,128)(2,1)S(1)} %get-tuple-element.41), channel_id=1, source_target_pairs={{0,64},{1,65},{2,66},{3,67},{4,68},{5,69},{6,70},{7,71},{8,72},{9,... | collective-permute-start | bytes 3538952 | tf_op jit(solution)/shard_map/ppermute | solution.py:28
  69.6 23.7 %all-to-all-start = ((bf16[16,48,768]{2,1,0:T(8,128)(2,1)}), bf16[16,48,768]{2,1,0:T(8,128)(2,1)}, u32[]{:S(2)}, u32[]{:S(2)}) async-start(bf16[16,48,768]{2,1,0:T(8,128)(2,1)} %bitcast.7), calls=%async_computation | async-start | bytes 2359296 | tf_op jit(solution)/shard_map/all_to_all | solution.py:152
  74.0 28.6 %collective-permute-start.6 = (bf16[640,768]{1,0:T(8,128)(2,1)}, bf16[640,768]{1,0:T(8,128)(2,1)}, u32[]{:S(2)}, u32[]{:S(2)}) collective-permute-start(bf16[640,768]{1,0:T(8,128)(2,1)} %copy-done.9), channel_id=1, source_target_pairs={{0,62},{1,63},{2,0},{3,1},{4,2},{5,3},{6,4},{7,5},{8,6},{9,7},{10,... | collective-permute-start | bytes 2949128 | tf_op jit(solution)/shard_map/ppermute | solution.py:28
  132.3 27.5 %copy-start.1 = (f32[640,768]{1,0:T(8,128)S(1)}, f32[640,768]{1,0:T(8,128)}, u32[]{:S(2)}) copy-start(f32[640,768]{1,0:T(8,128)} %copy-done) | copy-start | bytes 5898244
  154.3 9.2 %collective-permute-start.7 = (bf16[768,768]{1,0:T(8,128)(2,1)S(1)}, bf16[768,768]{1,0:T(8,128)(2,1)S(1)}, u32[]{:S(2)}, u32[]{:S(2)}) collective-permute-start(bf16[768,768]{1,0:T(8,128)(2,1)S(1)} %bitcast.5), channel_id=1, source_target_pairs={{0,64},{1,65},{2,66},{3,67},{4,68},{5,69},{6,70},{7,71},{8,72},{9,... | collective-permute-start | bytes 3538952 | tf_op jit(solution)/shard_map/ppermute | solution.py:28

commit v3 on v2

v3 whole, which is shorter than its diff:
```python
import functools

import jax
import jax.numpy as jnp
from jax import lax
from jax.experimental import pallas as pl
from jax.experimental.pallas import tpu as pltpu
from jax.sharding import Mesh
from jax.sharding import PartitionSpec as P

LOGIT_SCALE = 5.0
LOGIT_BIAS = -2.0
EPSILON = 1e-06

AXES = ("y_lo", "core", "x", "z", "y_hi")
SIZES = (2, 2, 4, 8, 2)
PLANE = ("y_lo", "y_hi", "x")
DEVS = 64
F32, BF16 = jnp.float32, jnp.bfloat16
VMEM, SMEM = pltpu.VMEM, pltpu.SMEM


def moved(block, flip, shift):
    pairs = []
    for source in range(4 * DEVS):
        group, dev = divmod(source, DEVS)
        pairs.append((source, (group ^ flip) * DEVS + (dev + shift) % DEVS))
    return lax.ppermute(block, AXES, pairs)


def dot(a, b, contract):
    return lax.dot_general(a, b, (contract, ((), ())), preferred_element_type=F32)


PLAIN, ROWS, COLUMNS = ((1,), (0,)), ((1,), (1,)), ((0,), (0,))


def project(inputs, weight):
    projected = dot(inputs, weight, PLAIN)
    inverse = lax.rsqrt(jnp.sum(projected * projected, axis=-1, keepdims=True) + EPSILON)
    return (projected * inverse, inverse)


def direction(grad, unit, scale):
    inner = jnp.sum(unit * grad, axis=-1, keepdims=True)
    return ((grad - unit * inner) * scale).astype(BF16)


def pair_weights(docids, queries, labels, doc_start):
    logits = LOGIT_SCALE * dot(docids, queries, ROWS) + LOGIT_BIAS
    rows = doc_start + lax.broadcasted_iota(jnp.int32, logits.shape, 0)
    return (jax.nn.sigmoid(logits) - jnp.where(labels == rows, 1.0, 0.0)).astype(BF16)


def pack_kernel(start, labels, queries, packed):
    count = packed.shape[0] - 16
    packed[0:count, :] = queries[start : start + count, :]
    label = labels[:, start : start + count]
    row = lax.broadcasted_iota(jnp.int32, (16, count), 0)
    digit = jnp.where(row == 0, label & 63, jnp.where(row == 1, (label >> 6) & 63, label >> 12))
    packed[count : count + 16, :] = jnp.zeros((16, packed.shape[1]), BF16)
    packed[count : count + 16, 0:count] = jnp.where(row < 3, digit, 0).astype(F32).astype(BF16)


def pack(labels, queries, start, count):
    (packed,) = call(
        functools.partial(pack_kernel, start),
        [jax.ShapeDtypeStruct((count + 16, queries.shape[1]), BF16)],
        labels, queries,
        scalars=False,
    )
    return packed


def unpacked(part):
    count = part.shape[0] - 16
    digits = part[count : count + 16, 0:count].astype(F32)
    labels = digits[0:1] + 64.0 * digits[1:2] + 4096.0 * digits[2:3]
    return part[0:count, :], labels.astype(jnp.int32)


def own_kernel(starts, labels, queries, docids, head_query, head_docid,
               docid_vec, docid_unit, docid_scale, docid_grad, query_head):
    unit, inverse = project(docids[...], head_docid[...])
    docid_unit[...] = unit
    docid_scale[...] = LOGIT_SCALE * inverse
    vec = unit.astype(BF16)
    docid_vec[...] = vec
    unit, inverse = project(queries[...], head_query[...])
    query_vec = unit.astype(BF16)
    weights = pair_weights(vec, query_vec, labels[...], starts[0])
    docid_grad[...] = dot(weights, query_vec, PLAIN)
    query_grad = dot(weights, vec, COLUMNS)
    query_head[...] = dot(queries[...], direction(query_grad, unit, LOGIT_SCALE * inverse), COLUMNS)


def pair(starts, part, head_query, docid_vec, far_vec):
    queries, labels = unpacked(part)
    unit, inverse = project(queries, head_query[...])
    query_vec = unit.astype(BF16)
    weights = pair_weights(far_vec, query_vec, labels, starts[1])
    far_grad = dot(weights, query_vec, PLAIN)
    query_grad = dot(weights, far_vec, COLUMNS)
    weights = pair_weights(docid_vec, query_vec, labels, starts[0])
    docid_grad = dot(weights, query_vec, PLAIN)
    query_grad = query_grad + dot(weights, docid_vec, COLUMNS)
    head = dot(queries, direction(query_grad, unit, LOGIT_SCALE * inverse), COLUMNS)
    return docid_grad, far_grad, head


def first_kernel(starts, part, head_query, docid_vec, docid_in, head_in, far, head_docid,
                 docid_out, far_out, head_out, far_vec, far_unit, far_scale):
    unit, inverse = project(far[...], head_docid[...])
    far_unit[...] = unit
    far_scale[...] = LOGIT_SCALE * inverse
    vec = unit.astype(BF16)
    far_vec[...] = vec
    docid_grad, far_out[...], head = pair(starts, part, head_query, docid_vec[...], vec)
    docid_out[...] = docid_in[...] + docid_grad
    head_out[...] = head_in[...] + head


def next_kernel(starts, part, head_query, docid_vec, docid_in, head_in, far_vec, far_in,
                docid_out, far_out, head_out):
    docid_grad, far_grad, head = pair(starts, part, head_query, docid_vec[...], far_vec[...])
    docid_out[...] = docid_in[...] + docid_grad
    far_out[...] = far_in[...] + far_grad
    head_out[...] = head_in[...] + head


def last_kernel(starts, part, head_query, docid_vec, docid_in, head_in, far_vec, far_in,
                docids, docid_unit, docid_scale, far, far_unit, far_scale,
                docid_out, far_sent, kept, sent):
    docid_grad, far_grad, query = pair(starts, part, head_query, docid_vec[...], far_vec[...])
    docid_grad = docid_grad + docid_in[...]
    far_grad = far_grad + far_in[...]
    query = query + head_in[...]
    docid_out[...] = docid_grad
    far_sent[...] = far_grad.astype(BF16)
    head = dot(docids[...], direction(docid_grad, docid_unit[...], docid_scale[...]), COLUMNS)
    head = head + dot(far[...], direction(far_grad, far_unit[...], far_scale[...]), COLUMNS)
    mine = jnp.zeros(head.shape, jnp.int32) + starts[2] == 0
    kept[...] = jnp.where(mine, query, head)
    sent[...] = jnp.where(mine, head, query).astype(BF16)


def update_kernel(docid_grad, back, docid_unit, docid_scale, head_docid, update):
    grad = docid_grad[...] + back[...].astype(F32)
    direct = direction(grad, docid_unit[...], docid_scale[...])
    grad = dot(direct, head_docid[...], ROWS)
    scale = lax.rsqrt(jnp.mean(grad * grad, axis=-1, keepdims=True) + EPSILON)
    update[...] = (grad * scale).astype(BF16)


def rms_scale(grad):
    grad = grad.astype(F32)
    return lax.rsqrt(jnp.sum(grad * grad) / (grad.shape[0] * grad.shape[1]) + EPSILON)


def write(head, target, staged, sems):
    depth, block = staged.shape[0], staged.shape[1]
    scale = rms_scale(head[...])
    copies = []
    for step in range(depth):
        rows = slice(step * block, (step + 1) * block)
        staged[step] = head[rows, :].astype(F32) * scale
        copies.append(pltpu.make_async_copy(staged.at[step], target.at[rows], sems.at[step]))
        copies[-1].start()
    for copy in copies:
        copy.wait()


def mine_kernel(starts, mine, query_step, docid_step, staged, sems):
    @pl.when(starts[2] == 0)
    def _():
        write(mine, query_step, staged, sems)

    @pl.when(starts[2] != 0)
    def _():
        write(mine, docid_step, staged, sems)


def other_kernel(starts, other, query_in, docid_in, query_step, docid_step, staged, sems):
    del query_in, docid_in

    @pl.when(starts[2] == 0)
    def _():
        write(other, docid_step, staged, sems)

    @pl.when(starts[2] != 0)
    def _():
        write(other, query_step, staged, sems)


def steps(starts, mine, other):
    rows, width = mine.shape
    depth = 3
    outside = pl.BlockSpec(memory_space=pltpu.HBM)
    common = dict(
        out_shape=[jax.ShapeDtypeStruct((rows, width), F32)] * 2,
        out_specs=[outside] * 2,
        scratch_shapes=[VMEM((depth, rows // depth, width), F32), pltpu.SemaphoreType.DMA((depth,))],
        compiler_params=pltpu.CompilerParams(vmem_limit_bytes=24 * 2**20),
    )
    given = [pl.BlockSpec(memory_space=SMEM), pl.BlockSpec(memory_space=VMEM)]
    written = pl.pallas_call(mine_kernel, in_specs=given, **common)(starts, mine)
    return pl.pallas_call(
        other_kernel, in_specs=given + [outside] * 2, input_output_aliases={2: 0, 3: 1}, **common
    )(starts, other, *written)


def call(kernel, outs, *args, flops=0, scalars=True):
    specs = [pl.BlockSpec(memory_space=VMEM) for _ in args]
    if scalars:
        specs[0] = pl.BlockSpec(memory_space=SMEM)
    moved_bytes = sum(a.size * a.dtype.itemsize for a in args)
    moved_bytes += sum(o.size * o.dtype.itemsize for o in outs)
    return pl.pallas_call(
        kernel,
        out_shape=outs,
        in_specs=specs,
        out_specs=[pl.BlockSpec(memory_space=VMEM) for _ in outs],
        compiler_params=pltpu.CompilerParams(vmem_limit_bytes=20 * 2**20),
        cost_estimate=pl.CostEstimate(flops=flops, transcendentals=0, bytes_accessed=moved_bytes),
    )(*args)


def total(kept, sent, update):
    rows, width = kept.shape
    value = kept + moved(sent, 1, 0).astype(F32)
    plane, line = SIZES[0] * SIZES[2] * SIZES[4], SIZES[3]
    for axes, size in ((PLANE[:2], SIZES[0] * SIZES[4]), (PLANE[2], SIZES[2])):
        piece = value.astype(BF16).reshape(size, -1, width)
        piece = lax.all_to_all(piece, axes, 0, 0, tiled=True)
        value = jnp.sum(piece.astype(F32), axis=0)
    piece = value.astype(BF16)
    piece, update = lax.optimization_barrier((piece, update))
    piece = piece.reshape(line, -1, 128)
    piece = lax.all_to_all(piece, "z", 0, 0, tiled=True)
    piece = jnp.sum(piece.astype(F32), axis=0).astype(BF16)
    piece = jnp.broadcast_to(piece[None], (line,) + piece.shape)
    piece = lax.all_to_all(piece, "z", 0, 0, tiled=True).reshape(rows // plane, width)
    piece = jnp.broadcast_to(piece[None], (plane,) + piece.shape)
    mine = lax.all_to_all(piece, PLANE, 0, 0, tiled=True).reshape(rows, width)
    return mine, moved(mine, 1, 0), update


def per_device(queries, docids, labels, head_query, head_docid):
    rows, width = queries.shape
    side = head_query.shape[1]
    core = lax.axis_index("core")
    group = lax.axis_index("y_lo") * 2 + core
    dev = (lax.axis_index("x") * 8 + lax.axis_index("z")) * 2 + lax.axis_index("y_hi")
    own_start = (group * DEVS + dev) * rows
    far_start = (group * DEVS + (dev - 2) % DEVS) * rows
    starts = jnp.stack([own_start, far_start, core]).astype(jnp.int32)

    far = moved(docids, 0, 2)
    cut = 384
    row = labels[None]
    whole = pack(row, queries, 0, rows)
    queries_2 = moved(whole, 2, -2)
    rest, whole = lax.optimization_barrier((queries, whole))
    part_a = pack(row, rest, 0, cut)
    queries_1a = moved(part_a, 1, -1)
    rest, part_a = lax.optimization_barrier((rest, part_a))
    queries_1b = moved(pack(row, rest, cut, rows - cut), 1, -1)

    def out(shape, dtype=F32):
        return jax.ShapeDtypeStruct(shape, dtype)

    block, column, head = (rows, side), (rows, 1), (width, side)
    mul = 2 * rows * width * side
    pair_flops = 2 * rows * rows * side
    docid_vec, docid_unit, docid_scale, docid_grad, query_head = call(
        own_kernel,
        [out(block, BF16), out(block), out(column), out(block), out(head)],
        starts, row, queries, docids, head_query, head_docid,
        flops=3 * mul + 3 * pair_flops,
    )
    docid_grad, far_grad, query_head, far_vec, far_unit, far_scale = call(
        first_kernel,
        [out(block), out(block), out(head), out(block, BF16), out(block), out(column)],
        starts, queries_2, head_query, docid_vec, docid_grad, query_head, far, head_docid,
        flops=3 * mul + 6 * pair_flops,
    )
    queries_1a, far_grad = lax.optimization_barrier((queries_1a, far_grad))
    docid_grad, far_grad, query_head = call(
        next_kernel,
        [out(block), out(block), out(head)],
        starts, queries_1a, head_query, docid_vec, docid_grad, query_head, far_vec, far_grad,
        flops=mul + 4 * pair_flops,
    )
    queries_1b, far_grad = lax.optimization_barrier((queries_1b, far_grad))
    docid_grad, far_sent, kept, sent = call(
        last_kernel,
        [out(block), out(block, BF16), out(head), out(head, BF16)],
        starts, queries_1b, head_query, docid_vec, docid_grad, query_head, far_vec, far_grad,
        docids, docid_unit, docid_scale, far, far_unit, far_scale,
        flops=3 * mul + 4 * pair_flops,
    )
    back = moved(far_sent, 0, -2)
    (doc_update,) = call(
        update_kernel,
        [out((rows, width), BF16)],
        docid_grad, back, docid_unit, docid_scale, head_docid,
        flops=40 * mul, scalars=False,
    )
    mine, other, doc_update = total(kept, sent, doc_update)
    query_step, docid_step = steps(starts, mine, other)
    return (doc_update, query_step, docid_step)


def solution(mesh):
    split = Mesh(mesh.devices.reshape(SIZES), AXES)
    rows = P(AXES)
    return jax.shard_map(
        per_device,
        mesh=split,
        in_specs=(rows, rows, rows, P(), P()),
        out_specs=(rows, P(), P()),
        check_vma=False,
    )
```

time: 168 us -> 156 us (0.929)
  waiting for transfers between devices: 34.1 us -> 7.18 us
  blocking collectives: 50.4 us -> 58.1 us
  Pallas kernels: 37.4 us -> 41.4 us
  local copies, waits for them, and re-layouts: 5.79 us -> 7.85 us
    all_to_all x0 -> x2, blocking collectives: none -> 29 us  [the longest x1 19.2 us: total(): piece = lax.all_to_all(piece, axes, 0, 0, tiled=True)]
    all_to_all x1, blocking collectives: 28.6 us -> 9.78 us  [total(): piece = lax.all_to_all(piece, 'z', 0, 0, tiled=True)]
    ppermute x8 -> x7, waiting for transfers between devices: 22.5 us -> 7.18 us  [moved(): return lax.ppermute(block, AXES, pairs)]
    all_to_all x1, waiting for transfers between devices: 11.6 us -> 0.01 us  [total(): piece = lax.all_to_all(piece, axes, 0, 0, tiled=True)]
    pallas_call x0 -> x2, Pallas kernels: none -> 5.59 us  [the longest x1 2.8 us: steps(): pl.pallas_call(other_kernel, in_specs=given + [outside] * 2, input_output...]
    reduce_sum x2 -> x1, other arithmetic: 2.58 us -> 0.02 us  [total(): piece = jnp.sum(piece.astype(F32), axis=0).astype(BF16)]
    all_to_all x1, blocking collectives: 21.9 us -> 19.4 us  [total(): mine = lax.all_to_all(piece, PLANE, 0, 0, tiled=True).reshape(rows, width)]
    reduce_sum x0 -> x2, other arithmetic: none -> 2.27 us  [total(): value = jnp.sum(piece.astype(F32), axis=0)]
  transfers between devices with their start and end apart: 9 -> 8, of which waited for: 5 -> 2; matrix products, arithmetic and copies ran while one was open for 1% -> 2% of each run, Pallas kernels for 13% -> 20%
where the time goes in v3:
time: 156 us; the launch traced here: 155 us
  blocking collectives  58.1 us (37%)
  Pallas kernels  41.4 us (27%)
  starting transfers between devices  36.4 us (23%)
  local copies, waits for them, and re-layouts  7.85 us (5%)
  waiting for transfers between devices  7.18 us (5%)
  other arithmetic  2.76 us (2%)
    pallas_call x8, Pallas kernels, call(): pl.pallas_call(kernel, out_shape=outs, in_specs=specs, out_specs=[pl.Bloc...  35.8 us
    ppermute x7, starting transfers between devices, moved(): return lax.ppermute(block, AXES, pairs)  32.7 us
    all_to_all x1, blocking collectives, total(): mine = lax.all_to_all(piece, PLANE, 0, 0, tiled=True).reshape(rows, width)  19.4 us
    all_to_all x1, blocking collectives, total(): piece = lax.all_to_all(piece, axes, 0, 0, tiled=True)  19.2 us
    all_to_all x1, blocking collectives, total(): piece = lax.all_to_all(piece, 'z', 0, 0, tiled=True)  9.78 us
    all_to_all x1, blocking collectives, total(): lax.all_to_all(piece, 'z', 0, 0, tiled=True).reshape(rows // plane, width)  9.78 us
    ppermute x7, waiting for transfers between devices, moved(): return lax.ppermute(block, AXES, pairs)  7.18 us
    unnamed x26, local copies, waits for them, and re-layouts  6.87 us
  transfers between devices with their start and end apart: 8, of which 2 were waited for; matrix products, arithmetic and copies ran while one was open for 2% of the time, Pallas kernels for 20%

profile of v3, /device:TPU:1, one launch (start us, length us, event | category | flops | bytes accessed | tf_op | source)
XLA Modules:
  0.0 154.8 jit_solution(4440074993720298158)
XLA Ops:
  0.6 0.7 broadcast_in_dim.16.labels
  1.3 0.0 copy-start
  1.3 1.2 copy-done
  2.5 0.1 shard_map.76
  2.6 0.0 copy-start.1
  2.6 9.7 %collective-permute-start.2 = (bf16[656,768]{1,0:T(8,128)(2,1)S(1)}, bf16[656,768]{1,0:T(8,128)(2,1)}, u32[]{:S(2)}, u32[]{:S(2)}) collective-permute-start(bf16[656,768]{1,0:T(8,128)(2,1)S(1)} %shard_map.76), channel_id=1, source_target_pairs={{0,190},{1,191},{2,128},{3,129},{4,130},{5,131},{6,132},{7,133},{8... | collective-permute-start | bytes 3022856 | tf_op jit(solution)/shard_map/ppermute | solution.py:28
  12.3 0.0 collective-permute-start.3
  12.4 8.3 %collective-permute-start.1 = (bf16[400,768]{1,0:T(8,128)(2,1)S(1)}, bf16[400,768]{1,0:T(8,128)(2,1)}, u32[]{:S(2)}, u32[]{:S(2)}) collective-permute-start(bf16[400,768]{1,0:T(8,128)(2,1)S(1)} %shard_map.77), channel_id=1, source_target_pairs={{0,127},{1,64},{2,65},{3,66},{4,67},{5,68},{6,69},{7,70},{8,71},{9... | collective-permute-start | bytes 1843208 | tf_op jit(solution)/shard_map/ppermute | solution.py:28
  20.7 0.3 collective-permute-start
  21.0 0.1 pad_add_fusion.starts
  21.1 0.0 copy-done.1
  21.1 0.0 copy-start.2
  21.1 1.3 copy-done.2
  22.4 0.0 copy-start.4
  22.4 1.3 copy-done.4
  23.6 0.0 copy-start.3
  23.6 0.0 copy-start.5
  23.6 7.5 %shard_map.79 = (bf16[640,768]{1,0:T(8,128)(2,1)S(1)}, f32[640,768]{1,0:T(8,128)S(1)}, f32[640,1]{1,0:T(8,128)S(1)}, f32[640,768]{1,0:T(8,128)S(1)}, f32[768,768]{1,0:T(8,128)S(1)}) custom-call(s32[3]{0:T(128)S(1)} %pad_add_fusion.starts, s32[1,640]{1,0:T(1,128)S(1)} %broadcast_in_dim.16.labels, bf16[640,768]{1,0:T(8,128)(2,1)S(1)} %copy-done.1, ...), custom_call_target="tpu_custom_call" | custom-call | flops 4152360960 | bytes 11605004 | tf_op jit(solution)/shard_map/pallas_call | solution.py:218
  31.1 0.0 copy-start.7
  31.1 0.0 copy-start.11
  31.1 7.1 %collective-permute-done.3.far = bf16[640,768]{1,0:T(8,128)(2,1)} collective-permute-done((bf16[640,768]{1,0:T(8,128)(2,1)}, bf16[640,768]{1,0:T(8,128)(2,1)}, u32[]{:S(2)}, u32[]{:S(2)}) %collective-permute-start.3) | collective-permute-done | bytes 983072 | tf_op jit(solution)/shard_map/ppermute | solution.py:28
  38.2 0.0 collective-permute-done.2.part
  38.2 0.0 copy-done.3
  38.2 0.0 copy-done.5
  38.3 10.3 %shard_map.80 = (f32[640,768]{1,0:T(8,128)S(1)}, f32[640,768]{1,0:T(8,128)S(1)}, f32[768,768]{1,0:T(8,128)S(1)}, bf16[640,768]{1,0:T(8,128)(2,1)S(1)}, f32[640,768]{1,0:T(8,128)S(1)}, /*index=5*/f32[640,1]{1,0:T(8,128)S(1)}) custom-call(s32[3]{0:T(128)S(1)} %pad_add_fusion.starts, bf16[656,768]{1,0:T(8,128)(2,1)} %collective-permute-done.2.part, ...), custom_call_target="tpu_custom_call" | custom-call | flops 6039797760 | bytes 18901516 | tf_op jit(solution)/shard_map/pallas_call | solution.py:218
  48.6 0.0 collective-permute-done.1.part
  48.6 6.7 %shard_map.81 = (f32[640,768]{1,0:T(8,128)S(1)}, f32[640,768]{1,0:T(8,128)S(1)}, f32[768,768]{1,0:T(8,128)S(1)}) custom-call(s32[3]{0:T(128)S(1)} %pad_add_fusion.starts, bf16[400,768]{1,0:T(8,128)(2,1)} %collective-permute-done.1.part, bf16[768,768]{1,0:T(8,128)(2,1)S(1)} %copy-done.3, bf16[640,768]{1,0:T(8,128)(2,1)S(1)} %get-tuple-element.35.docid_vec, ...), custom_call_target="tpu_custom_call" | custom-call | flops 3271557120 | bytes 16343052 | tf_op jit(solution)/shard_map/pallas_call | solution.py:218
  55.3 0.1 collective-permute-done.part
  55.4 0.0 copy-done.7
  55.4 0.0 copy-done.11
  55.4 7.5 %shard_map.82 = (f32[640,768]{1,0:T(8,128)S(1)}, bf16[640,768]{1,0:T(8,128)(2,1)S(1)}, f32[768,768]{1,0:T(8,128)S(1)}, bf16[768,768]{1,0:T(8,128)(2,1)S(1)}) custom-call(s32[3]{0:T(128)S(1)} %pad_add_fusion.starts, bf16[272,768]{1,0:T(8,128)(2,1)S(1)} %collective-permute-done.part, bf16[768,768]{1,0:T(8,128)(2,1)S(1)} %copy-done.3, ...), custom_call_target="tpu_custom_call" | custom-call | flops 4781506560 | bytes 22246412 | tf_op jit(solution)/shard_map/pallas_call | solution.py:218
  62.9 0.0 copy-start.9
  62.9 1.9 %collective-permute-start.4 = (bf16[768,768]{1,0:T(8,128)(2,1)S(1)}, bf16[768,768]{1,0:T(8,128)(2,1)S(1)}, u32[]{:S(2)}, u32[]{:S(2)}) collective-permute-start(bf16[768,768]{1,0:T(8,128)(2,1)S(1)} %get-tuple-element.54), channel_id=1, source_target_pairs={{0,64},{1,65},{2,66},{3,67},{4,68},{5,69},{6,70},{7,71},{8,72},{9,... | collective-permute-start | bytes 3538952 | tf_op jit(solution)/shard_map/ppermute | solution.py:28
  64.8 7.6 %collective-permute-start.5 = (bf16[640,768]{1,0:T(8,128)(2,1)S(1)}, bf16[640,768]{1,0:T(8,128)(2,1)}, u32[]{:S(2)}, u32[]{:S(2)}) collective-permute-start(bf16[640,768]{1,0:T(8,128)(2,1)S(1)} %get-tuple-element.56), channel_id=1, source_target_pairs={{0,62},{1,63},{2,0},{3,1},{4,2},{5,3},{6,4},{7,5},{8,6},{9,7},{10,... | collective-permute-start | bytes 2949128 | tf_op jit(solution)/shard_map/ppermute | solution.py:28
  72.4 0.0 collective-permute-done.4
  72.4 0.4 add_convert_fusion
  72.8 0.0 copy-done.9
  72.8 0.0 copy-start.6
  72.8 0.0 copy-start.12
  72.8 19.2 %all_to_all.25 = bf16[4,192,768]{2,1,0:T(8,128)(2,1)} all-to-all(bf16[4,192,768]{2,1,0:T(8,128)(2,1)S(1)} %bitcast.8), channel_id=1, replica_groups=mesh['y_lo'=2,'core'=2,'x'=4,'z'=8,'y_hi'=2] {'y_lo','y_hi'}, dimensions={0} | all-to-all | bytes 2359296 | tf_op jit(solution)/shard_map/all_to_all | solution.py:234
  92.0 2.2 %reduce_sum.36 = bf16[192,768]{1,0:T(8,128)(2,1)} reduce(bf16[4,192,768]{2,1,0:T(8,128)(2,1)} %all_to_all.25, bf16[]{:T(256)} %constant.46.clone.1), dimensions={0}, to_apply=%region_0.1 | reduce | flops 442368 | bytes 1474562 | tf_op jit(solution)/shard_map/reduce_sum | solution.py:235
  94.2 3.7 %all-to-all-start.1 = ((bf16[4,48,768]{2,1,0:T(8,128)(2,1)}), bf16[4,48,768]{2,1,0:T(8,128)(2,1)S(1)}, u32[]{:S(2)}, u32[]{:S(2)}) async-start(bf16[4,48,768]{2,1,0:T(8,128)(2,1)} %bitcast.4), calls=%async_computation.1 | async-start | bytes 589824 | tf_op jit(solution)/shard_map/all_to_all | solution.py:234
  98.0 0.0 collective-permute-done.5.back
  98.0 0.0 copy-done.6
  98.0 0.0 copy-done.12
  98.0 0.0 copy-start.8
  98.0 1.5 copy-done.8
  99.5 0.0 copy-start.10
  99.5 1.5 copy-done.10
  101.1 3.6 %shard_map.83 = bf16[640,768]{1,0:T(8,128)(2,1)} custom-call(f32[640,768]{1,0:T(8,128)S(1)} %copy-done.10, bf16[640,768]{1,0:T(8,128)(2,1)} %collective-permute-done.5.back, f32[640,768]{1,0:T(8,128)S(1)} %copy-done.8, f32[640,1]{1,0:T(8,128)S(1)} %copy-done.12, bf16[768,768]{1,0:T(8,128)(2,1)S(1)} %copy-done.6), custom_call_target="tpu_custom_call" | custom-call | flops 30198988800 | bytes 7080448 | tf_op jit(solution)/shard_map/pallas_call | solution.py:218
  104.7 0.0 all-to-all-done.1
  104.8 0.1 reshape.22
  104.9 9.8 %all_to_all.26 = bf16[8,36,128]{2,1,0:T(8,128)(2,1)S(1)} all-to-all(bf16[8,36,128]{2,1,0:T(8,128)(2,1)S(1)} %reshape.22), channel_id=1, replica_groups=mesh['y_lo'=2,'core'=2,'x'=4,'z'=8,'y_hi'=2] {'z'}, dimensions={0} | all-to-all | bytes 147456 | tf_op jit(solution)/shard_map/all_to_all | solution.py:239
  114.7 9.8 %all_to_all.27 = bf16[8,36,128]{2,1,0:T(8,128)(2,1)S(1)} all-to-all(bf16[8,36,128]{2,1,0:T(8,128)(2,1)S(1)} %broadcast_in_dim.17), channel_id=1, replica_groups=mesh['y_lo'=2,'core'=2,'x'=4,'z'=8,'y_hi'=2] {'z'}, dimensions={0} | all-to-all | bytes 147456 | tf_op jit(solution)/shard_map/all_to_all | solution.py:242
  124.5 0.1 broadcast_in_dim.18
  124.6 0.1 broadcast_in_dim.19
  124.7 19.4 %all_to_all.28 = bf16[16,48,768]{2,1,0:T(8,128)(2,1)S(1)} all-to-all(bf16[16,48,768]{2,1,0:T(8,128)(2,1)S(1)} %broadcast_in_dim.19), channel_id=1, replica_groups=mesh['y_lo'=2,'core'=2,'x'=4,'z'=8,'y_hi'=2] {'y_lo','y_hi','x'}, dimensions={0} | all-to-all | bytes 2359296 | tf_op jit(solution)/shard_map/all_to_all | solution.py:244
  144.1 4.9 %collective-permute-start.6 = (bf16[768,768]{1,0:T(8,128)(2,1)S(1)}, bf16[768,768]{1,0:T(8,128)(2,1)S(1)}, u32[]{:S(2)}, u32[]{:S(2)}) collective-permute-start(bf16[768,768]{1,0:T(8,128)(2,1)S(1)} %bitcast.6), channel_id=1, source_target_pairs={{0,64},{1,65},{2,66},{3,67},{4,68},{5,69},{6,70},{7,71},{8,72},{9,... | collective-permute-start | bytes 3538952 | tf_op jit(solution)/shard_map/ppermute | solution.py:28
  149.0 2.8 %shard_map.84 = (f32[768,768]{1,0:T(8,128)}, f32[768,768]{1,0:T(8,128)}) custom-call(s32[3]{0:T(128)S(1)} %pad_add_fusion.starts, bf16[768,768]{1,0:T(8,128)(2,1)S(1)} %bitcast.7), custom_call_target="tpu_custom_call" | custom-call | tf_op jit(solution)/shard_map/pallas_call | solution.py:206
  151.8 0.0 collective-permute-done.6.other
  151.8 2.8 %shard_map.85 = (f32[768,768]{1,0:T(8,128)}, f32[768,768]{1,0:T(8,128)}) custom-call(s32[3]{0:T(128)S(1)} %pad_add_fusion.starts, bf16[768,768]{1,0:T(8,128)(2,1)S(1)} %collective-permute-done.6.other, f32[768,768]{1,0:T(8,128)} %get-tuple-element.59.query_in, f32[768,768]{1,0:T(8,128)} %get-tuple-element.60.docid_in), custom_call_target="tpu_custom_call", output_to_operand_aliasing={{0}: (2, {}), {1}: (3, {})} | custom-call | tf_op jit(solution)/shard_map/pallas_call | solution.py:207
  (5 shorter events, 0.2 us)
Async XLA Ops:
  1.3 1.2 copy-start
  2.6 18.5 %copy-start.1 = (bf16[640,768]{1,0:T(8,128)(2,1)S(1)}, bf16[640,768]{1,0:T(8,128)(2,1)}, u32[]{:S(2)}) copy-start(bf16[640,768]{1,0:T(8,128)(2,1)} %queries.5) | copy-start | bytes 2949124
  2.6 35.6 %collective-permute-start.2 = (bf16[656,768]{1,0:T(8,128)(2,1)S(1)}, bf16[656,768]{1,0:T(8,128)(2,1)}, u32[]{:S(2)}, u32[]{:S(2)}) collective-permute-start(bf16[656,768]{1,0:T(8,128)(2,1)S(1)} %shard_map.76), channel_id=1, source_target_pairs={{0,190},{1,191},{2,128},{3,129},{4,130},{5,131},{6,132},{7,133},{8... | collective-permute-start | bytes 3022856 | tf_op jit(solution)/shard_map/ppermute | solution.py:28
  12.3 25.9 %collective-permute-start.3 = (bf16[640,768]{1,0:T(8,128)(2,1)}, bf16[640,768]{1,0:T(8,128)(2,1)}, u32[]{:S(2)}, u32[]{:S(2)}) collective-permute-start(bf16[640,768]{1,0:T(8,128)(2,1)} %docids.3), channel_id=1, source_target_pairs={{0,2},{1,3},{2,4},{3,5},{4,6},{5,7},{6,8},{7,9},{8,10},{9,11},{10,... | collective-permute-start | bytes 2949128 | tf_op jit(solution)/shard_map/ppermute | solution.py:28
  12.4 36.2 %collective-permute-start.1 = (bf16[400,768]{1,0:T(8,128)(2,1)S(1)}, bf16[400,768]{1,0:T(8,128)(2,1)}, u32[]{:S(2)}, u32[]{:S(2)}) collective-permute-start(bf16[400,768]{1,0:T(8,128)(2,1)S(1)} %shard_map.77), channel_id=1, source_target_pairs={{0,127},{1,64},{2,65},{3,66},{4,67},{5,68},{6,69},{7,70},{8,71},{9... | collective-permute-start | bytes 1843208 | tf_op jit(solution)/shard_map/ppermute | solution.py:28
  20.7 34.7 %collective-permute-start = (bf16[272,768]{1,0:T(8,128)(2,1)S(1)}, bf16[272,768]{1,0:T(8,128)(2,1)S(1)}, u32[]{:S(2)}, u32[]{:S(2)}) collective-permute-start(bf16[272,768]{1,0:T(8,128)(2,1)S(1)} %shard_map.78), channel_id=1, source_target_pairs={{0,127},{1,64},{2,65},{3,66},{4,67},{5,68},{6,69},{7,70},{8,71},{9... | collective-permute-start | bytes 1253384 | tf_op jit(solution)/shard_map/ppermute | solution.py:28
  21.1 1.3 copy-start.2
  22.4 1.3 copy-start.4
  23.6 14.6 %copy-start.3 = (bf16[768,768]{1,0:T(8,128)(2,1)S(1)}, bf16[768,768]{1,0:T(8,128)(2,1)}, u32[]{:S(2)}) copy-start(bf16[768,768]{1,0:T(8,128)(2,1)} %head_query.7) | copy-start | bytes 3538948
  23.6 14.6 %copy-start.5 = (bf16[768,768]{1,0:T(8,128)(2,1)S(1)}, bf16[768,768]{1,0:T(8,128)(2,1)}, u32[]{:S(2)}) copy-start(bf16[768,768]{1,0:T(8,128)(2,1)} %head_docid.5) | copy-start | bytes 3538948
  31.1 24.3 %copy-start.7 = (f32[640,768]{1,0:T(8,128)}, f32[640,768]{1,0:T(8,128)S(1)}, u32[]{:S(2)}) copy-start(f32[640,768]{1,0:T(8,128)S(1)} %get-tuple-element.49.docid_unit) | copy-start | bytes 5898244
  31.1 24.2 %copy-start.11 = (f32[640,1]{1,0:T(8,128)}, f32[640,1]{1,0:T(8,128)S(1)}, u32[]{:S(2)}) copy-start(f32[640,1]{1,0:T(8,128)S(1)} %get-tuple-element.50.docid_scale) | copy-start | bytes 7684
  62.9 9.9 %copy-start.9 = (f32[640,768]{1,0:T(8,128)}, f32[640,768]{1,0:T(8,128)S(1)}, u32[]{:S(2)}) copy-start(f32[640,768]{1,0:T(8,128)S(1)} %get-tuple-element.55.docid_grad) | copy-start | bytes 5898244
  62.9 9.5 %collective-permute-start.4 = (bf16[768,768]{1,0:T(8,128)(2,1)S(1)}, bf16[768,768]{1,0:T(8,128)(2,1)S(1)}, u32[]{:S(2)}, u32[]{:S(2)}) collective-permute-start(bf16[768,768]{1,0:T(8,128)(2,1)S(1)} %get-tuple-element.54), channel_id=1, source_target_pairs={{0,64},{1,65},{2,66},{3,67},{4,68},{5,69},{6,70},{7,71},{8,72},{9,... | collective-permute-start | bytes 3538952 | tf_op jit(solution)/shard_map/ppermute | solution.py:28
  64.8 33.1 %collective-permute-start.5 = (bf16[640,768]{1,0:T(8,128)(2,1)S(1)}, bf16[640,768]{1,0:T(8,128)(2,1)}, u32[]{:S(2)}, u32[]{:S(2)}) collective-permute-start(bf16[640,768]{1,0:T(8,128)(2,1)S(1)} %get-tuple-element.56), channel_id=1, source_target_pairs={{0,62},{1,63},{2,0},{3,1},{4,2},{5,3},{6,4},{7,5},{8,6},{9,7},{10,... | collective-permute-start | bytes 2949128 | tf_op jit(solution)/shard_map/ppermute | solution.py:28
  72.8 25.2 %copy-start.6 = (bf16[768,768]{1,0:T(8,128)(2,1)S(1)}, bf16[768,768]{1,0:T(8,128)(2,1)}, u32[]{:S(2)}) copy-start(bf16[768,768]{1,0:T(8,128)(2,1)} %head_docid.5) | copy-start | bytes 3538948
  72.8 25.2 %copy-start.12 = (f32[640,1]{1,0:T(8,128)S(1)}, f32[640,1]{1,0:T(8,128)}, u32[]{:S(2)}) copy-start(f32[640,1]{1,0:T(8,128)} %copy-done.11) | copy-start | bytes 7684
  94.2 10.5 %all-to-all-start.1 = ((bf16[4,48,768]{2,1,0:T(8,128)(2,1)}), bf16[4,48,768]{2,1,0:T(8,128)(2,1)S(1)}, u32[]{:S(2)}, u32[]{:S(2)}) async-start(bf16[4,48,768]{2,1,0:T(8,128)(2,1)} %bitcast.4), calls=%async_computation.1 | async-start | bytes 589824 | tf_op jit(solution)/shard_map/all_to_all | solution.py:234
  98.0 1.5 %copy-start.8 = (f32[640,768]{1,0:T(8,128)S(1)}, f32[640,768]{1,0:T(8,128)}, u32[]{:S(2)}) copy-start(f32[640,768]{1,0:T(8,128)} %copy-done.7) | copy-start | bytes 5898244
  99.5 1.5 copy-start.10
  144.1 7.7 %collective-permute-start.6 = (bf16[768,768]{1,0:T(8,128)(2,1)S(1)}, bf16[768,768]{1,0:T(8,128)(2,1)S(1)}, u32[]{:S(2)}, u32[]{:S(2)}) collective-permute-start(bf16[768,768]{1,0:T(8,128)(2,1)S(1)} %bitcast.6), channel_id=1, source_target_pairs={{0,64},{1,65},{2,66},{3,67},{4,68},{5,69},{6,70},{7,71},{8,72},{9,... | collective-permute-start | bytes 3538952 | tf_op jit(solution)/shard_map/ppermute | solution.py:28

commit v4 on v3

--- a/solution.py
+++ b/solution.py
@@ -94,8 +94,7 @@
     query_head[...] = dot(queries[...], direction(query_grad, unit, LOGIT_SCALE * inverse), COLUMNS)
 
 
-def pair(starts, part, head_query, docid_vec, far_vec):
-    queries, labels = unpacked(part)
+def pair(starts, queries, labels, head_query, docid_vec, far_vec):
     unit, inverse = project(queries, head_query[...])
     query_vec = unit.astype(BF16)
     weights = pair_weights(far_vec, query_vec, labels, starts[1])
@@ -108,21 +107,21 @@
     return docid_grad, far_grad, head
 
 
-def first_kernel(starts, part, head_query, docid_vec, docid_in, head_in, far, head_docid,
+def first_kernel(starts, queries, labels, head_query, docid_vec, docid_in, head_in, far, head_docid,
                  docid_out, far_out, head_out, far_vec, far_unit, far_scale):
     unit, inverse = project(far[...], head_docid[...])
     far_unit[...] = unit
     far_scale[...] = LOGIT_SCALE * inverse
     vec = unit.astype(BF16)
     far_vec[...] = vec
-    docid_grad, far_out[...], head = pair(starts, part, head_query, docid_vec[...], vec)
+    docid_grad, far_out[...], head = pair(starts, queries[...], labels[...], head_query, docid_vec[...], vec)
     docid_out[...] = docid_in[...] + docid_grad
     head_out[...] = head_in[...] + head
 
 
 def next_kernel(starts, part, head_query, docid_vec, docid_in, head_in, far_vec, far_in,
                 docid_out, far_out, head_out):
-    docid_grad, far_grad, head = pair(starts, part, head_query, docid_vec[...], far_vec[...])
+    docid_grad, far_grad, head = pair(starts, *unpacked(part), head_query, docid_vec[...], far_vec[...])
     docid_out[...] = docid_in[...] + docid_grad
     far_out[...] = far_in[...] + far_grad
     head_out[...] = head_in[...] + head
@@ -131,7 +130,7 @@
 def last_kernel(starts, part, head_query, docid_vec, docid_in, head_in, far_vec, far_in,
                 docids, docid_unit, docid_scale, far, far_unit, far_scale,
                 docid_out, far_sent, kept, sent):
-    docid_grad, far_grad, query = pair(starts, part, head_query, docid_vec[...], far_vec[...])
+    docid_grad, far_grad, query = pair(starts, *unpacked(part), head_query, docid_vec[...], far_vec[...])
     docid_grad = docid_grad + docid_in[...]
     far_grad = far_grad + far_in[...]
     query = query + head_in[...]
@@ -229,15 +228,13 @@
     rows, width = kept.shape
     value = kept + moved(sent, 1, 0).astype(F32)
     plane, line = SIZES[0] * SIZES[2] * SIZES[4], SIZES[3]
-    for axes, size in ((PLANE[:2], SIZES[0] * SIZES[4]), (PLANE[2], SIZES[2])):
-        piece = value.astype(BF16).reshape(size, -1, width)
-        piece = lax.all_to_all(piece, axes, 0, 0, tiled=True)
-        value = jnp.sum(piece.astype(F32), axis=0)
-    piece = value.astype(BF16)
+    piece = value.astype(BF16).reshape(SIZES[0] * SIZES[4], -1, width)
+    piece = lax.all_to_all(piece, PLANE[:2], 0, 0, tiled=True)
+    piece = jnp.sum(piece.astype(F32), axis=0).astype(BF16)
+    piece = piece.reshape(SIZES[2] * line, -1, 128)
+    piece = lax.all_to_all(piece, ("x", "z"), 0, 0, tiled=True)
+    piece = jnp.sum(piece.astype(F32), axis=0).astype(BF16)
     piece, update = lax.optimization_barrier((piece, update))
-    piece = piece.reshape(line, -1, 128)
-    piece = lax.all_to_all(piece, "z", 0, 0, tiled=True)
-    piece = jnp.sum(piece.astype(F32), axis=0).astype(BF16)
     piece = jnp.broadcast_to(piece[None], (line,) + piece.shape)
     piece = lax.all_to_all(piece, "z", 0, 0, tiled=True).reshape(rows // plane, width)
     piece = jnp.broadcast_to(piece[None], (plane,) + piece.shape)
@@ -258,12 +255,10 @@
     far = moved(docids, 0, 2)
     cut = 384
     row = labels[None]
-    whole = pack(row, queries, 0, rows)
-    queries_2 = moved(whole, 2, -2)
-    rest, whole = lax.optimization_barrier((queries, whole))
-    part_a = pack(row, rest, 0, cut)
+    queries_2, labels_2 = moved(queries, 2, -2), moved(labels, 2, -2)
+    part_a = pack(row, queries, 0, cut)
     queries_1a = moved(part_a, 1, -1)
-    rest, part_a = lax.optimization_barrier((rest, part_a))
+    rest, part_a = lax.optimization_barrier((queries, part_a))
     queries_1b = moved(pack(row, rest, cut, rows - cut), 1, -1)
 
     def out(shape, dtype=F32):
@@ -281,7 +276,7 @@
     docid_grad, far_grad, query_head, far_vec, far_unit, far_scale = call(
         first_kernel,
         [out(block), out(block), out(head), out(block, BF16), out(block), out(column)],
-        starts, queries_2, head_query, docid_vec, docid_grad, query_head, far, head_docid,
+        starts, queries_2, labels_2[None], head_query, docid_vec, docid_grad, query_head, far, head_docid,
         flops=3 * mul + 6 * pair_flops,
     )
     queries_1a, far_grad = lax.optimization_barrier((queries_1a, far_grad))

time: 156 us -> 148 us (0.949)
  blocking collectives: 58.1 us -> 49.6 us
  waiting for transfers between devices: 7.18 us -> 12.6 us
  Pallas kernels: 41.4 us -> 38.4 us
    all_to_all x2 -> x1, blocking collectives: 29 us -> 19.1 us  [total(): piece = lax.all_to_all(piece, PLANE[:2], 0, 0, tiled=True)]
    all_to_all x1, waiting for transfers between devices: 0.01 us -> 4.3 us  [total(): piece = lax.all_to_all(piece, ('x', 'z'), 0, 0, tiled=True)]
    pallas_call x8 -> x7, Pallas kernels: 35.8 us -> 32.8 us  [call(): pl.pallas_call(kernel, out_shape=outs, in_specs=specs, out_specs=[pl.Bloc...]
    all_to_all x1, blocking collectives: 9.78 us -> 12.5 us  [total(): lax.all_to_all(piece, 'z', 0, 0, tiled=True).reshape(rows // plane, width)]
    reduce_sum x2 -> x0, other arithmetic: 2.27 us -> none  [total(): value = jnp.sum(piece.astype(F32), axis=0)]
    ppermute x7 -> x8, starting transfers between devices: 32.7 us -> 30.6 us  [moved(): return lax.ppermute(block, AXES, pairs)]
    reduce_sum x1 -> x2, other arithmetic: 0.02 us -> 1.69 us  [total(): piece = jnp.sum(piece.astype(F32), axis=0).astype(BF16)]
    ppermute x7 -> x8, waiting for transfers between devices: 7.18 us -> 8.26 us  [moved(): return lax.ppermute(block, AXES, pairs)]
  transfers between devices with their start and end apart: 8 -> 9, of which waited for: 2 -> 4; matrix products, arithmetic and copies ran while one was open for 2% -> 3% of each run, Pallas kernels for 20% -> 20%
where the time goes in v4:
time: 148 us; the launch traced here: 147 us
  blocking collectives  49.6 us (34%)
  Pallas kernels  38.4 us (26%)
  starting transfers between devices  35.1 us (24%)
  waiting for transfers between devices  12.6 us (9%)
  local copies, waits for them, and re-layouts  8.72 us (6%)
  other arithmetic  2.12 us (1%)
    pallas_call x7, Pallas kernels, call(): pl.pallas_call(kernel, out_shape=outs, in_specs=specs, out_specs=[pl.Bloc...  32.8 us
    ppermute x8, starting transfers between devices, moved(): return lax.ppermute(block, AXES, pairs)  30.6 us
    all_to_all x1, blocking collectives, total(): piece = lax.all_to_all(piece, PLANE[:2], 0, 0, tiled=True)  19.1 us
    all_to_all x1, blocking collectives, total(): mine = lax.all_to_all(piece, PLANE, 0, 0, tiled=True).reshape(rows, width)  18 us
    all_to_all x1, blocking collectives, total(): lax.all_to_all(piece, 'z', 0, 0, tiled=True).reshape(rows // plane, width)  12.5 us
    ppermute x8, waiting for transfers between devices, moved(): return lax.ppermute(block, AXES, pairs)  8.26 us
    unnamed x24, local copies, waits for them, and re-layouts  6.79 us
    all_to_all x1, starting transfers between devices, total(): piece = lax.all_to_all(piece, ('x', 'z'), 0, 0, tiled=True)  4.46 us
  transfers between devices with their start and end apart: 9, of which 4 were waited for; matrix products, arithmetic and copies ran while one was open for 3% of the time, Pallas kernels for 20%

profile of v4, /device:TPU:1, one launch (start us, length us, event | category | flops | bytes accessed | tf_op | source)
XLA Modules:
  0.0 147.4 jit_solution(1993275167654037183)
XLA Ops:
  0.6 2.5 %collective-permute-start.4 = (bf16[640,768]{1,0:T(8,128)(2,1)}, bf16[640,768]{1,0:T(8,128)(2,1)}, u32[]{:S(2)}, u32[]{:S(2)}) collective-permute-start(bf16[640,768]{1,0:T(8,128)(2,1)} %docids.3), channel_id=1, source_target_pairs={{0,2},{1,3},{2,4},{3,5},{4,6},{5,7},{6,8},{7,9},{8,10},{9,11},{10,... | collective-permute-start | bytes 2949128 | tf_op jit(solution)/shard_map/ppermute | solution.py:28
  3.2 7.2 %collective-permute-start.2 = (bf16[640,768]{1,0:T(8,128)(2,1)}, bf16[640,768]{1,0:T(8,128)(2,1)}, u32[]{:S(2)}, u32[]{:S(2)}) collective-permute-start(bf16[640,768]{1,0:T(8,128)(2,1)} %queries.4), channel_id=1, source_target_pairs={{0,190},{1,191},{2,128},{3,129},{4,130},{5,131},{6,132},{7,133},{8... | collective-permute-start | bytes 2949128 | tf_op jit(solution)/shard_map/ppermute | solution.py:28
  10.4 1.3 collective-permute-start.3
  11.7 0.7 broadcast_in_dim.19.labels
  12.4 0.0 copy-start
  12.4 1.2 copy-done
  13.6 0.0 copy-start.1
  13.6 0.0 copy-start.2
  13.7 4.8 %collective-permute-start.1 = (bf16[400,768]{1,0:T(8,128)(2,1)S(1)}, bf16[400,768]{1,0:T(8,128)(2,1)}, u32[]{:S(2)}, u32[]{:S(2)}) collective-permute-start(bf16[400,768]{1,0:T(8,128)(2,1)S(1)} %shard_map.76), channel_id=1, source_target_pairs={{0,127},{1,64},{2,65},{3,66},{4,67},{5,68},{6,69},{7,70},{8,71},{9... | collective-permute-start | bytes 1843208 | tf_op jit(solution)/shard_map/ppermute | solution.py:28
  18.5 0.3 collective-permute-start
  18.8 0.1 pad_add_fusion.starts
  18.9 0.0 copy-done.1
  18.9 0.0 copy-done.2
  18.9 0.0 copy-start.3
  18.9 1.3 copy-done.3
  20.2 0.0 copy-start.6
  20.2 1.2 copy-done.6
  21.4 0.0 copy-start.4
  21.4 6.7 %shard_map.78 = (bf16[640,768]{1,0:T(8,128)(2,1)S(1)}, f32[640,768]{1,0:T(8,128)S(1)}, f32[640,1]{1,0:T(8,128)S(1)}, f32[640,768]{1,0:T(8,128)S(1)}, f32[768,768]{1,0:T(8,128)S(1)}) custom-call(s32[3]{0:T(128)S(1)} %pad_add_fusion.starts, s32[1,640]{1,0:T(1,128)S(1)} %broadcast_in_dim.19.labels, bf16[640,768]{1,0:T(8,128)(2,1)S(1)} %copy-done.1, ...), custom_call_target="tpu_custom_call" | custom-call | flops 4152360960 | bytes 11605004 | tf_op jit(solution)/shard_map/pallas_call | solution.py:217
  28.0 0.0 copy-start.8
  28.1 3.1 %collective-permute-done.3 = s32[640]{0:T(1024)S(1)} collective-permute-done((s32[640]{0:T(1024)}, s32[640]{0:T(1024)S(1)}, u32[]{:S(2)}, u32[]{:S(2)}) %collective-permute-start.3) | collective-permute-done | bytes 2592 | tf_op jit(solution)/shard_map/ppermute | solution.py:28
  31.2 0.0 collective-permute-done.4.far
  31.2 0.0 collective-permute-done.2.queries
  31.2 0.0 copy-done.4
  31.2 10.2 %shard_map.79 = (f32[640,768]{1,0:T(8,128)S(1)}, f32[640,768]{1,0:T(8,128)S(1)}, f32[768,768]{1,0:T(8,128)S(1)}, bf16[640,768]{1,0:T(8,128)(2,1)S(1)}, f32[640,768]{1,0:T(8,128)S(1)}, /*index=5*/f32[640,1]{1,0:T(8,128)S(1)}) custom-call(s32[3]{0:T(128)S(1)} %pad_add_fusion.starts, bf16[640,768]{1,0:T(8,128)(2,1)} %collective-permute-done.2.queries, ...), custom_call_target="tpu_custom_call" | custom-call | flops 6039797760 | bytes 18879500 | tf_op jit(solution)/shard_map/pallas_call | solution.py:217
  41.4 2.9 %collective-permute-done.1.part = bf16[400,768]{1,0:T(8,128)(2,1)} collective-permute-done((bf16[400,768]{1,0:T(8,128)(2,1)S(1)}, bf16[400,768]{1,0:T(8,128)(2,1)}, u32[]{:S(2)}, u32[]{:S(2)}) %collective-permute-start.1) | collective-permute-done | bytes 614432 | tf_op jit(solution)/shard_map/ppermute | solution.py:28
  44.3 0.0 copy-start.7
  44.3 6.7 %shard_map.80 = (f32[640,768]{1,0:T(8,128)S(1)}, f32[640,768]{1,0:T(8,128)S(1)}, f32[768,768]{1,0:T(8,128)S(1)}) custom-call(s32[3]{0:T(128)S(1)} %pad_add_fusion.starts, bf16[400,768]{1,0:T(8,128)(2,1)} %collective-permute-done.1.part, bf16[768,768]{1,0:T(8,128)(2,1)S(1)} %copy-done.2, bf16[640,768]{1,0:T(8,128)(2,1)S(1)} %get-tuple-element.33.docid_vec, ...), custom_call_target="tpu_custom_call" | custom-call | flops 3271557120 | bytes 16343052 | tf_op jit(solution)/shard_map/pallas_call | solution.py:217
  51.0 2.2 %collective-permute-done.part = bf16[272,768]{1,0:T(8,128)(2,1)} collective-permute-done((bf16[272,768]{1,0:T(8,128)(2,1)S(1)}, bf16[272,768]{1,0:T(8,128)(2,1)}, u32[]{:S(2)}, u32[]{:S(2)}) %collective-permute-start) | collective-permute-done | bytes 417824 | tf_op jit(solution)/shard_map/ppermute | solution.py:28
  53.3 0.0 copy-done.8
  53.3 0.0 copy-done.7
  53.3 6.8 %shard_map.81 = (f32[640,768]{1,0:T(8,128)S(1)}, bf16[640,768]{1,0:T(8,128)(2,1)}, f32[768,768]{1,0:T(8,128)S(1)}, bf16[768,768]{1,0:T(8,128)(2,1)S(1)}) custom-call(s32[3]{0:T(128)S(1)} %pad_add_fusion.starts, bf16[272,768]{1,0:T(8,128)(2,1)} %collective-permute-done.part, bf16[768,768]{1,0:T(8,128)(2,1)S(1)} %copy-done.2, ...), custom_call_target="tpu_custom_call" | custom-call | flops 4781506560 | bytes 22246412 | tf_op jit(solution)/shard_map/pallas_call | solution.py:217
  60.1 0.0 copy-start.10
  60.1 1.6 %collective-permute-start.5 = (bf16[768,768]{1,0:T(8,128)(2,1)S(1)}, bf16[768,768]{1,0:T(8,128)(2,1)S(1)}, u32[]{:S(2)}, u32[]{:S(2)}) collective-permute-start(bf16[768,768]{1,0:T(8,128)(2,1)S(1)} %get-tuple-element.52), channel_id=1, source_target_pairs={{0,64},{1,65},{2,66},{3,67},{4,68},{5,69},{6,70},{7,71},{8,72},{9,... | collective-permute-start | bytes 3538952 | tf_op jit(solution)/shard_map/ppermute | solution.py:28
  61.7 7.9 %collective-permute-start.6 = (bf16[640,768]{1,0:T(8,128)(2,1)}, bf16[640,768]{1,0:T(8,128)(2,1)S(1)}, u32[]{:S(2)}, u32[]{:S(2)}) collective-permute-start(bf16[640,768]{1,0:T(8,128)(2,1)} %get-tuple-element.54), channel_id=1, source_target_pairs={{0,62},{1,63},{2,0},{3,1},{4,2},{5,3},{6,4},{7,5},{8,6},{9,7},{10,... | collective-permute-start | bytes 2949128 | tf_op jit(solution)/shard_map/ppermute | solution.py:28
  69.6 0.0 collective-permute-done.5
  69.6 0.3 add_convert_fusion
  70.0 0.0 copy-done.10
  70.0 19.1 %all_to_all.20 = bf16[4,192,768]{2,1,0:T(8,128)(2,1)} all-to-all(bf16[4,192,768]{2,1,0:T(8,128)(2,1)S(1)} %bitcast.7), channel_id=1, replica_groups=mesh['y_lo'=2,'core'=2,'x'=4,'z'=8,'y_hi'=2] {'y_lo','y_hi'}, dimensions={0} | all-to-all | bytes 2359296 | tf_op jit(solution)/shard_map/all_to_all | solution.py:232
  89.1 0.0 copy-start.5
  89.1 1.6 %reduce_sum.24 = bf16[192,768]{1,0:T(8,128)(2,1)S(1)} reduce(bf16[4,192,768]{2,1,0:T(8,128)(2,1)} %all_to_all.20, bf16[]{:T(256)} %constant.45.clone.1), dimensions={0}, to_apply=%region_0.1 | reduce | flops 442368 | bytes 1474562 | tf_op jit(solution)/shard_map/reduce_sum | solution.py:233
  90.7 1.0 reshape.18
  91.7 4.5 %all-to-all-start.1 = ((bf16[32,36,128]{2,1,0:T(8,128)(2,1)}), bf16[32,36,128]{2,1,0:T(8,128)(2,1)S(1)}, u32[]{:S(2)}, u32[]{:S(2)}) async-start(bf16[32,36,128]{2,1,0:T(8,128)(2,1)} %reshape.18), calls=%async_computation.1 | async-start | bytes 655360 | tf_op jit(solution)/shard_map/all_to_all | solution.py:235
  96.2 0.0 collective-permute-done.6.back
  96.2 0.0 copy-done.5
  96.2 0.0 copy-start.9
  96.2 1.5 %copy-done.9 = f32[640,768]{1,0:T(8,128)S(1)} copy-done((f32[640,768]{1,0:T(8,128)S(1)}, f32[640,768]{1,0:T(8,128)}, u32[]{:S(2)}) %copy-start.9) | copy-done | bytes 1966104
  97.7 0.0 copy-start.11
  97.7 1.5 %copy-done.11 = f32[640,768]{1,0:T(8,128)S(1)} copy-done((f32[640,768]{1,0:T(8,128)S(1)}, f32[640,768]{1,0:T(8,128)}, u32[]{:S(2)}) %copy-start.11) | copy-done | bytes 1966104
  99.3 2.3 %shard_map.82 = bf16[640,768]{1,0:T(8,128)(2,1)} custom-call(f32[640,768]{1,0:T(8,128)S(1)} %copy-done.11, bf16[640,768]{1,0:T(8,128)(2,1)S(1)} %collective-permute-done.6.back, f32[640,768]{1,0:T(8,128)S(1)} %copy-done.9, f32[640,1]{1,0:T(8,128)S(1)} %get-tuple-element.48.docid_scale, bf16[768,768]{1,0:T(8,128)(2,1)S(1)} %copy-done.5), custom_call_target="tpu_custom_call" | custom-call | flops 30198988800 | bytes 7080448 | tf_op jit(solution)/shard_map/pallas_call | solution.py:217
  101.6 4.3 %all-to-all-done.1 = bf16[32,36,128]{2,1,0:T(8,128)(2,1)S(1)} async-done(((bf16[32,36,128]{2,1,0:T(8,128)(2,1)}), bf16[32,36,128]{2,1,0:T(8,128)(2,1)S(1)}, u32[]{:S(2)}, u32[]{:S(2)}) %all-to-all-start.1) | async-done | bytes 294944 | tf_op jit(solution)/shard_map/all_to_all | solution.py:235
  105.9 0.1 reduce_sum.25
  106.0 12.5 %all_to_all.21 = bf16[8,36,128]{2,1,0:T(8,128)(2,1)S(1)} all-to-all(bf16[8,36,128]{2,1,0:T(8,128)(2,1)S(1)} %broadcast_in_dim.21), channel_id=1, replica_groups=mesh['y_lo'=2,'core'=2,'x'=4,'z'=8,'y_hi'=2] {'z'}, dimensions={0} | all-to-all | bytes 147456 | tf_op jit(solution)/shard_map/all_to_all | solution.py:239
  118.6 0.1 broadcast_in_dim.22
  118.7 0.1 broadcast_in_dim.23
  118.7 18.0 %all_to_all.22 = bf16[16,48,768]{2,1,0:T(8,128)(2,1)S(1)} all-to-all(bf16[16,48,768]{2,1,0:T(8,128)(2,1)S(1)} %broadcast_in_dim.23), channel_id=1, replica_groups=mesh['y_lo'=2,'core'=2,'x'=4,'z'=8,'y_hi'=2] {'y_lo','y_hi','x'}, dimensions={0} | all-to-all | bytes 2359296 | tf_op jit(solution)/shard_map/all_to_all | solution.py:241
  136.7 4.9 %collective-permute-start.7 = (bf16[768,768]{1,0:T(8,128)(2,1)S(1)}, bf16[768,768]{1,0:T(8,128)(2,1)S(1)}, u32[]{:S(2)}, u32[]{:S(2)}) collective-permute-start(bf16[768,768]{1,0:T(8,128)(2,1)S(1)} %bitcast.5), channel_id=1, source_target_pairs={{0,64},{1,65},{2,66},{3,67},{4,68},{5,69},{6,70},{7,71},{8,72},{9,... | collective-permute-start | bytes 3538952 | tf_op jit(solution)/shard_map/ppermute | solution.py:28
  141.6 2.8 %shard_map.83 = (f32[768,768]{1,0:T(8,128)}, f32[768,768]{1,0:T(8,128)}) custom-call(s32[3]{0:T(128)S(1)} %pad_add_fusion.starts, bf16[768,768]{1,0:T(8,128)(2,1)S(1)} %bitcast.6), custom_call_target="tpu_custom_call" | custom-call | tf_op jit(solution)/shard_map/pallas_call | solution.py:205
  144.4 0.0 collective-permute-done.7.other
  144.4 2.8 %shard_map.84 = (f32[768,768]{1,0:T(8,128)}, f32[768,768]{1,0:T(8,128)}) custom-call(s32[3]{0:T(128)S(1)} %pad_add_fusion.starts, bf16[768,768]{1,0:T(8,128)(2,1)S(1)} %collective-permute-done.7.other, f32[768,768]{1,0:T(8,128)} %get-tuple-element.57.query_in, f32[768,768]{1,0:T(8,128)} %get-tuple-element.58.docid_in), custom_call_target="tpu_custom_call", output_to_operand_aliasing={{0}: (2, {}), {1}: (3, {})} | custom-call | tf_op jit(solution)/shard_map/pallas_call | solution.py:206
  (4 shorter events, 0.1 us)
Async XLA Ops:
  0.6 30.5 %collective-permute-start.4 = (bf16[640,768]{1,0:T(8,128)(2,1)}, bf16[640,768]{1,0:T(8,128)(2,1)}, u32[]{:S(2)}, u32[]{:S(2)}) collective-permute-start(bf16[640,768]{1,0:T(8,128)(2,1)} %docids.3), channel_id=1, source_target_pairs={{0,2},{1,3},{2,4},{3,5},{4,6},{5,7},{6,8},{7,9},{8,10},{9,11},{10,... | collective-permute-start | bytes 2949128 | tf_op jit(solution)/shard_map/ppermute | solution.py:28
  3.2 28.0 %collective-permute-start.2 = (bf16[640,768]{1,0:T(8,128)(2,1)}, bf16[640,768]{1,0:T(8,128)(2,1)}, u32[]{:S(2)}, u32[]{:S(2)}) collective-permute-start(bf16[640,768]{1,0:T(8,128)(2,1)} %queries.4), channel_id=1, source_target_pairs={{0,190},{1,191},{2,128},{3,129},{4,130},{5,131},{6,132},{7,133},{8... | collective-permute-start | bytes 2949128 | tf_op jit(solution)/shard_map/ppermute | solution.py:28
  10.4 20.7 %collective-permute-start.3 = (s32[640]{0:T(1024)}, s32[640]{0:T(1024)S(1)}, u32[]{:S(2)}, u32[]{:S(2)}) collective-permute-start(s32[640]{0:T(1024)} %param.7), channel_id=1, source_target_pairs={{0,190},{1,191},{2,128},{3,129},{4,130},{5,131},{6,132},{7,133},{8... | collective-permute-start | bytes 7688 | tf_op jit(solution)/shard_map/ppermute | solution.py:28
  12.4 1.2 copy-start
  13.6 5.3 %copy-start.1 = (bf16[640,768]{1,0:T(8,128)(2,1)S(1)}, bf16[640,768]{1,0:T(8,128)(2,1)}, u32[]{:S(2)}) copy-start(bf16[640,768]{1,0:T(8,128)(2,1)} %queries.4) | copy-start | bytes 2949124
  13.6 5.3 %copy-start.2 = (bf16[768,768]{1,0:T(8,128)(2,1)S(1)}, bf16[768,768]{1,0:T(8,128)(2,1)}, u32[]{:S(2)}) copy-start(bf16[768,768]{1,0:T(8,128)(2,1)} %head_query.7) | copy-start | bytes 3538948
  13.7 30.6 %collective-permute-start.1 = (bf16[400,768]{1,0:T(8,128)(2,1)S(1)}, bf16[400,768]{1,0:T(8,128)(2,1)}, u32[]{:S(2)}, u32[]{:S(2)}) collective-permute-start(bf16[400,768]{1,0:T(8,128)(2,1)S(1)} %shard_map.76), channel_id=1, source_target_pairs={{0,127},{1,64},{2,65},{3,66},{4,67},{5,68},{6,69},{7,70},{8,71},{9... | collective-permute-start | bytes 1843208 | tf_op jit(solution)/shard_map/ppermute | solution.py:28
  18.5 34.7 %collective-permute-start = (bf16[272,768]{1,0:T(8,128)(2,1)S(1)}, bf16[272,768]{1,0:T(8,128)(2,1)}, u32[]{:S(2)}, u32[]{:S(2)}) collective-permute-start(bf16[272,768]{1,0:T(8,128)(2,1)S(1)} %shard_map.77), channel_id=1, source_target_pairs={{0,127},{1,64},{2,65},{3,66},{4,67},{5,68},{6,69},{7,70},{8,71},{9... | collective-permute-start | bytes 1253384 | tf_op jit(solution)/shard_map/ppermute | solution.py:28
  18.9 1.3 copy-start.3
  20.2 1.2 copy-start.6
  21.4 9.8 %copy-start.4 = (bf16[768,768]{1,0:T(8,128)(2,1)S(1)}, bf16[768,768]{1,0:T(8,128)(2,1)}, u32[]{:S(2)}) copy-start(bf16[768,768]{1,0:T(8,128)(2,1)} %head_docid.5) | copy-start | bytes 3538948
  28.0 25.2 %copy-start.8 = (f32[640,768]{1,0:T(8,128)}, f32[640,768]{1,0:T(8,128)S(1)}, u32[]{:S(2)}) copy-start(f32[640,768]{1,0:T(8,128)S(1)} %get-tuple-element.47.docid_unit) | copy-start | bytes 5898244
  44.3 9.0 %copy-start.7 = (bf16[640,768]{1,0:T(8,128)(2,1)S(1)}, bf16[640,768]{1,0:T(8,128)(2,1)}, u32[]{:S(2)}) copy-start(bf16[640,768]{1,0:T(8,128)(2,1)} %docids.3) | copy-start | bytes 2949124
  60.1 9.9 %copy-start.10 = (f32[640,768]{1,0:T(8,128)}, f32[640,768]{1,0:T(8,128)S(1)}, u32[]{:S(2)}) copy-start(f32[640,768]{1,0:T(8,128)S(1)} %get-tuple-element.53.docid_grad) | copy-start | bytes 5898244
  60.1 9.6 %collective-permute-start.5 = (bf16[768,768]{1,0:T(8,128)(2,1)S(1)}, bf16[768,768]{1,0:T(8,128)(2,1)S(1)}, u32[]{:S(2)}, u32[]{:S(2)}) collective-permute-start(bf16[768,768]{1,0:T(8,128)(2,1)S(1)} %get-tuple-element.52), channel_id=1, source_target_pairs={{0,64},{1,65},{2,66},{3,67},{4,68},{5,69},{6,70},{7,71},{8,72},{9,... | collective-permute-start | bytes 3538952 | tf_op jit(solution)/shard_map/ppermute | solution.py:28
  61.7 34.5 %collective-permute-start.6 = (bf16[640,768]{1,0:T(8,128)(2,1)}, bf16[640,768]{1,0:T(8,128)(2,1)S(1)}, u32[]{:S(2)}, u32[]{:S(2)}) collective-permute-start(bf16[640,768]{1,0:T(8,128)(2,1)} %get-tuple-element.54), channel_id=1, source_target_pairs={{0,62},{1,63},{2,0},{3,1},{4,2},{5,3},{6,4},{7,5},{8,6},{9,7},{10,... | collective-permute-start | bytes 2949128 | tf_op jit(solution)/shard_map/ppermute | solution.py:28
  89.1 7.1 %copy-start.5 = (bf16[768,768]{1,0:T(8,128)(2,1)S(1)}, bf16[768,768]{1,0:T(8,128)(2,1)}, u32[]{:S(2)}) copy-start(bf16[768,768]{1,0:T(8,128)(2,1)} %head_docid.5) | copy-start | bytes 3538948
  91.7 14.2 %all-to-all-start.1 = ((bf16[32,36,128]{2,1,0:T(8,128)(2,1)}), bf16[32,36,128]{2,1,0:T(8,128)(2,1)S(1)}, u32[]{:S(2)}, u32[]{:S(2)}) async-start(bf16[32,36,128]{2,1,0:T(8,128)(2,1)} %reshape.18), calls=%async_computation.1 | async-start | bytes 655360 | tf_op jit(solution)/shard_map/all_to_all | solution.py:235
  96.2 1.5 %copy-start.9 = (f32[640,768]{1,0:T(8,128)S(1)}, f32[640,768]{1,0:T(8,128)}, u32[]{:S(2)}) copy-start(f32[640,768]{1,0:T(8,128)} %copy-done.8) | copy-start | bytes 5898244
  97.7 1.5 %copy-start.11 = (f32[640,768]{1,0:T(8,128)S(1)}, f32[640,768]{1,0:T(8,128)}, u32[]{:S(2)}) copy-start(f32[640,768]{1,0:T(8,128)} %copy-done.10) | copy-start | bytes 5898244
  136.7 7.7 %collective-permute-start.7 = (bf16[768,768]{1,0:T(8,128)(2,1)S(1)}, bf16[768,768]{1,0:T(8,128)(2,1)S(1)}, u32[]{:S(2)}, u32[]{:S(2)}) collective-permute-start(bf16[768,768]{1,0:T(8,128)(2,1)S(1)} %bitcast.5), channel_id=1, source_target_pairs={{0,64},{1,65},{2,66},{3,67},{4,68},{5,69},{6,70},{7,71},{8,72},{9,... | collective-permute-start | bytes 3538952 | tf_op jit(solution)/shard_map/ppermute | solution.py:28

commit v5 on v4

--- a/solution.py
+++ b/solution.py
@@ -94,27 +94,39 @@
     query_head[...] = dot(queries[...], direction(query_grad, unit, LOGIT_SCALE * inverse), COLUMNS)
 
 
-def pair(starts, queries, labels, head_query, docid_vec, far_vec):
-    unit, inverse = project(queries, head_query[...])
-    query_vec = unit.astype(BF16)
+def query_kernel(queries, head_query, query_vec, query_unit, query_scale):
+    unit, inverse = project(queries[...], head_query[...])
+    query_unit[...] = unit
+    query_scale[...] = LOGIT_SCALE * inverse
+    query_vec[...] = unit.astype(BF16)
+
+
+def scored(starts, queries, labels, query_vec, unit, scale, docid_vec, far_vec):
     weights = pair_weights(far_vec, query_vec, labels, starts[1])
     far_grad = dot(weights, query_vec, PLAIN)
     query_grad = dot(weights, far_vec, COLUMNS)
     weights = pair_weights(docid_vec, query_vec, labels, starts[0])
     docid_grad = dot(weights, query_vec, PLAIN)
     query_grad = query_grad + dot(weights, docid_vec, COLUMNS)
-    head = dot(queries, direction(query_grad, unit, LOGIT_SCALE * inverse), COLUMNS)
+    head = dot(queries, direction(query_grad, unit, scale), COLUMNS)
     return docid_grad, far_grad, head
 
 
-def first_kernel(starts, queries, labels, head_query, docid_vec, docid_in, head_in, far, head_docid,
+def pair(starts, queries, labels, head_query, docid_vec, far_vec):
+    unit, inverse = project(queries, head_query[...])
+    return scored(starts, queries, labels, unit.astype(BF16), unit, LOGIT_SCALE * inverse, docid_vec, far_vec)
+
+
+def first_kernel(starts, queries, labels, query_vec, query_unit, query_scale, docid_vec, docid_in, head_in, far, head_docid,
                  docid_out, far_out, head_out, far_vec, far_unit, far_scale):
     unit, inverse = project(far[...], head_docid[...])
     far_unit[...] = unit
     far_scale[...] = LOGIT_SCALE * inverse
     vec = unit.astype(BF16)
     far_vec[...] = vec
-    docid_grad, far_out[...], head = pair(starts, queries[...], labels[...], head_query, docid_vec[...], vec)
+    docid_grad, far_out[...], head = scored(
+        starts, queries[...], labels[...], query_vec[...], query_unit[...], query_scale[...], docid_vec[...], vec
+    )
     docid_out[...] = docid_in[...] + docid_grad
     head_out[...] = head_in[...] + head
 
@@ -273,10 +285,16 @@
         starts, row, queries, docids, head_query, head_docid,
         flops=3 * mul + 3 * pair_flops,
     )
+    query_vec, query_unit, query_scale = call(
+        query_kernel,
+        [out(block, BF16), out(block), out(column)],
+        queries_2, head_query,
+        flops=4 * mul, scalars=False,
+    )
     docid_grad, far_grad, query_head, far_vec, far_unit, far_scale = call(
         first_kernel,
         [out(block), out(block), out(head), out(block, BF16), out(block), out(column)],
-        starts, queries_2, labels_2[None], head_query, docid_vec, docid_grad, query_head, far, head_docid,
+        starts, queries_2, labels_2[None], query_vec, query_unit, query_scale, docid_vec, docid_grad, query_head, far, head_docid,
         flops=3 * mul + 6 * pair_flops,
     )
     queries_1a, far_grad = lax.optimization_barrier((queries_1a, far_grad))

time: 148 us -> 148 us (level)
  waiting for transfers between devices: 12.6 us -> 8.77 us
  starting transfers between devices: 35.1 us -> 37.2 us
  Pallas kernels: 38.4 us -> 39.9 us
    ppermute x8, waiting for transfers between devices: 8.26 us -> 4.48 us  [moved(): return lax.ppermute(block, AXES, pairs)]
    ppermute x8, starting transfers between devices: 30.6 us -> 32.8 us  [moved(): return lax.ppermute(block, AXES, pairs)]
    pallas_call x7 -> x8, Pallas kernels: 32.8 us -> 34.3 us  [call(): pl.pallas_call(kernel, out_shape=outs, in_specs=specs, out_specs=[pl.Bloc...]
  transfers between devices with their start and end apart: 9 -> 9, of which waited for: 4 -> 4; matrix products, arithmetic and copies ran while one was open for 3% -> 3% of each run, Pallas kernels for 20% -> 21%
where the time goes in v5:
time: 148 us; the launch traced here: 147 us
  blocking collectives  49.7 us (34%)
  Pallas kernels  39.9 us (27%)
  starting transfers between devices  37.2 us (25%)
  waiting for transfers between devices  8.77 us (6%)
  local copies, waits for them, and re-layouts  8.71 us (6%)
  other arithmetic  2.12 us (1%)
    pallas_call x8, Pallas kernels, call(): pl.pallas_call(kernel, out_shape=outs, in_specs=specs, out_specs=[pl.Bloc...  34.3 us
    ppermute x8, starting transfers between devices, moved(): return lax.ppermute(block, AXES, pairs)  32.8 us
    all_to_all x1, blocking collectives, total(): piece = lax.all_to_all(piece, PLANE[:2], 0, 0, tiled=True)  19.1 us
    all_to_all x1, blocking collectives, total(): mine = lax.all_to_all(piece, PLANE, 0, 0, tiled=True).reshape(rows, width)  18 us
    all_to_all x1, blocking collectives, total(): lax.all_to_all(piece, 'z', 0, 0, tiled=True).reshape(rows // plane, width)  12.5 us
    unnamed x24, local copies, waits for them, and re-layouts  6.79 us
    ppermute x8, waiting for transfers between devices, moved(): return lax.ppermute(block, AXES, pairs)  4.48 us
    all_to_all x1, starting transfers between devices, total(): piece = lax.all_to_all(piece, ('x', 'z'), 0, 0, tiled=True)  4.37 us
  transfers between devices with their start and end apart: 9, of which 4 were waited for; matrix products, arithmetic and copies ran while one was open for 3% of the time, Pallas kernels for 21%

profile of v5, /device:TPU:1, one launch (start us, length us, event | category | flops | bytes accessed | tf_op | source)
XLA Modules:
  0.0 147.4 jit_solution(12956440257542026423)
XLA Ops:
  0.6 9.7 %collective-permute-start.2 = (bf16[640,768]{1,0:T(8,128)(2,1)}, bf16[640,768]{1,0:T(8,128)(2,1)}, u32[]{:S(2)}, u32[]{:S(2)}) collective-permute-start(bf16[640,768]{1,0:T(8,128)(2,1)} %queries.4), channel_id=1, source_target_pairs={{0,190},{1,191},{2,128},{3,129},{4,130},{5,131},{6,132},{7,133},{8... | collective-permute-start | bytes 2949128 | tf_op jit(solution)/shard_map/ppermute | solution.py:28
  10.3 0.0 collective-permute-start.4
  10.3 4.7 %collective-permute-start.3 = (s32[640]{0:T(1024)}, s32[640]{0:T(1024)S(1)}, u32[]{:S(2)}, u32[]{:S(2)}) collective-permute-start(s32[640]{0:T(1024)} %param.7), channel_id=1, source_target_pairs={{0,190},{1,191},{2,128},{3,129},{4,130},{5,131},{6,132},{7,133},{8... | collective-permute-start | bytes 7688 | tf_op jit(solution)/shard_map/ppermute | solution.py:28
  15.0 0.7 broadcast_in_dim.19.labels
  15.7 0.0 copy-start
  15.7 1.2 copy-done
  16.9 0.0 copy-start.1
  16.9 0.0 copy-start.2
  17.0 3.6 %collective-permute-start.1 = (bf16[400,768]{1,0:T(8,128)(2,1)S(1)}, bf16[400,768]{1,0:T(8,128)(2,1)}, u32[]{:S(2)}, u32[]{:S(2)}) collective-permute-start(bf16[400,768]{1,0:T(8,128)(2,1)S(1)} %shard_map.76), channel_id=1, source_target_pairs={{0,127},{1,64},{2,65},{3,66},{4,67},{5,68},{6,69},{7,70},{8,71},{9... | collective-permute-start | bytes 1843208 | tf_op jit(solution)/shard_map/ppermute | solution.py:28
  20.7 0.3 collective-permute-start
  21.0 0.1 pad_add_fusion.starts
  21.0 0.0 copy-done.1
  21.0 0.0 copy-done.2
  21.0 0.0 copy-start.3
  21.0 1.3 copy-done.3
  22.3 0.0 copy-start.6
  22.3 1.2 copy-done.6
  23.5 6.7 %shard_map.79 = (bf16[640,768]{1,0:T(8,128)(2,1)S(1)}, f32[640,768]{1,0:T(8,128)S(1)}, f32[640,1]{1,0:T(8,128)S(1)}, f32[640,768]{1,0:T(8,128)S(1)}, f32[768,768]{1,0:T(8,128)S(1)}) custom-call(s32[3]{0:T(128)S(1)} %pad_add_fusion.starts, s32[1,640]{1,0:T(1,128)S(1)} %broadcast_in_dim.19.labels, bf16[640,768]{1,0:T(8,128)(2,1)S(1)} %copy-done.1, ...), custom_call_target="tpu_custom_call" | custom-call | flops 4152360960 | bytes 11605004 | tf_op jit(solution)/shard_map/pallas_call | solution.py:229
  30.2 0.0 copy-start.8
  30.2 0.9 collective-permute-done.3
  31.1 0.0 copy-start.4
  31.1 0.0 collective-permute-done.2.queries
  31.1 2.4 %shard_map.78 = (bf16[640,768]{1,0:T(8,128)(2,1)S(1)}, f32[640,768]{1,0:T(8,128)S(1)}, f32[640,1]{1,0:T(8,128)S(1)}) custom-call(bf16[640,768]{1,0:T(8,128)(2,1)} %collective-permute-done.2.queries, bf16[768,768]{1,0:T(8,128)(2,1)S(1)} %copy-done.2), custom_call_target="tpu_custom_call" | custom-call | flops 3019898880 | bytes 5114368 | tf_op jit(solution)/shard_map/pallas_call | solution.py:229
  33.5 2.8 %collective-permute-done.4.far = bf16[640,768]{1,0:T(8,128)(2,1)} collective-permute-done((bf16[640,768]{1,0:T(8,128)(2,1)}, bf16[640,768]{1,0:T(8,128)(2,1)}, u32[]{:S(2)}, u32[]{:S(2)}) %collective-permute-start.4) | collective-permute-done | bytes 983072 | tf_op jit(solution)/shard_map/ppermute | solution.py:28
  36.3 0.0 copy-done.4
  36.3 9.3 %shard_map.80 = (f32[640,768]{1,0:T(8,128)S(1)}, f32[640,768]{1,0:T(8,128)S(1)}, f32[768,768]{1,0:T(8,128)S(1)}, bf16[640,768]{1,0:T(8,128)(2,1)S(1)}, f32[640,768]{1,0:T(8,128)S(1)}, /*index=5*/f32[640,1]{1,0:T(8,128)S(1)}) custom-call(s32[3]{0:T(128)S(1)} %pad_add_fusion.starts, bf16[640,768]{1,0:T(8,128)(2,1)} %collective-permute-done.2.queries, ...), custom_call_target="tpu_custom_call" | custom-call | flops 6039797760 | bytes 20651532 | tf_op jit(solution)/shard_map/pallas_call | solution.py:229
  45.6 0.0 collective-permute-done.1.part
  45.6 0.0 copy-start.7
  45.6 6.7 %shard_map.81 = (f32[640,768]{1,0:T(8,128)S(1)}, f32[640,768]{1,0:T(8,128)S(1)}, f32[768,768]{1,0:T(8,128)S(1)}) custom-call(s32[3]{0:T(128)S(1)} %pad_add_fusion.starts, bf16[400,768]{1,0:T(8,128)(2,1)} %collective-permute-done.1.part, bf16[768,768]{1,0:T(8,128)(2,1)S(1)} %copy-done.2, bf16[640,768]{1,0:T(8,128)(2,1)S(1)} %get-tuple-element.39.docid_vec, ...), custom_call_target="tpu_custom_call" | custom-call | flops 3271557120 | bytes 16343052 | tf_op jit(solution)/shard_map/pallas_call | solution.py:229
  52.4 0.8 collective-permute-done.part
  53.2 0.0 copy-done.8
  53.2 0.0 copy-done.7
  53.2 6.8 %shard_map.82 = (f32[640,768]{1,0:T(8,128)S(1)}, bf16[640,768]{1,0:T(8,128)(2,1)}, f32[768,768]{1,0:T(8,128)S(1)}, bf16[768,768]{1,0:T(8,128)(2,1)S(1)}) custom-call(s32[3]{0:T(128)S(1)} %pad_add_fusion.starts, bf16[272,768]{1,0:T(8,128)(2,1)} %collective-permute-done.part, bf16[768,768]{1,0:T(8,128)(2,1)S(1)} %copy-done.2, ...), custom_call_target="tpu_custom_call" | custom-call | flops 4781506560 | bytes 22246412 | tf_op jit(solution)/shard_map/pallas_call | solution.py:229
  60.0 0.0 copy-start.10
  60.0 1.6 %collective-permute-start.5 = (bf16[768,768]{1,0:T(8,128)(2,1)S(1)}, bf16[768,768]{1,0:T(8,128)(2,1)S(1)}, u32[]{:S(2)}, u32[]{:S(2)}) collective-permute-start(bf16[768,768]{1,0:T(8,128)(2,1)S(1)} %get-tuple-element.58), channel_id=1, source_target_pairs={{0,64},{1,65},{2,66},{3,67},{4,68},{5,69},{6,70},{7,71},{8,72},{9,... | collective-permute-start | bytes 3538952 | tf_op jit(solution)/shard_map/ppermute | solution.py:28
  61.6 8.0 %collective-permute-start.6 = (bf16[640,768]{1,0:T(8,128)(2,1)}, bf16[640,768]{1,0:T(8,128)(2,1)S(1)}, u32[]{:S(2)}, u32[]{:S(2)}) collective-permute-start(bf16[640,768]{1,0:T(8,128)(2,1)} %get-tuple-element.60), channel_id=1, source_target_pairs={{0,62},{1,63},{2,0},{3,1},{4,2},{5,3},{6,4},{7,5},{8,6},{9,7},{10,... | collective-permute-start | bytes 2949128 | tf_op jit(solution)/shard_map/ppermute | solution.py:28
  69.6 0.0 collective-permute-done.5
  69.6 0.3 add_convert_fusion
  70.0 0.0 copy-done.10
  70.0 19.1 %all_to_all.20 = bf16[4,192,768]{2,1,0:T(8,128)(2,1)} all-to-all(bf16[4,192,768]{2,1,0:T(8,128)(2,1)S(1)} %bitcast.7), channel_id=1, replica_groups=mesh['y_lo'=2,'core'=2,'x'=4,'z'=8,'y_hi'=2] {'y_lo','y_hi'}, dimensions={0} | all-to-all | bytes 2359296 | tf_op jit(solution)/shard_map/all_to_all | solution.py:244
  89.1 0.0 copy-start.5
  89.1 1.6 %reduce_sum.24 = bf16[192,768]{1,0:T(8,128)(2,1)S(1)} reduce(bf16[4,192,768]{2,1,0:T(8,128)(2,1)} %all_to_all.20, bf16[]{:T(256)} %constant.45.clone.1), dimensions={0}, to_apply=%region_0.1 | reduce | flops 442368 | bytes 1474562 | tf_op jit(solution)/shard_map/reduce_sum | solution.py:245
  90.7 1.0 reshape.18
  91.7 4.4 %all-to-all-start.1 = ((bf16[32,36,128]{2,1,0:T(8,128)(2,1)}), bf16[32,36,128]{2,1,0:T(8,128)(2,1)S(1)}, u32[]{:S(2)}, u32[]{:S(2)}) async-start(bf16[32,36,128]{2,1,0:T(8,128)(2,1)} %reshape.18), calls=%async_computation.1 | async-start | bytes 655360 | tf_op jit(solution)/shard_map/all_to_all | solution.py:247
  96.1 0.0 collective-permute-done.6.back
  96.1 0.0 copy-done.5
  96.1 0.0 copy-start.9
  96.1 1.5 %copy-done.9 = f32[640,768]{1,0:T(8,128)S(1)} copy-done((f32[640,768]{1,0:T(8,128)S(1)}, f32[640,768]{1,0:T(8,128)}, u32[]{:S(2)}) %copy-start.9) | copy-done | bytes 1966104
  97.7 0.0 copy-start.11
  97.7 1.5 %copy-done.11 = f32[640,768]{1,0:T(8,128)S(1)} copy-done((f32[640,768]{1,0:T(8,128)S(1)}, f32[640,768]{1,0:T(8,128)}, u32[]{:S(2)}) %copy-start.11) | copy-done | bytes 1966104
  99.2 2.3 %shard_map.83 = bf16[640,768]{1,0:T(8,128)(2,1)} custom-call(f32[640,768]{1,0:T(8,128)S(1)} %copy-done.11, bf16[640,768]{1,0:T(8,128)(2,1)S(1)} %collective-permute-done.6.back, f32[640,768]{1,0:T(8,128)S(1)} %copy-done.9, f32[640,1]{1,0:T(8,128)S(1)} %get-tuple-element.54.docid_scale, bf16[768,768]{1,0:T(8,128)(2,1)S(1)} %copy-done.5), custom_call_target="tpu_custom_call" | custom-call | flops 30198988800 | bytes 7080448 | tf_op jit(solution)/shard_map/pallas_call | solution.py:229
  101.6 4.3 %all-to-all-done.1 = bf16[32,36,128]{2,1,0:T(8,128)(2,1)S(1)} async-done(((bf16[32,36,128]{2,1,0:T(8,128)(2,1)}), bf16[32,36,128]{2,1,0:T(8,128)(2,1)S(1)}, u32[]{:S(2)}, u32[]{:S(2)}) %all-to-all-start.1) | async-done | bytes 294944 | tf_op jit(solution)/shard_map/all_to_all | solution.py:247
  105.9 0.1 reduce_sum.25
  105.9 12.5 %all_to_all.21 = bf16[8,36,128]{2,1,0:T(8,128)(2,1)S(1)} all-to-all(bf16[8,36,128]{2,1,0:T(8,128)(2,1)S(1)} %broadcast_in_dim.21), channel_id=1, replica_groups=mesh['y_lo'=2,'core'=2,'x'=4,'z'=8,'y_hi'=2] {'z'}, dimensions={0} | all-to-all | bytes 147456 | tf_op jit(solution)/shard_map/all_to_all | solution.py:251
  118.5 0.1 broadcast_in_dim.22
  118.6 0.1 broadcast_in_dim.23
  118.7 18.0 %all_to_all.22 = bf16[16,48,768]{2,1,0:T(8,128)(2,1)S(1)} all-to-all(bf16[16,48,768]{2,1,0:T(8,128)(2,1)S(1)} %broadcast_in_dim.23), channel_id=1, replica_groups=mesh['y_lo'=2,'core'=2,'x'=4,'z'=8,'y_hi'=2] {'y_lo','y_hi','x'}, dimensions={0} | all-to-all | bytes 2359296 | tf_op jit(solution)/shard_map/all_to_all | solution.py:253
  136.7 4.9 %collective-permute-start.7 = (bf16[768,768]{1,0:T(8,128)(2,1)S(1)}, bf16[768,768]{1,0:T(8,128)(2,1)S(1)}, u32[]{:S(2)}, u32[]{:S(2)}) collective-permute-start(bf16[768,768]{1,0:T(8,128)(2,1)S(1)} %bitcast.5), channel_id=1, source_target_pairs={{0,64},{1,65},{2,66},{3,67},{4,68},{5,69},{6,70},{7,71},{8,72},{9,... | collective-permute-start | bytes 3538952 | tf_op jit(solution)/shard_map/ppermute | solution.py:28
  141.6 2.8 %shard_map.84 = (f32[768,768]{1,0:T(8,128)}, f32[768,768]{1,0:T(8,128)}) custom-call(s32[3]{0:T(128)S(1)} %pad_add_fusion.starts, bf16[768,768]{1,0:T(8,128)(2,1)S(1)} %bitcast.6), custom_call_target="tpu_custom_call" | custom-call | tf_op jit(solution)/shard_map/pallas_call | solution.py:217
  144.4 0.0 collective-permute-done.7.other
  144.4 2.8 %shard_map.85 = (f32[768,768]{1,0:T(8,128)}, f32[768,768]{1,0:T(8,128)}) custom-call(s32[3]{0:T(128)S(1)} %pad_add_fusion.starts, bf16[768,768]{1,0:T(8,128)(2,1)S(1)} %collective-permute-done.7.other, f32[768,768]{1,0:T(8,128)} %get-tuple-element.63.query_in, f32[768,768]{1,0:T(8,128)} %get-tuple-element.64.docid_in), custom_call_target="tpu_custom_call", output_to_operand_aliasing={{0}: (2, {}), {1}: (3, {})} | custom-call | tf_op jit(solution)/shard_map/pallas_call | solution.py:218
  (4 shorter events, 0.1 us)
Async XLA Ops:
  0.6 30.4 %collective-permute-start.2 = (bf16[640,768]{1,0:T(8,128)(2,1)}, bf16[640,768]{1,0:T(8,128)(2,1)}, u32[]{:S(2)}, u32[]{:S(2)}) collective-permute-start(bf16[640,768]{1,0:T(8,128)(2,1)} %queries.4), channel_id=1, source_target_pairs={{0,190},{1,191},{2,128},{3,129},{4,130},{5,131},{6,132},{7,133},{8... | collective-permute-start | bytes 2949128 | tf_op jit(solution)/shard_map/ppermute | solution.py:28
  10.3 25.9 %collective-permute-start.4 = (bf16[640,768]{1,0:T(8,128)(2,1)}, bf16[640,768]{1,0:T(8,128)(2,1)}, u32[]{:S(2)}, u32[]{:S(2)}) collective-permute-start(bf16[640,768]{1,0:T(8,128)(2,1)} %docids.3), channel_id=1, source_target_pairs={{0,2},{1,3},{2,4},{3,5},{4,6},{5,7},{6,8},{7,9},{8,10},{9,11},{10,... | collective-permute-start | bytes 2949128 | tf_op jit(solution)/shard_map/ppermute | solution.py:28
  10.3 20.7 %collective-permute-start.3 = (s32[640]{0:T(1024)}, s32[640]{0:T(1024)S(1)}, u32[]{:S(2)}, u32[]{:S(2)}) collective-permute-start(s32[640]{0:T(1024)} %param.7), channel_id=1, source_target_pairs={{0,190},{1,191},{2,128},{3,129},{4,130},{5,131},{6,132},{7,133},{8... | collective-permute-start | bytes 7688 | tf_op jit(solution)/shard_map/ppermute | solution.py:28
  15.7 1.2 copy-start
  16.9 4.1 %copy-start.1 = (bf16[640,768]{1,0:T(8,128)(2,1)S(1)}, bf16[640,768]{1,0:T(8,128)(2,1)}, u32[]{:S(2)}) copy-start(bf16[640,768]{1,0:T(8,128)(2,1)} %queries.4) | copy-start | bytes 2949124
  16.9 4.1 %copy-start.2 = (bf16[768,768]{1,0:T(8,128)(2,1)S(1)}, bf16[768,768]{1,0:T(8,128)(2,1)}, u32[]{:S(2)}) copy-start(bf16[768,768]{1,0:T(8,128)(2,1)} %head_query.7) | copy-start | bytes 3538948
  17.0 28.6 %collective-permute-start.1 = (bf16[400,768]{1,0:T(8,128)(2,1)S(1)}, bf16[400,768]{1,0:T(8,128)(2,1)}, u32[]{:S(2)}, u32[]{:S(2)}) collective-permute-start(bf16[400,768]{1,0:T(8,128)(2,1)S(1)} %shard_map.76), channel_id=1, source_target_pairs={{0,127},{1,64},{2,65},{3,66},{4,67},{5,68},{6,69},{7,70},{8,71},{9... | collective-permute-start | bytes 1843208 | tf_op jit(solution)/shard_map/ppermute | solution.py:28
  20.7 32.5 %collective-permute-start = (bf16[272,768]{1,0:T(8,128)(2,1)S(1)}, bf16[272,768]{1,0:T(8,128)(2,1)}, u32[]{:S(2)}, u32[]{:S(2)}) collective-permute-start(bf16[272,768]{1,0:T(8,128)(2,1)S(1)} %shard_map.77), channel_id=1, source_target_pairs={{0,127},{1,64},{2,65},{3,66},{4,67},{5,68},{6,69},{7,70},{8,71},{9... | collective-permute-start | bytes 1253384 | tf_op jit(solution)/shard_map/ppermute | solution.py:28
  21.0 1.3 copy-start.3
  22.3 1.2 copy-start.6
  30.2 23.0 %copy-start.8 = (f32[640,768]{1,0:T(8,128)}, f32[640,768]{1,0:T(8,128)S(1)}, u32[]{:S(2)}) copy-start(f32[640,768]{1,0:T(8,128)S(1)} %get-tuple-element.53.docid_unit) | copy-start | bytes 5898244
  31.1 5.2 %copy-start.4 = (bf16[768,768]{1,0:T(8,128)(2,1)S(1)}, bf16[768,768]{1,0:T(8,128)(2,1)}, u32[]{:S(2)}) copy-start(bf16[768,768]{1,0:T(8,128)(2,1)} %head_docid.5) | copy-start | bytes 3538948
  45.6 7.5 %copy-start.7 = (bf16[640,768]{1,0:T(8,128)(2,1)S(1)}, bf16[640,768]{1,0:T(8,128)(2,1)}, u32[]{:S(2)}) copy-start(bf16[640,768]{1,0:T(8,128)(2,1)} %docids.3) | copy-start | bytes 2949124
  60.0 10.0 %copy-start.10 = (f32[640,768]{1,0:T(8,128)}, f32[640,768]{1,0:T(8,128)S(1)}, u32[]{:S(2)}) copy-start(f32[640,768]{1,0:T(8,128)S(1)} %get-tuple-element.59.docid_grad) | copy-start | bytes 5898244
  60.0 9.6 %collective-permute-start.5 = (bf16[768,768]{1,0:T(8,128)(2,1)S(1)}, bf16[768,768]{1,0:T(8,128)(2,1)S(1)}, u32[]{:S(2)}, u32[]{:S(2)}) collective-permute-start(bf16[768,768]{1,0:T(8,128)(2,1)S(1)} %get-tuple-element.58), channel_id=1, source_target_pairs={{0,64},{1,65},{2,66},{3,67},{4,68},{5,69},{6,70},{7,71},{8,72},{9,... | collective-permute-start | bytes 3538952 | tf_op jit(solution)/shard_map/ppermute | solution.py:28
  61.6 34.5 %collective-permute-start.6 = (bf16[640,768]{1,0:T(8,128)(2,1)}, bf16[640,768]{1,0:T(8,128)(2,1)S(1)}, u32[]{:S(2)}, u32[]{:S(2)}) collective-permute-start(bf16[640,768]{1,0:T(8,128)(2,1)} %get-tuple-element.60), channel_id=1, source_target_pairs={{0,62},{1,63},{2,0},{3,1},{4,2},{5,3},{6,4},{7,5},{8,6},{9,7},{10,... | collective-permute-start | bytes 2949128 | tf_op jit(solution)/shard_map/ppermute | solution.py:28
  89.1 7.0 %copy-start.5 = (bf16[768,768]{1,0:T(8,128)(2,1)S(1)}, bf16[768,768]{1,0:T(8,128)(2,1)}, u32[]{:S(2)}) copy-start(bf16[768,768]{1,0:T(8,128)(2,1)} %head_docid.5) | copy-start | bytes 3538948
  91.7 14.1 %all-to-all-start.1 = ((bf16[32,36,128]{2,1,0:T(8,128)(2,1)}), bf16[32,36,128]{2,1,0:T(8,128)(2,1)S(1)}, u32[]{:S(2)}, u32[]{:S(2)}) async-start(bf16[32,36,128]{2,1,0:T(8,128)(2,1)} %reshape.18), calls=%async_computation.1 | async-start | bytes 655360 | tf_op jit(solution)/shard_map/all_to_all | solution.py:247
  96.1 1.5 %copy-start.9 = (f32[640,768]{1,0:T(8,128)S(1)}, f32[640,768]{1,0:T(8,128)}, u32[]{:S(2)}) copy-start(f32[640,768]{1,0:T(8,128)} %copy-done.8) | copy-start | bytes 5898244
  97.7 1.5 %copy-start.11 = (f32[640,768]{1,0:T(8,128)S(1)}, f32[640,768]{1,0:T(8,128)}, u32[]{:S(2)}) copy-start(f32[640,768]{1,0:T(8,128)} %copy-done.10) | copy-start | bytes 5898244
  136.7 7.7 %collective-permute-start.7 = (bf16[768,768]{1,0:T(8,128)(2,1)S(1)}, bf16[768,768]{1,0:T(8,128)(2,1)S(1)}, u32[]{:S(2)}, u32[]{:S(2)}) collective-permute-start(bf16[768,768]{1,0:T(8,128)(2,1)S(1)} %bitcast.5), channel_id=1, source_target_pairs={{0,64},{1,65},{2,66},{3,67},{4,68},{5,69},{6,70},{7,71},{8,72},{9,... | collective-permute-start | bytes 3538952 | tf_op jit(solution)/shard_map/ppermute | solution.py:28

commit v6 on v5

--- a/solution.py
+++ b/solution.py
@@ -148,8 +148,10 @@
     query = query + head_in[...]
     docid_out[...] = docid_grad
     far_sent[...] = far_grad.astype(BF16)
-    head = dot(docids[...], direction(docid_grad, docid_unit[...], docid_scale[...]), COLUMNS)
-    head = head + dot(far[...], direction(far_grad, far_unit[...], far_scale[...]), COLUMNS)
+    own_direct = direction(docid_grad, docid_unit[...], docid_scale[...])
+    far_direct = direction(far_grad, far_unit[...], far_scale[...])
+    rows = jnp.concatenate([docids[...], far[...]])
+    head = dot(rows, jnp.concatenate([own_direct, far_direct]), COLUMNS)
     mine = jnp.zeros(head.shape, jnp.int32) + starts[2] == 0
     kept[...] = jnp.where(mine, query, head)
     sent[...] = jnp.where(mine, head, query).astype(BF16)

time: 148 us -> 148 us (level)
  no operation moved by 1% of the time
where the time goes in v6:
time: 148 us; the launch traced here: 147 us
  blocking collectives  49.6 us (34%)
  Pallas kernels  39.8 us (27%)
  starting transfers between devices  37.1 us (25%)
  waiting for transfers between devices  8.77 us (6%)
  local copies, waits for them, and re-layouts  8.71 us (6%)
  other arithmetic  2.12 us (1%)
    pallas_call x8, Pallas kernels, call(): pl.pallas_call(kernel, out_shape=outs, in_specs=specs, out_specs=[pl.Bloc...  34.2 us
    ppermute x8, starting transfers between devices, moved(): return lax.ppermute(block, AXES, pairs)  32.7 us
    all_to_all x1, blocking collectives, total(): piece = lax.all_to_all(piece, PLANE[:2], 0, 0, tiled=True)  19.1 us
    all_to_all x1, blocking collectives, total(): mine = lax.all_to_all(piece, PLANE, 0, 0, tiled=True).reshape(rows, width)  18 us
    all_to_all x1, blocking collectives, total(): lax.all_to_all(piece, 'z', 0, 0, tiled=True).reshape(rows // plane, width)  12.5 us
    unnamed x24, local copies, waits for them, and re-layouts  6.79 us
    ppermute x8, waiting for transfers between devices, moved(): return lax.ppermute(block, AXES, pairs)  4.48 us
    all_to_all x1, starting transfers between devices, total(): piece = lax.all_to_all(piece, ('x', 'z'), 0, 0, tiled=True)  4.46 us
  transfers between devices with their start and end apart: 9, of which 4 were waited for; matrix products, arithmetic and copies ran while one was open for 3% of the time, Pallas kernels for 21%

profile of v6, /device:TPU:1, one launch (start us, length us, event | category | flops | bytes accessed | tf_op | source)
XLA Modules:
  0.0 147.1 jit_solution(1667229063158373895)
XLA Ops:
  0.6 9.7 %collective-permute-start.2 = (bf16[640,768]{1,0:T(8,128)(2,1)}, bf16[640,768]{1,0:T(8,128)(2,1)}, u32[]{:S(2)}, u32[]{:S(2)}) collective-permute-start(bf16[640,768]{1,0:T(8,128)(2,1)} %queries.4), channel_id=1, source_target_pairs={{0,190},{1,191},{2,128},{3,129},{4,130},{5,131},{6,132},{7,133},{8... | collective-permute-start | bytes 2949128 | tf_op jit(solution)/shard_map/ppermute | solution.py:28
  10.3 0.0 collective-permute-start.4
  10.3 4.7 %collective-permute-start.3 = (s32[640]{0:T(1024)}, s32[640]{0:T(1024)S(1)}, u32[]{:S(2)}, u32[]{:S(2)}) collective-permute-start(s32[640]{0:T(1024)} %param.7), channel_id=1, source_target_pairs={{0,190},{1,191},{2,128},{3,129},{4,130},{5,131},{6,132},{7,133},{8... | collective-permute-start | bytes 7688 | tf_op jit(solution)/shard_map/ppermute | solution.py:28
  15.0 0.7 broadcast_in_dim.19.labels
  15.7 0.0 copy-start
  15.7 1.2 copy-done
  16.9 0.0 copy-start.1
  16.9 0.0 copy-start.2
  17.0 3.6 %collective-permute-start.1 = (bf16[400,768]{1,0:T(8,128)(2,1)S(1)}, bf16[400,768]{1,0:T(8,128)(2,1)}, u32[]{:S(2)}, u32[]{:S(2)}) collective-permute-start(bf16[400,768]{1,0:T(8,128)(2,1)S(1)} %shard_map.76), channel_id=1, source_target_pairs={{0,127},{1,64},{2,65},{3,66},{4,67},{5,68},{6,69},{7,70},{8,71},{9... | collective-permute-start | bytes 1843208 | tf_op jit(solution)/shard_map/ppermute | solution.py:28
  20.7 0.3 collective-permute-start
  21.0 0.1 pad_add_fusion.starts
  21.0 0.0 copy-done.1
  21.0 0.0 copy-done.2
  21.0 0.0 copy-start.3
  21.0 1.3 copy-done.3
  22.3 0.0 copy-start.6
  22.3 1.2 copy-done.6
  23.5 6.7 %shard_map.79 = (bf16[640,768]{1,0:T(8,128)(2,1)S(1)}, f32[640,768]{1,0:T(8,128)S(1)}, f32[640,1]{1,0:T(8,128)S(1)}, f32[640,768]{1,0:T(8,128)S(1)}, f32[768,768]{1,0:T(8,128)S(1)}) custom-call(s32[3]{0:T(128)S(1)} %pad_add_fusion.starts, s32[1,640]{1,0:T(1,128)S(1)} %broadcast_in_dim.19.labels, bf16[640,768]{1,0:T(8,128)(2,1)S(1)} %copy-done.1, ...), custom_call_target="tpu_custom_call" | custom-call | flops 4152360960 | bytes 11605004 | tf_op jit(solution)/shard_map/pallas_call | solution.py:231
  30.2 0.0 copy-start.8
  30.2 0.9 collective-permute-done.3
  31.1 0.0 copy-start.4
  31.1 0.0 collective-permute-done.2.queries
  31.1 2.4 %shard_map.78 = (bf16[640,768]{1,0:T(8,128)(2,1)S(1)}, f32[640,768]{1,0:T(8,128)S(1)}, f32[640,1]{1,0:T(8,128)S(1)}) custom-call(bf16[640,768]{1,0:T(8,128)(2,1)} %collective-permute-done.2.queries, bf16[768,768]{1,0:T(8,128)(2,1)S(1)} %copy-done.2), custom_call_target="tpu_custom_call" | custom-call | flops 3019898880 | bytes 5114368 | tf_op jit(solution)/shard_map/pallas_call | solution.py:231
  33.5 2.8 %collective-permute-done.4.far = bf16[640,768]{1,0:T(8,128)(2,1)} collective-permute-done((bf16[640,768]{1,0:T(8,128)(2,1)}, bf16[640,768]{1,0:T(8,128)(2,1)}, u32[]{:S(2)}, u32[]{:S(2)}) %collective-permute-start.4) | collective-permute-done | bytes 983072 | tf_op jit(solution)/shard_map/ppermute | solution.py:28
  36.3 0.0 copy-done.4
  36.3 9.3 %shard_map.80 = (f32[640,768]{1,0:T(8,128)S(1)}, f32[640,768]{1,0:T(8,128)S(1)}, f32[768,768]{1,0:T(8,128)S(1)}, bf16[640,768]{1,0:T(8,128)(2,1)S(1)}, f32[640,768]{1,0:T(8,128)S(1)}, /*index=5*/f32[640,1]{1,0:T(8,128)S(1)}) custom-call(s32[3]{0:T(128)S(1)} %pad_add_fusion.starts, bf16[640,768]{1,0:T(8,128)(2,1)} %collective-permute-done.2.queries, ...), custom_call_target="tpu_custom_call" | custom-call | flops 6039797760 | bytes 20651532 | tf_op jit(solution)/shard_map/pallas_call | solution.py:231
  45.6 0.0 collective-permute-done.1.part
  45.6 0.0 copy-start.7
  45.6 6.7 %shard_map.81 = (f32[640,768]{1,0:T(8,128)S(1)}, f32[640,768]{1,0:T(8,128)S(1)}, f32[768,768]{1,0:T(8,128)S(1)}) custom-call(s32[3]{0:T(128)S(1)} %pad_add_fusion.starts, bf16[400,768]{1,0:T(8,128)(2,1)} %collective-permute-done.1.part, bf16[768,768]{1,0:T(8,128)(2,1)S(1)} %copy-done.2, bf16[640,768]{1,0:T(8,128)(2,1)S(1)} %get-tuple-element.39.docid_vec, ...), custom_call_target="tpu_custom_call" | custom-call | flops 3271557120 | bytes 16343052 | tf_op jit(solution)/shard_map/pallas_call | solution.py:231
  52.4 0.8 collective-permute-done.part
  53.2 0.0 copy-done.8
  53.2 0.0 copy-done.7
  53.2 6.7 %shard_map.82 = (f32[640,768]{1,0:T(8,128)S(1)}, bf16[640,768]{1,0:T(8,128)(2,1)}, f32[768,768]{1,0:T(8,128)S(1)}, bf16[768,768]{1,0:T(8,128)(2,1)S(1)}) custom-call(s32[3]{0:T(128)S(1)} %pad_add_fusion.starts, bf16[272,768]{1,0:T(8,128)(2,1)} %collective-permute-done.part, bf16[768,768]{1,0:T(8,128)(2,1)S(1)} %copy-done.2, ...), custom_call_target="tpu_custom_call" | custom-call | flops 4781506560 | bytes 22246412 | tf_op jit(solution)/shard_map/pallas_call | solution.py:231
  59.8 0.0 copy-start.10
  59.8 1.5 %collective-permute-start.5 = (bf16[768,768]{1,0:T(8,128)(2,1)S(1)}, bf16[768,768]{1,0:T(8,128)(2,1)S(1)}, u32[]{:S(2)}, u32[]{:S(2)}) collective-permute-start(bf16[768,768]{1,0:T(8,128)(2,1)S(1)} %get-tuple-element.58), channel_id=1, source_target_pairs={{0,64},{1,65},{2,66},{3,67},{4,68},{5,69},{6,70},{7,71},{8,72},{9,... | collective-permute-start | bytes 3538952 | tf_op jit(solution)/shard_map/ppermute | solution.py:28
  61.4 8.0 %collective-permute-start.6 = (bf16[640,768]{1,0:T(8,128)(2,1)}, bf16[640,768]{1,0:T(8,128)(2,1)S(1)}, u32[]{:S(2)}, u32[]{:S(2)}) collective-permute-start(bf16[640,768]{1,0:T(8,128)(2,1)} %get-tuple-element.60), channel_id=1, source_target_pairs={{0,62},{1,63},{2,0},{3,1},{4,2},{5,3},{6,4},{7,5},{8,6},{9,7},{10,... | collective-permute-start | bytes 2949128 | tf_op jit(solution)/shard_map/ppermute | solution.py:28
  69.3 0.0 collective-permute-done.5
  69.3 0.3 add_convert_fusion
  69.7 0.0 copy-done.10
  69.7 19.1 %all_to_all.20 = bf16[4,192,768]{2,1,0:T(8,128)(2,1)} all-to-all(bf16[4,192,768]{2,1,0:T(8,128)(2,1)S(1)} %bitcast.7), channel_id=1, replica_groups=mesh['y_lo'=2,'core'=2,'x'=4,'z'=8,'y_hi'=2] {'y_lo','y_hi'}, dimensions={0} | all-to-all | bytes 2359296 | tf_op jit(solution)/shard_map/all_to_all | solution.py:246
  88.7 0.0 copy-start.5
  88.7 1.6 %reduce_sum.24 = bf16[192,768]{1,0:T(8,128)(2,1)S(1)} reduce(bf16[4,192,768]{2,1,0:T(8,128)(2,1)} %all_to_all.20, bf16[]{:T(256)} %constant.45.clone.1), dimensions={0}, to_apply=%region_0.1 | reduce | flops 442368 | bytes 1474562 | tf_op jit(solution)/shard_map/reduce_sum | solution.py:247
  90.4 1.0 reshape.18
  91.4 4.5 %all-to-all-start.1 = ((bf16[32,36,128]{2,1,0:T(8,128)(2,1)}), bf16[32,36,128]{2,1,0:T(8,128)(2,1)S(1)}, u32[]{:S(2)}, u32[]{:S(2)}) async-start(bf16[32,36,128]{2,1,0:T(8,128)(2,1)} %reshape.18), calls=%async_computation.1 | async-start | bytes 655360 | tf_op jit(solution)/shard_map/all_to_all | solution.py:249
  95.8 0.0 collective-permute-done.6.back
  95.8 0.0 copy-done.5
  95.9 0.0 copy-start.9
  95.9 1.5 %copy-done.9 = f32[640,768]{1,0:T(8,128)S(1)} copy-done((f32[640,768]{1,0:T(8,128)S(1)}, f32[640,768]{1,0:T(8,128)}, u32[]{:S(2)}) %copy-start.9) | copy-done | bytes 1966104
  97.4 0.0 copy-start.11
  97.4 1.5 %copy-done.11 = f32[640,768]{1,0:T(8,128)S(1)} copy-done((f32[640,768]{1,0:T(8,128)S(1)}, f32[640,768]{1,0:T(8,128)}, u32[]{:S(2)}) %copy-start.11) | copy-done | bytes 1966104
  99.0 2.3 %shard_map.83 = bf16[640,768]{1,0:T(8,128)(2,1)} custom-call(f32[640,768]{1,0:T(8,128)S(1)} %copy-done.11, bf16[640,768]{1,0:T(8,128)(2,1)S(1)} %collective-permute-done.6.back, f32[640,768]{1,0:T(8,128)S(1)} %copy-done.9, f32[640,1]{1,0:T(8,128)S(1)} %get-tuple-element.54.docid_scale, bf16[768,768]{1,0:T(8,128)(2,1)S(1)} %copy-done.5), custom_call_target="tpu_custom_call" | custom-call | flops 30198988800 | bytes 7080448 | tf_op jit(solution)/shard_map/pallas_call | solution.py:231
  101.3 4.3 %all-to-all-done.1 = bf16[32,36,128]{2,1,0:T(8,128)(2,1)S(1)} async-done(((bf16[32,36,128]{2,1,0:T(8,128)(2,1)}), bf16[32,36,128]{2,1,0:T(8,128)(2,1)S(1)}, u32[]{:S(2)}, u32[]{:S(2)}) %all-to-all-start.1) | async-done | bytes 294944 | tf_op jit(solution)/shard_map/all_to_all | solution.py:249
  105.6 0.1 reduce_sum.25
  105.7 12.5 %all_to_all.21 = bf16[8,36,128]{2,1,0:T(8,128)(2,1)S(1)} all-to-all(bf16[8,36,128]{2,1,0:T(8,128)(2,1)S(1)} %broadcast_in_dim.21), channel_id=1, replica_groups=mesh['y_lo'=2,'core'=2,'x'=4,'z'=8,'y_hi'=2] {'z'}, dimensions={0} | all-to-all | bytes 147456 | tf_op jit(solution)/shard_map/all_to_all | solution.py:253
  118.2 0.1 broadcast_in_dim.22
  118.3 0.1 broadcast_in_dim.23
  118.4 18.0 %all_to_all.22 = bf16[16,48,768]{2,1,0:T(8,128)(2,1)S(1)} all-to-all(bf16[16,48,768]{2,1,0:T(8,128)(2,1)S(1)} %broadcast_in_dim.23), channel_id=1, replica_groups=mesh['y_lo'=2,'core'=2,'x'=4,'z'=8,'y_hi'=2] {'y_lo','y_hi','x'}, dimensions={0} | all-to-all | bytes 2359296 | tf_op jit(solution)/shard_map/all_to_all | solution.py:255
  136.4 4.9 %collective-permute-start.7 = (bf16[768,768]{1,0:T(8,128)(2,1)S(1)}, bf16[768,768]{1,0:T(8,128)(2,1)S(1)}, u32[]{:S(2)}, u32[]{:S(2)}) collective-permute-start(bf16[768,768]{1,0:T(8,128)(2,1)S(1)} %bitcast.5), channel_id=1, source_target_pairs={{0,64},{1,65},{2,66},{3,67},{4,68},{5,69},{6,70},{7,71},{8,72},{9,... | collective-permute-start | bytes 3538952 | tf_op jit(solution)/shard_map/ppermute | solution.py:28
  141.3 2.8 %shard_map.84 = (f32[768,768]{1,0:T(8,128)}, f32[768,768]{1,0:T(8,128)}) custom-call(s32[3]{0:T(128)S(1)} %pad_add_fusion.starts, bf16[768,768]{1,0:T(8,128)(2,1)S(1)} %bitcast.6), custom_call_target="tpu_custom_call" | custom-call | tf_op jit(solution)/shard_map/pallas_call | solution.py:219
  144.1 0.0 collective-permute-done.7.other
  144.1 2.8 %shard_map.85 = (f32[768,768]{1,0:T(8,128)}, f32[768,768]{1,0:T(8,128)}) custom-call(s32[3]{0:T(128)S(1)} %pad_add_fusion.starts, bf16[768,768]{1,0:T(8,128)(2,1)S(1)} %collective-permute-done.7.other, f32[768,768]{1,0:T(8,128)} %get-tuple-element.63.query_in, f32[768,768]{1,0:T(8,128)} %get-tuple-element.64.docid_in), custom_call_target="tpu_custom_call", output_to_operand_aliasing={{0}: (2, {}), {1}: (3, {})} | custom-call | tf_op jit(solution)/shard_map/pallas_call | solution.py:220
  (4 shorter events, 0.1 us)
Async XLA Ops:
  0.6 30.4 %collective-permute-start.2 = (bf16[640,768]{1,0:T(8,128)(2,1)}, bf16[640,768]{1,0:T(8,128)(2,1)}, u32[]{:S(2)}, u32[]{:S(2)}) collective-permute-start(bf16[640,768]{1,0:T(8,128)(2,1)} %queries.4), channel_id=1, source_target_pairs={{0,190},{1,191},{2,128},{3,129},{4,130},{5,131},{6,132},{7,133},{8... | collective-permute-start | bytes 2949128 | tf_op jit(solution)/shard_map/ppermute | solution.py:28
  10.3 25.9 %collective-permute-start.4 = (bf16[640,768]{1,0:T(8,128)(2,1)}, bf16[640,768]{1,0:T(8,128)(2,1)}, u32[]{:S(2)}, u32[]{:S(2)}) collective-permute-start(bf16[640,768]{1,0:T(8,128)(2,1)} %docids.3), channel_id=1, source_target_pairs={{0,2},{1,3},{2,4},{3,5},{4,6},{5,7},{6,8},{7,9},{8,10},{9,11},{10,... | collective-permute-start | bytes 2949128 | tf_op jit(solution)/shard_map/ppermute | solution.py:28
  10.3 20.7 %collective-permute-start.3 = (s32[640]{0:T(1024)}, s32[640]{0:T(1024)S(1)}, u32[]{:S(2)}, u32[]{:S(2)}) collective-permute-start(s32[640]{0:T(1024)} %param.7), channel_id=1, source_target_pairs={{0,190},{1,191},{2,128},{3,129},{4,130},{5,131},{6,132},{7,133},{8... | collective-permute-start | bytes 7688 | tf_op jit(solution)/shard_map/ppermute | solution.py:28
  15.7 1.2 copy-start
  16.9 4.1 %copy-start.1 = (bf16[640,768]{1,0:T(8,128)(2,1)S(1)}, bf16[640,768]{1,0:T(8,128)(2,1)}, u32[]{:S(2)}) copy-start(bf16[640,768]{1,0:T(8,128)(2,1)} %queries.4) | copy-start | bytes 2949124
  16.9 4.1 %copy-start.2 = (bf16[768,768]{1,0:T(8,128)(2,1)S(1)}, bf16[768,768]{1,0:T(8,128)(2,1)}, u32[]{:S(2)}) copy-start(bf16[768,768]{1,0:T(8,128)(2,1)} %head_query.7) | copy-start | bytes 3538948
  17.0 28.6 %collective-permute-start.1 = (bf16[400,768]{1,0:T(8,128)(2,1)S(1)}, bf16[400,768]{1,0:T(8,128)(2,1)}, u32[]{:S(2)}, u32[]{:S(2)}) collective-permute-start(bf16[400,768]{1,0:T(8,128)(2,1)S(1)} %shard_map.76), channel_id=1, source_target_pairs={{0,127},{1,64},{2,65},{3,66},{4,67},{5,68},{6,69},{7,70},{8,71},{9... | collective-permute-start | bytes 1843208 | tf_op jit(solution)/shard_map/ppermute | solution.py:28
  20.7 32.5 %collective-permute-start = (bf16[272,768]{1,0:T(8,128)(2,1)S(1)}, bf16[272,768]{1,0:T(8,128)(2,1)}, u32[]{:S(2)}, u32[]{:S(2)}) collective-permute-start(bf16[272,768]{1,0:T(8,128)(2,1)S(1)} %shard_map.77), channel_id=1, source_target_pairs={{0,127},{1,64},{2,65},{3,66},{4,67},{5,68},{6,69},{7,70},{8,71},{9... | collective-permute-start | bytes 1253384 | tf_op jit(solution)/shard_map/ppermute | solution.py:28
  21.0 1.3 copy-start.3
  22.3 1.2 copy-start.6
  30.2 23.0 %copy-start.8 = (f32[640,768]{1,0:T(8,128)}, f32[640,768]{1,0:T(8,128)S(1)}, u32[]{:S(2)}) copy-start(f32[640,768]{1,0:T(8,128)S(1)} %get-tuple-element.53.docid_unit) | copy-start | bytes 5898244
  31.1 5.2 %copy-start.4 = (bf16[768,768]{1,0:T(8,128)(2,1)S(1)}, bf16[768,768]{1,0:T(8,128)(2,1)}, u32[]{:S(2)}) copy-start(bf16[768,768]{1,0:T(8,128)(2,1)} %head_docid.5) | copy-start | bytes 3538948
  45.6 7.5 %copy-start.7 = (bf16[640,768]{1,0:T(8,128)(2,1)S(1)}, bf16[640,768]{1,0:T(8,128)(2,1)}, u32[]{:S(2)}) copy-start(bf16[640,768]{1,0:T(8,128)(2,1)} %docids.3) | copy-start | bytes 2949124
  59.8 9.9 %copy-start.10 = (f32[640,768]{1,0:T(8,128)}, f32[640,768]{1,0:T(8,128)S(1)}, u32[]{:S(2)}) copy-start(f32[640,768]{1,0:T(8,128)S(1)} %get-tuple-element.59.docid_grad) | copy-start | bytes 5898244
  59.8 9.5 %collective-permute-start.5 = (bf16[768,768]{1,0:T(8,128)(2,1)S(1)}, bf16[768,768]{1,0:T(8,128)(2,1)S(1)}, u32[]{:S(2)}, u32[]{:S(2)}) collective-permute-start(bf16[768,768]{1,0:T(8,128)(2,1)S(1)} %get-tuple-element.58), channel_id=1, source_target_pairs={{0,64},{1,65},{2,66},{3,67},{4,68},{5,69},{6,70},{7,71},{8,72},{9,... | collective-permute-start | bytes 3538952 | tf_op jit(solution)/shard_map/ppermute | solution.py:28
  61.4 34.5 %collective-permute-start.6 = (bf16[640,768]{1,0:T(8,128)(2,1)}, bf16[640,768]{1,0:T(8,128)(2,1)S(1)}, u32[]{:S(2)}, u32[]{:S(2)}) collective-permute-start(bf16[640,768]{1,0:T(8,128)(2,1)} %get-tuple-element.60), channel_id=1, source_target_pairs={{0,62},{1,63},{2,0},{3,1},{4,2},{5,3},{6,4},{7,5},{8,6},{9,7},{10,... | collective-permute-start | bytes 2949128 | tf_op jit(solution)/shard_map/ppermute | solution.py:28
  88.7 7.1 %copy-start.5 = (bf16[768,768]{1,0:T(8,128)(2,1)S(1)}, bf16[768,768]{1,0:T(8,128)(2,1)}, u32[]{:S(2)}) copy-start(bf16[768,768]{1,0:T(8,128)(2,1)} %head_docid.5) | copy-start | bytes 3538948
  91.4 14.2 %all-to-all-start.1 = ((bf16[32,36,128]{2,1,0:T(8,128)(2,1)}), bf16[32,36,128]{2,1,0:T(8,128)(2,1)S(1)}, u32[]{:S(2)}, u32[]{:S(2)}) async-start(bf16[32,36,128]{2,1,0:T(8,128)(2,1)} %reshape.18), calls=%async_computation.1 | async-start | bytes 655360 | tf_op jit(solution)/shard_map/all_to_all | solution.py:249
  95.9 1.5 %copy-start.9 = (f32[640,768]{1,0:T(8,128)S(1)}, f32[640,768]{1,0:T(8,128)}, u32[]{:S(2)}) copy-start(f32[640,768]{1,0:T(8,128)} %copy-done.8) | copy-start | bytes 5898244
  97.4 1.5 %copy-start.11 = (f32[640,768]{1,0:T(8,128)S(1)}, f32[640,768]{1,0:T(8,128)}, u32[]{:S(2)}) copy-start(f32[640,768]{1,0:T(8,128)} %copy-done.10) | copy-start | bytes 5898244
  136.4 7.7 %collective-permute-start.7 = (bf16[768,768]{1,0:T(8,128)(2,1)S(1)}, bf16[768,768]{1,0:T(8,128)(2,1)S(1)}, u32[]{:S(2)}, u32[]{:S(2)}) collective-permute-start(bf16[768,768]{1,0:T(8,128)(2,1)S(1)} %bitcast.5), channel_id=1, source_target_pairs={{0,64},{1,65},{2,66},{3,67},{4,68},{5,69},{6,70},{7,71},{8,72},{9,... | collective-permute-start | bytes 3538952 | tf_op jit(solution)/shard_map/ppermute | solution.py:28

commit v7 on v4

--- a/solution.py
+++ b/solution.py
@@ -231,7 +231,7 @@
     piece = value.astype(BF16).reshape(SIZES[0] * SIZES[4], -1, width)
     piece = lax.all_to_all(piece, PLANE[:2], 0, 0, tiled=True)
     piece = jnp.sum(piece.astype(F32), axis=0).astype(BF16)
-    piece = piece.reshape(SIZES[2] * line, -1, 128)
+    piece = piece.reshape(SIZES[2] * line, -1, width)
     piece = lax.all_to_all(piece, ("x", "z"), 0, 0, tiled=True)
     piece = jnp.sum(piece.astype(F32), axis=0).astype(BF16)
     piece, update = lax.optimization_barrier((piece, update))

time: 148 us -> 149 us (level)
  transfers between devices with their start and end apart: 9 -> 9, of which waited for: 4 -> 4; matrix products, arithmetic and copies ran while one was open for 3% -> 2% of each run, Pallas kernels for 20% -> 19%
where the time goes in v7:
time: 149 us
  blocking collectives  50.6 us (34%)
  Pallas kernels  38.4 us (26%)
  starting transfers between devices  35.1 us (24%)
  waiting for transfers between devices  13.3 us (9%)
  local copies, waits for them, and re-layouts  8.49 us (6%)
  other arithmetic  2.14 us (1%)
    pallas_call x7, Pallas kernels, call(): pl.pallas_call(kernel, out_shape=outs, in_specs=specs, out_specs=[pl.Bloc...  32.8 us
    ppermute x8, starting transfers between devices, moved(): return lax.ppermute(block, AXES, pairs)  30.6 us
    all_to_all x1, blocking collectives, total(): piece = lax.all_to_all(piece, PLANE[:2], 0, 0, tiled=True)  19.1 us
    all_to_all x1, blocking collectives, total(): mine = lax.all_to_all(piece, PLANE, 0, 0, tiled=True).reshape(rows, width)  18.3 us
    all_to_all x1, blocking collectives, total(): lax.all_to_all(piece, 'z', 0, 0, tiled=True).reshape(rows // plane, width)  13.2 us
    ppermute x8, waiting for transfers between devices, moved(): return lax.ppermute(block, AXES, pairs)  8.26 us
    unnamed x24, local copies, waits for them, and re-layouts  6.79 us
    all_to_all x1, waiting for transfers between devices, total(): piece = lax.all_to_all(piece, ('x', 'z'), 0, 0, tiled=True)  5.01 us
  transfers between devices with their start and end apart: 9, of which 4 were waited for; matrix products, arithmetic and copies ran while one was open for 2% of the time, Pallas kernels for 19%

profile of v7, /device:TPU:1, one launch (start us, length us, event | category | flops | bytes accessed | tf_op | source)
XLA Modules:
  0.0 148.9 jit_solution(6322636045696536434)
XLA Ops:
  0.6 2.5 %collective-permute-start.4 = (bf16[640,768]{1,0:T(8,128)(2,1)}, bf16[640,768]{1,0:T(8,128)(2,1)}, u32[]{:S(2)}, u32[]{:S(2)}) collective-permute-start(bf16[640,768]{1,0:T(8,128)(2,1)} %docids.3), channel_id=1, source_target_pairs={{0,2},{1,3},{2,4},{3,5},{4,6},{5,7},{6,8},{7,9},{8,10},{9,11},{10,... | collective-permute-start | bytes 2949128 | tf_op jit(solution)/shard_map/ppermute | solution.py:28
  3.2 7.2 %collective-permute-start.2 = (bf16[640,768]{1,0:T(8,128)(2,1)}, bf16[640,768]{1,0:T(8,128)(2,1)}, u32[]{:S(2)}, u32[]{:S(2)}) collective-permute-start(bf16[640,768]{1,0:T(8,128)(2,1)} %queries.4), channel_id=1, source_target_pairs={{0,190},{1,191},{2,128},{3,129},{4,130},{5,131},{6,132},{7,133},{8... | collective-permute-start | bytes 2949128 | tf_op jit(solution)/shard_map/ppermute | solution.py:28
  10.4 1.3 collective-permute-start.3
  11.7 0.7 broadcast_in_dim.19.labels
  12.4 0.0 copy-start
  12.4 1.2 copy-done
  13.6 0.0 copy-start.1
  13.6 0.0 copy-start.2
  13.7 4.8 %collective-permute-start.1 = (bf16[400,768]{1,0:T(8,128)(2,1)S(1)}, bf16[400,768]{1,0:T(8,128)(2,1)}, u32[]{:S(2)}, u32[]{:S(2)}) collective-permute-start(bf16[400,768]{1,0:T(8,128)(2,1)S(1)} %shard_map.76), channel_id=1, source_target_pairs={{0,127},{1,64},{2,65},{3,66},{4,67},{5,68},{6,69},{7,70},{8,71},{9... | collective-permute-start | bytes 1843208 | tf_op jit(solution)/shard_map/ppermute | solution.py:28
  18.5 0.3 collective-permute-start
  18.8 0.1 pad_add_fusion.starts
  18.9 0.0 copy-done.1
  18.9 0.0 copy-done.2
  18.9 0.0 copy-start.3
  18.9 1.3 copy-done.3
  20.2 0.0 copy-start.6
  20.2 1.2 copy-done.6
  21.4 0.0 copy-start.4
  21.4 6.7 %shard_map.78 = (bf16[640,768]{1,0:T(8,128)(2,1)S(1)}, f32[640,768]{1,0:T(8,128)S(1)}, f32[640,1]{1,0:T(8,128)S(1)}, f32[640,768]{1,0:T(8,128)S(1)}, f32[768,768]{1,0:T(8,128)S(1)}) custom-call(s32[3]{0:T(128)S(1)} %pad_add_fusion.starts, s32[1,640]{1,0:T(1,128)S(1)} %broadcast_in_dim.19.labels, bf16[640,768]{1,0:T(8,128)(2,1)S(1)} %copy-done.1, ...), custom_call_target="tpu_custom_call" | custom-call | flops 4152360960 | bytes 11605004 | tf_op jit(solution)/shard_map/pallas_call | solution.py:217
  28.0 0.0 copy-start.8
  28.1 3.1 %collective-permute-done.3 = s32[640]{0:T(1024)S(1)} collective-permute-done((s32[640]{0:T(1024)}, s32[640]{0:T(1024)S(1)}, u32[]{:S(2)}, u32[]{:S(2)}) %collective-permute-start.3) | collective-permute-done | bytes 2592 | tf_op jit(solution)/shard_map/ppermute | solution.py:28
  31.2 0.0 collective-permute-done.4.far
  31.2 0.0 collective-permute-done.2.queries
  31.2 0.0 copy-done.4
  31.2 10.2 %shard_map.79 = (f32[640,768]{1,0:T(8,128)S(1)}, f32[640,768]{1,0:T(8,128)S(1)}, f32[768,768]{1,0:T(8,128)S(1)}, bf16[640,768]{1,0:T(8,128)(2,1)S(1)}, f32[640,768]{1,0:T(8,128)S(1)}, /*index=5*/f32[640,1]{1,0:T(8,128)S(1)}) custom-call(s32[3]{0:T(128)S(1)} %pad_add_fusion.starts, bf16[640,768]{1,0:T(8,128)(2,1)} %collective-permute-done.2.queries, ...), custom_call_target="tpu_custom_call" | custom-call | flops 6039797760 | bytes 18879500 | tf_op jit(solution)/shard_map/pallas_call | solution.py:217
  41.4 2.9 %collective-permute-done.1.part = bf16[400,768]{1,0:T(8,128)(2,1)} collective-permute-done((bf16[400,768]{1,0:T(8,128)(2,1)S(1)}, bf16[400,768]{1,0:T(8,128)(2,1)}, u32[]{:S(2)}, u32[]{:S(2)}) %collective-permute-start.1) | collective-permute-done | bytes 614432 | tf_op jit(solution)/shard_map/ppermute | solution.py:28
  44.3 0.0 copy-start.7
  44.3 6.7 %shard_map.80 = (f32[640,768]{1,0:T(8,128)S(1)}, f32[640,768]{1,0:T(8,128)S(1)}, f32[768,768]{1,0:T(8,128)S(1)}) custom-call(s32[3]{0:T(128)S(1)} %pad_add_fusion.starts, bf16[400,768]{1,0:T(8,128)(2,1)} %collective-permute-done.1.part, bf16[768,768]{1,0:T(8,128)(2,1)S(1)} %copy-done.2, bf16[640,768]{1,0:T(8,128)(2,1)S(1)} %get-tuple-element.33.docid_vec, ...), custom_call_target="tpu_custom_call" | custom-call | flops 3271557120 | bytes 16343052 | tf_op jit(solution)/shard_map/pallas_call | solution.py:217
  51.0 2.2 %collective-permute-done.part = bf16[272,768]{1,0:T(8,128)(2,1)} collective-permute-done((bf16[272,768]{1,0:T(8,128)(2,1)S(1)}, bf16[272,768]{1,0:T(8,128)(2,1)}, u32[]{:S(2)}, u32[]{:S(2)}) %collective-permute-start) | collective-permute-done | bytes 417824 | tf_op jit(solution)/shard_map/ppermute | solution.py:28
  53.3 0.0 copy-done.8
  53.3 0.0 copy-done.7
  53.3 6.8 %shard_map.81 = (f32[640,768]{1,0:T(8,128)S(1)}, bf16[640,768]{1,0:T(8,128)(2,1)}, f32[768,768]{1,0:T(8,128)S(1)}, bf16[768,768]{1,0:T(8,128)(2,1)S(1)}) custom-call(s32[3]{0:T(128)S(1)} %pad_add_fusion.starts, bf16[272,768]{1,0:T(8,128)(2,1)} %collective-permute-done.part, bf16[768,768]{1,0:T(8,128)(2,1)S(1)} %copy-done.2, ...), custom_call_target="tpu_custom_call" | custom-call | flops 4781506560 | bytes 22246412 | tf_op jit(solution)/shard_map/pallas_call | solution.py:217
  60.1 0.0 copy-start.10
  60.1 1.6 %collective-permute-start.5 = (bf16[768,768]{1,0:T(8,128)(2,1)S(1)}, bf16[768,768]{1,0:T(8,128)(2,1)S(1)}, u32[]{:S(2)}, u32[]{:S(2)}) collective-permute-start(bf16[768,768]{1,0:T(8,128)(2,1)S(1)} %get-tuple-element.52), channel_id=1, source_target_pairs={{0,64},{1,65},{2,66},{3,67},{4,68},{5,69},{6,70},{7,71},{8,72},{9,... | collective-permute-start | bytes 3538952 | tf_op jit(solution)/shard_map/ppermute | solution.py:28
  61.7 7.9 %collective-permute-start.6 = (bf16[640,768]{1,0:T(8,128)(2,1)}, bf16[640,768]{1,0:T(8,128)(2,1)S(1)}, u32[]{:S(2)}, u32[]{:S(2)}) collective-permute-start(bf16[640,768]{1,0:T(8,128)(2,1)} %get-tuple-element.54), channel_id=1, source_target_pairs={{0,62},{1,63},{2,0},{3,1},{4,2},{5,3},{6,4},{7,5},{8,6},{9,7},{10,... | collective-permute-start | bytes 2949128 | tf_op jit(solution)/shard_map/ppermute | solution.py:28
  69.6 0.0 collective-permute-done.5
  69.6 0.3 add_convert_fusion
  70.0 0.0 copy-done.10
  70.0 19.1 %all_to_all.20 = bf16[4,192,768]{2,1,0:T(8,128)(2,1)} all-to-all(bf16[4,192,768]{2,1,0:T(8,128)(2,1)S(1)} %bitcast.7), channel_id=1, replica_groups=mesh['y_lo'=2,'core'=2,'x'=4,'z'=8,'y_hi'=2] {'y_lo','y_hi'}, dimensions={0} | all-to-all | bytes 2359296 | tf_op jit(solution)/shard_map/all_to_all | solution.py:232
  89.1 0.0 copy-start.5
  89.1 1.6 %reduce_sum.24 = bf16[192,768]{1,0:T(8,128)(2,1)S(1)} reduce(bf16[4,192,768]{2,1,0:T(8,128)(2,1)} %all_to_all.20, bf16[]{:T(256)} %constant.45.clone.1), dimensions={0}, to_apply=%region_0.1 | reduce | flops 442368 | bytes 1474562 | tf_op jit(solution)/shard_map/reduce_sum | solution.py:233
  90.7 0.9 reshape.18
  91.5 4.5 %all-to-all-start.1 = ((bf16[32,6,768]{2,1,0:T(8,128)(2,1)}), bf16[32,6,768]{2,1,0:T(8,128)(2,1)S(1)}, u32[]{:S(2)}, u32[]{:S(2)}) async-start(bf16[32,6,768]{2,1,0:T(8,128)(2,1)} %reshape.18), calls=%async_computation.1 | async-start | bytes 786432 | tf_op jit(solution)/shard_map/all_to_all | solution.py:235
  96.0 0.0 collective-permute-done.6.back
  96.0 0.0 copy-done.5
  96.0 0.0 copy-start.9
  96.0 1.5 %copy-done.9 = f32[640,768]{1,0:T(8,128)S(1)} copy-done((f32[640,768]{1,0:T(8,128)S(1)}, f32[640,768]{1,0:T(8,128)}, u32[]{:S(2)}) %copy-start.9) | copy-done | bytes 1966104
  97.6 0.0 copy-start.11
  97.6 1.5 %copy-done.11 = f32[640,768]{1,0:T(8,128)S(1)} copy-done((f32[640,768]{1,0:T(8,128)S(1)}, f32[640,768]{1,0:T(8,128)}, u32[]{:S(2)}) %copy-start.11) | copy-done | bytes 1966104
  99.1 2.3 %shard_map.82 = bf16[640,768]{1,0:T(8,128)(2,1)} custom-call(f32[640,768]{1,0:T(8,128)S(1)} %copy-done.11, bf16[640,768]{1,0:T(8,128)(2,1)S(1)} %collective-permute-done.6.back, f32[640,768]{1,0:T(8,128)S(1)} %copy-done.9, f32[640,1]{1,0:T(8,128)S(1)} %get-tuple-element.48.docid_scale, bf16[768,768]{1,0:T(8,128)(2,1)S(1)} %copy-done.5), custom_call_target="tpu_custom_call" | custom-call | flops 30198988800 | bytes 7080448 | tf_op jit(solution)/shard_map/pallas_call | solution.py:217
  101.5 5.0 %all-to-all-done.1 = bf16[32,6,768]{2,1,0:T(8,128)(2,1)S(1)} async-done(((bf16[32,6,768]{2,1,0:T(8,128)(2,1)}), bf16[32,6,768]{2,1,0:T(8,128)(2,1)S(1)}, u32[]{:S(2)}, u32[]{:S(2)}) %all-to-all-start.1) | async-done | bytes 294944 | tf_op jit(solution)/shard_map/all_to_all | solution.py:235
  106.5 0.1 reduce_sum.25
  106.6 13.2 %all_to_all.21 = bf16[8,6,768]{2,1,0:T(8,128)(2,1)S(1)} all-to-all(bf16[8,6,768]{2,1,0:T(8,128)(2,1)S(1)} %broadcast_in_dim.21), channel_id=1, replica_groups=mesh['y_lo'=2,'core'=2,'x'=4,'z'=8,'y_hi'=2] {'z'}, dimensions={0} | all-to-all | bytes 147456 | tf_op jit(solution)/shard_map/all_to_all | solution.py:239
  119.8 0.1 broadcast_in_dim.23
  119.9 18.3 %all_to_all.22 = bf16[16,48,768]{2,1,0:T(8,128)(2,1)S(1)} all-to-all(bf16[16,48,768]{2,1,0:T(8,128)(2,1)S(1)} %broadcast_in_dim.23), channel_id=1, replica_groups=mesh['y_lo'=2,'core'=2,'x'=4,'z'=8,'y_hi'=2] {'y_lo','y_hi','x'}, dimensions={0} | all-to-all | bytes 2359296 | tf_op jit(solution)/shard_map/all_to_all | solution.py:241
  138.2 4.9 %collective-permute-start.7 = (bf16[768,768]{1,0:T(8,128)(2,1)S(1)}, bf16[768,768]{1,0:T(8,128)(2,1)S(1)}, u32[]{:S(2)}, u32[]{:S(2)}) collective-permute-start(bf16[768,768]{1,0:T(8,128)(2,1)S(1)} %bitcast.5), channel_id=1, source_target_pairs={{0,64},{1,65},{2,66},{3,67},{4,68},{5,69},{6,70},{7,71},{8,72},{9,... | collective-permute-start | bytes 3538952 | tf_op jit(solution)/shard_map/ppermute | solution.py:28
  143.1 2.8 %shard_map.83 = (f32[768,768]{1,0:T(8,128)}, f32[768,768]{1,0:T(8,128)}) custom-call(s32[3]{0:T(128)S(1)} %pad_add_fusion.starts, bf16[768,768]{1,0:T(8,128)(2,1)S(1)} %bitcast.6), custom_call_target="tpu_custom_call" | custom-call | tf_op jit(solution)/shard_map/pallas_call | solution.py:205
  145.9 0.0 collective-permute-done.7.other
  145.9 2.8 %shard_map.84 = (f32[768,768]{1,0:T(8,128)}, f32[768,768]{1,0:T(8,128)}) custom-call(s32[3]{0:T(128)S(1)} %pad_add_fusion.starts, bf16[768,768]{1,0:T(8,128)(2,1)S(1)} %collective-permute-done.7.other, f32[768,768]{1,0:T(8,128)} %get-tuple-element.57.query_in, f32[768,768]{1,0:T(8,128)} %get-tuple-element.58.docid_in), custom_call_target="tpu_custom_call", output_to_operand_aliasing={{0}: (2, {}), {1}: (3, {})} | custom-call | tf_op jit(solution)/shard_map/pallas_call | solution.py:206
  (5 shorter events, 0.1 us)
Async XLA Ops:
  0.6 30.5 %collective-permute-start.4 = (bf16[640,768]{1,0:T(8,128)(2,1)}, bf16[640,768]{1,0:T(8,128)(2,1)}, u32[]{:S(2)}, u32[]{:S(2)}) collective-permute-start(bf16[640,768]{1,0:T(8,128)(2,1)} %docids.3), channel_id=1, source_target_pairs={{0,2},{1,3},{2,4},{3,5},{4,6},{5,7},{6,8},{7,9},{8,10},{9,11},{10,... | collective-permute-start | bytes 2949128 | tf_op jit(solution)/shard_map/ppermute | solution.py:28
  3.2 28.0 %collective-permute-start.2 = (bf16[640,768]{1,0:T(8,128)(2,1)}, bf16[640,768]{1,0:T(8,128)(2,1)}, u32[]{:S(2)}, u32[]{:S(2)}) collective-permute-start(bf16[640,768]{1,0:T(8,128)(2,1)} %queries.4), channel_id=1, source_target_pairs={{0,190},{1,191},{2,128},{3,129},{4,130},{5,131},{6,132},{7,133},{8... | collective-permute-start | bytes 2949128 | tf_op jit(solution)/shard_map/ppermute | solution.py:28
  10.4 20.7 %collective-permute-start.3 = (s32[640]{0:T(1024)}, s32[640]{0:T(1024)S(1)}, u32[]{:S(2)}, u32[]{:S(2)}) collective-permute-start(s32[640]{0:T(1024)} %param.7), channel_id=1, source_target_pairs={{0,190},{1,191},{2,128},{3,129},{4,130},{5,131},{6,132},{7,133},{8... | collective-permute-start | bytes 7688 | tf_op jit(solution)/shard_map/ppermute | solution.py:28
  12.4 1.2 copy-start
  13.6 5.3 %copy-start.1 = (bf16[640,768]{1,0:T(8,128)(2,1)S(1)}, bf16[640,768]{1,0:T(8,128)(2,1)}, u32[]{:S(2)}) copy-start(bf16[640,768]{1,0:T(8,128)(2,1)} %queries.4) | copy-start | bytes 2949124
  13.6 5.3 %copy-start.2 = (bf16[768,768]{1,0:T(8,128)(2,1)S(1)}, bf16[768,768]{1,0:T(8,128)(2,1)}, u32[]{:S(2)}) copy-start(bf16[768,768]{1,0:T(8,128)(2,1)} %head_query.7) | copy-start | bytes 3538948
  13.7 30.6 %collective-permute-start.1 = (bf16[400,768]{1,0:T(8,128)(2,1)S(1)}, bf16[400,768]{1,0:T(8,128)(2,1)}, u32[]{:S(2)}, u32[]{:S(2)}) collective-permute-start(bf16[400,768]{1,0:T(8,128)(2,1)S(1)} %shard_map.76), channel_id=1, source_target_pairs={{0,127},{1,64},{2,65},{3,66},{4,67},{5,68},{6,69},{7,70},{8,71},{9... | collective-permute-start | bytes 1843208 | tf_op jit(solution)/shard_map/ppermute | solution.py:28
  18.5 34.7 %collective-permute-start = (bf16[272,768]{1,0:T(8,128)(2,1)S(1)}, bf16[272,768]{1,0:T(8,128)(2,1)}, u32[]{:S(2)}, u32[]{:S(2)}) collective-permute-start(bf16[272,768]{1,0:T(8,128)(2,1)S(1)} %shard_map.77), channel_id=1, source_target_pairs={{0,127},{1,64},{2,65},{3,66},{4,67},{5,68},{6,69},{7,70},{8,71},{9... | collective-permute-start | bytes 1253384 | tf_op jit(solution)/shard_map/ppermute | solution.py:28
  18.9 1.3 copy-start.3
  20.2 1.2 copy-start.6
  21.4 9.8 %copy-start.4 = (bf16[768,768]{1,0:T(8,128)(2,1)S(1)}, bf16[768,768]{1,0:T(8,128)(2,1)}, u32[]{:S(2)}) copy-start(bf16[768,768]{1,0:T(8,128)(2,1)} %head_docid.5) | copy-start | bytes 3538948
  28.0 25.2 %copy-start.8 = (f32[640,768]{1,0:T(8,128)}, f32[640,768]{1,0:T(8,128)S(1)}, u32[]{:S(2)}) copy-start(f32[640,768]{1,0:T(8,128)S(1)} %get-tuple-element.47.docid_unit) | copy-start | bytes 5898244
  44.3 9.0 %copy-start.7 = (bf16[640,768]{1,0:T(8,128)(2,1)S(1)}, bf16[640,768]{1,0:T(8,128)(2,1)}, u32[]{:S(2)}) copy-start(bf16[640,768]{1,0:T(8,128)(2,1)} %docids.3) | copy-start | bytes 2949124
  60.1 9.9 %copy-start.10 = (f32[640,768]{1,0:T(8,128)}, f32[640,768]{1,0:T(8,128)S(1)}, u32[]{:S(2)}) copy-start(f32[640,768]{1,0:T(8,128)S(1)} %get-tuple-element.53.docid_grad) | copy-start | bytes 5898244
  60.1 9.6 %collective-permute-start.5 = (bf16[768,768]{1,0:T(8,128)(2,1)S(1)}, bf16[768,768]{1,0:T(8,128)(2,1)S(1)}, u32[]{:S(2)}, u32[]{:S(2)}) collective-permute-start(bf16[768,768]{1,0:T(8,128)(2,1)S(1)} %get-tuple-element.52), channel_id=1, source_target_pairs={{0,64},{1,65},{2,66},{3,67},{4,68},{5,69},{6,70},{7,71},{8,72},{9,... | collective-permute-start | bytes 3538952 | tf_op jit(solution)/shard_map/ppermute | solution.py:28
  61.7 34.3 %collective-permute-start.6 = (bf16[640,768]{1,0:T(8,128)(2,1)}, bf16[640,768]{1,0:T(8,128)(2,1)S(1)}, u32[]{:S(2)}, u32[]{:S(2)}) collective-permute-start(bf16[640,768]{1,0:T(8,128)(2,1)} %get-tuple-element.54), channel_id=1, source_target_pairs={{0,62},{1,63},{2,0},{3,1},{4,2},{5,3},{6,4},{7,5},{8,6},{9,7},{10,... | collective-permute-start | bytes 2949128 | tf_op jit(solution)/shard_map/ppermute | solution.py:28
  89.1 7.0 %copy-start.5 = (bf16[768,768]{1,0:T(8,128)(2,1)S(1)}, bf16[768,768]{1,0:T(8,128)(2,1)}, u32[]{:S(2)}) copy-start(bf16[768,768]{1,0:T(8,128)(2,1)} %head_docid.5) | copy-start | bytes 3538948
  91.5 14.9 %all-to-all-start.1 = ((bf16[32,6,768]{2,1,0:T(8,128)(2,1)}), bf16[32,6,768]{2,1,0:T(8,128)(2,1)S(1)}, u32[]{:S(2)}, u32[]{:S(2)}) async-start(bf16[32,6,768]{2,1,0:T(8,128)(2,1)} %reshape.18), calls=%async_computation.1 | async-start | bytes 786432 | tf_op jit(solution)/shard_map/all_to_all | solution.py:235
  96.0 1.5 %copy-start.9 = (f32[640,768]{1,0:T(8,128)S(1)}, f32[640,768]{1,0:T(8,128)}, u32[]{:S(2)}) copy-start(f32[640,768]{1,0:T(8,128)} %copy-done.8) | copy-start | bytes 5898244
  97.6 1.5 %copy-start.11 = (f32[640,768]{1,0:T(8,128)S(1)}, f32[640,768]{1,0:T(8,128)}, u32[]{:S(2)}) copy-start(f32[640,768]{1,0:T(8,128)} %copy-done.10) | copy-start | bytes 5898244
  138.2 7.7 %collective-permute-start.7 = (bf16[768,768]{1,0:T(8,128)(2,1)S(1)}, bf16[768,768]{1,0:T(8,128)(2,1)S(1)}, u32[]{:S(2)}, u32[]{:S(2)}) collective-permute-start(bf16[768,768]{1,0:T(8,128)(2,1)S(1)} %bitcast.5), channel_id=1, source_target_pairs={{0,64},{1,65},{2,66},{3,67},{4,68},{5,69},{6,70},{7,71},{8,72},{9,... | collective-permute-start | bytes 3538952 | tf_op jit(solution)/shard_map/ppermute | solution.py:28
